TPU v7x, 32 devices: a whole 2x2x4 slice. The times are simulated.
32 devices in a mesh: row: 8 (over y, x, core), col: 4 (over z).
Axes of the slice: x: 2, y: 2, z: 4, core: 2. Of those that a mesh axis runs over, the one named last changes fastest.
Arguments:
- nodes: bfloat16 [128, 512], P(('row', 'col')), may hold values from -50 to 50
- coords: float32 [3, 128], P(None, ('row', 'col')), may hold values from -18 to 18
- atom_types: int32 [128], P(('row', 'col')), may hold values from 0 to 29
- segment_ids: int32 [128], P(('row', 'col')), may hold values from 0 to 1
- pair_mask: int32 [128, 128], P('row', 'col'), may hold values 0 or 1
- pair_bias: bfloat16 [64, 128, 128], P(None, 'row', 'col'), may hold values from -10 to 310
- ln_gain: float32 [512], replicated, may hold values from 0.1 to 1.9
- w_qkv: bfloat16 [512, 1536], replicated, may hold values from -0.25 to 0.25
- gauss_mul: float32 [60, 60], replicated, may hold values from 0.25 to 1.75
- gauss_add: float32 [60, 60], replicated, may hold values from -4 to 4
- gauss_mean: float32 [128], replicated, may hold values from 0 to 16
- gauss_width: float32 [128], replicated, may hold values from 0.5 to 2.5
- w_gauss: bfloat16 [128, 128], replicated, may hold values from -2 to 2
- w_heads: bfloat16 [128, 64], replicated, may hold values from -2 to 2
- w_coord1: bfloat16 [64, 64], replicated, may hold values from -0.75 to 0.75
- w_coord2: bfloat16 [64], replicated, may hold values from -0.75 to 0.75
Outputs:
- attended: bfloat16 [128, 512], P(('row', 'col'))
- moved: float32 [3, 128], P(None, ('row', 'col'))
All inputs are finite; a program needn't handle non-finite values. No bound on the sum of `pair_mask` on one device may be relied on, other than what follows from the above.
Results may differ from a plain program's by a relative error of at most 0.015.
Values may be sent and summed in bfloat16 or wider, within the bound.
No kernel may reach another device: no remote copies, remote signals or barrier semaphores. Data moves between devices by JAX's collectives and lax.ppermute only.
A program may use at most 64 MiB of HBM per device.

v0:
```python
import math

import jax
import jax.numpy as jnp
from jax import lax
from jax.sharding import PartitionSpec as P

ln_epsilon = 1e-05
masked_fill = -1000000000.0
root_shift = 0.01


def layer_normed(nodes, ln_gain):
    features = nodes.astype(jnp.float32)
    row_mean = jnp.mean(features, axis=1, keepdims=True)
    centred = features - row_mean
    spread = jnp.mean(centred * centred, axis=1, keepdims=True)
    return (centred * lax.rsqrt(spread + ln_epsilon) * ln_gain[None, :]).astype(jnp.bfloat16)


def gaussians(expanded, gauss_mean, gauss_width):
    scaled = (expanded[None, :, :] - gauss_mean[:, None, None]) / gauss_width[:, None, None]
    norming = math.sqrt(2.0 * math.pi) * gauss_width[:, None, None]
    return (jnp.exp(-0.5 * scaled * scaled) / norming).astype(jnp.bfloat16)


def shards(
    nodes,
    coords,
    atom_types,
    segment_ids,
    pair_mask,
    pair_bias,
    ln_gain,
    w_qkv,
    gauss_mul,
    gauss_add,
    gauss_mean,
    gauss_width,
    w_gauss,
    w_heads,
    w_coord1,
    w_coord2,
):
    col_count = lax.axis_size("col")
    row_count = lax.axis_size("row")
    col_index = lax.axis_index("col")
    row_index = lax.axis_index("row")
    own_rows = nodes.shape[0]
    query_rows = own_rows * col_count
    key_cols = own_rows * row_count
    model_width = nodes.shape[1]
    head_count = pair_bias.shape[0]
    head_dim = model_width // head_count
    kind_count = gauss_mul.shape[0]
    all_atoms = own_rows * row_count * col_count
    highest = lax.Precision.HIGHEST
    normed = layer_normed(nodes, ln_gain)
    kinds = atom_types + kind_count // 2 * segment_ids
    own_table = jnp.concatenate([coords, kinds.astype(jnp.float32)[None, :]], axis=0)
    atom_table = lax.all_gather(own_table, ("row", "col"), axis=1, tiled=True)
    query_table = lax.dynamic_slice_in_dim(atom_table, row_index * query_rows, query_rows, 1)
    key_table = lax.dynamic_slice_in_dim(atom_table, col_index * key_cols, key_cols, 1)
    projected = jnp.dot(
        lax.all_gather(normed, "col", axis=0, tiled=True), w_qkv, preferred_element_type=jnp.float32
    ).astype(jnp.bfloat16)
    queries = projected[:, :model_width].reshape(query_rows, head_count, head_dim)
    row_keys = projected[:, model_width:]
    every_key = lax.all_gather(row_keys, "row", axis=0, tiled=True)
    col_keys = lax.dynamic_slice_in_dim(every_key, col_index * key_cols, key_cols, 0)
    keys_block = col_keys[:, :model_width].reshape(key_cols, head_count, head_dim)
    values_block = col_keys[:, model_width:].reshape(key_cols, head_count, head_dim)
    offsets = query_table[:3, :, None] - key_table[:3, None, :]
    distance = jnp.sqrt(jnp.sum(offsets * offsets, axis=0) + root_shift)
    kind_range = jnp.arange(kind_count, dtype=jnp.float32)
    query_onehot = (query_table[3][:, None] == kind_range[None, :]).astype(jnp.float32)
    key_onehot = (key_table[3][:, None] == kind_range[None, :]).astype(jnp.float32)
    both_tables = jnp.concatenate([gauss_mul, gauss_add], axis=1)
    row_lookup = jnp.dot(query_onehot, both_tables, precision=highest)
    scale_pair = jnp.dot(row_lookup[:, :kind_count], key_onehot.T, precision=highest)
    shift_pair = jnp.dot(row_lookup[:, kind_count:], key_onehot.T, precision=highest)
    expanded = scale_pair * distance + shift_pair
    features = gaussians(expanded, gauss_mean, gauss_width)
    hidden = jax.nn.gelu(
        jnp.einsum("kij,kl->lij", features, w_gauss, preferred_element_type=jnp.float32)
    ).astype(jnp.bfloat16)
    geometry = jnp.einsum("kij,kh->hij", hidden, w_heads, preferred_element_type=jnp.float32)
    affinity = jnp.einsum(
        "ihd,jhd->hij", queries, keys_block, preferred_element_type=jnp.float32
    ) / math.sqrt(head_dim)
    logits = pair_bias.astype(jnp.float32) + geometry + affinity
    pair_new = logits.astype(jnp.bfloat16)
    mixed = jax.nn.gelu(
        jnp.einsum("hij,hg->gij", pair_new, w_coord1, preferred_element_type=jnp.float32)
    ).astype(jnp.bfloat16)
    strength = jnp.einsum("gij,g->ij", mixed, w_coord2, preferred_element_type=jnp.float32)
    strength = jnp.where(pair_mask == 1, strength, 0.0)
    row_total = jnp.sum(strength, axis=1)
    pulled = jnp.dot(strength, key_table[:3].T, precision=highest)
    displace = (query_table[:3].T * row_total[:, None] - pulled) / all_atoms
    masked = jnp.where(pair_mask[None, :, :] == 1, logits, masked_fill)
    local_max = jnp.max(masked, axis=2)
    global_max = lax.pmax(local_max, "col")
    weights = jnp.exp(masked - global_max[:, :, None])
    denominator = jnp.sum(weights, axis=2)
    numerator = jnp.einsum(
        "hij,jhd->ihd",
        weights.astype(jnp.bfloat16),
        values_block,
        preferred_element_type=jnp.float32,
    ).reshape(query_rows, model_width)
    own_sums, own_totals, own_move = (
        lax.psum_scatter(
            numerator.astype(jnp.bfloat16), "col", scatter_dimension=0, tiled=True
        ).astype(jnp.float32),
        lax.psum_scatter(
            denominator.T.astype(jnp.bfloat16), "col", scatter_dimension=0, tiled=True
        ).astype(jnp.float32),
        lax.psum_scatter(
            displace.astype(jnp.bfloat16), "col", scatter_dimension=0, tiled=True
        ).astype(jnp.float32),
    )
    attended = (
        (own_sums.reshape(own_rows, head_count, head_dim) / own_totals[:, :, None])
        .reshape(own_rows, model_width)
        .astype(jnp.bfloat16)
    )
    moved = coords + own_move.T
    return (attended, moved)


def solution(mesh):
    in_specs = (
        P(("row", "col"), None),
        P(None, ("row", "col")),
        P(("row", "col")),
        P(("row", "col")),
        P("row", "col"),
        P(None, "row", "col"),
        P(),
        P(),
        P(),
        P(),
        P(),
        P(),
        P(),
        P(),
        P(),
        P(),
    )
    out_specs = (P(("row", "col"), None), P(None, ("row", "col")))
    return jax.shard_map(shards, mesh=mesh, in_specs=in_specs, out_specs=out_specs, check_vma=False)
```

profile of v0, /device:TPU:0, one launch (start us, length us, event | category | flops | bytes accessed | tf_op | source)
XLA Modules:
  0.0 129.0 jit_solution(5624946512102041335)
XLA Ops:
  0.6 0.9 convert_reduce_fusion
  1.6 0.9 fusion.64
  2.5 0.8 fusion.73
  3.2 14.8 %all-gather = bf16[4,4,512]{2,1,0:T(4,128)(2,1)S(1)} all-gather(bf16[1,4,512]{2,1,0:T(4,128)(2,1)S(1)} %fusion.73), channel_id=1, replica_groups=mesh['row'=8,'col'=4] {'col'}, dimensions={0}, use_global_device_ids=true | all-gather | bytes 20480 | tf_op jit(solution)/shard_map/all_gather | solution.py:65
  18.0 0.3 convolution_convert_fusion
  18.5 9.5 %all_gather.10 = bf16[128,1024]{1,0:T(8,128)(2,1)S(1)} all-gather(bf16[16,1024]{1,0:T(8,128)(2,1)S(1)} %slice.42), channel_id=1, replica_groups=mesh['row'=8,'col'=4] {'row'}, dimensions={0}, use_global_device_ids=true | all-gather | bytes 294912 | tf_op jit(solution)/shard_map/all_gather | solution.py:69
  27.9 0.1 copy.46
  28.1 0.1 copy.45
  28.2 0.3 fusion.29
  28.5 0.3 copy.47
  28.8 0.1 copy.43
  28.9 68.0 %all-gather.1 = f32[32,4,4]{2,1,0:T(4,128)S(1)} all-gather(f32[1,4,4]{2,1,0:T(4,128)S(1)} %bitcast.91), channel_id=1, replica_groups=mesh['row'=8,'col'=4] {'row','col'}, dimensions={0}, use_global_device_ids=true | all-gather | bytes 2112 | tf_op jit(solution)/shard_map/all_gather | solution.py:61
  97.0 0.2 fusion.53
  97.2 0.1 copy.55
  97.4 0.2 convolution_multiply_fusion
  97.6 0.2 convolution_add_fusion
  97.9 0.4 fusion.1
  98.3 0.4 fusion.23
  98.8 0.1 select_reduce_fusion.1
  98.9 0.2 select_reduce_fusion
  99.0 8.5 %pmax.7 = f32[64,16]{0,1:T(8,128)S(1)} all-reduce(f32[64,16]{0,1:T(8,128)S(1)} %select_reduce_fusion), channel_id=1, replica_groups=mesh['row'=8,'col'=4] {'col'}, use_global_device_ids=true, to_apply=%region_4.5 | all-reduce | flops 1024 | bytes 8192 | tf_op jit(solution)/shard_map/pmax | solution.py:103
  107.6 0.2 fusion.26
  107.8 0.3 copy.48
  108.0 0.1 copy.42
  108.1 0.3 fusion.2
  108.5 0.1 fusion.4
  108.6 17.6 %all-reduce.3 = (bf16[16,64]{1,0:T(8,128)(2,1)S(1)}, bf16[16,512]{1,0:T(8,128)(2,1)S(1)}, bf16[16,3]{0,1:T(4,128)(2,1)S(1)}) all-reduce(bf16[16,64]{1,0:T(8,128)(2,1)S(1)} %bitcast.90, bf16[16,512]{1,0:T(8,128)(2,1)S(1)} %copy.49, bf16[16,3]{0,1:T(4,128)(2,1)S(1)} %fusion.4), channel_id=3, replica_groups=mesh['row'=8,'col'=4] {'col'}, use_global_device_ids=true, to_apply=%region_7.8.clone | all-reduce | flops 9264 | bytes 37056
  126.3 0.6 dynamic-slice.2
  127.5 0.1 div.53
  127.6 0.1 div.54
  127.7 0.6 fusion.71
  128.3 0.6 bitcast_add_fusion
  (47 shorter events, 0.4 us)
Async XLA Ops:
  0.6 17.4 %copy-start = (bf16[512,1536]{1,0:T(8,128)(2,1)S(1)}, bf16[512,1536]{1,0:T(8,128)(2,1)}, u32[]{:S(2)}) copy-start(bf16[512,1536]{1,0:T(8,128)(2,1)} %param.23) | copy-start | bytes 4718596
  18.4 10.4 %copy-start.11 = (f32[128]{0:T(128)S(1)}, f32[128]{0:T(128)}, u32[]{:S(2)}) copy-start(f32[128]{0:T(128)} %param.27) | copy-start | bytes 1540
  18.4 10.4 %copy-start.9 = (s32[4]{0:T(128)S(1)}, s32[4]{0:T(128)}, u32[]{:S(2)}) copy-start(s32[4]{0:T(128)} %param.18) | copy-start | bytes 52
  18.4 10.4 %copy-start.10 = (s32[4]{0:T(128)S(1)}, s32[4]{0:T(128)}, u32[]{:S(2)}) copy-start(s32[4]{0:T(128)} %param.19) | copy-start | bytes 52
  18.4 10.4 %copy-start.4 = (f32[3,4]{1,0:T(4,128)S(1)}, f32[3,4]{1,0:T(4,128)}, u32[]{:S(2)}) copy-start(f32[3,4]{1,0:T(4,128)} %param.17) | copy-start | bytes 148
  18.4 78.6 %copy-start.1 = (f32[60,60]{1,0:T(8,128)S(1)}, f32[60,60]{1,0:T(8,128)}, u32[]{:S(2)}) copy-start(f32[60,60]{1,0:T(8,128)} %param.25) | copy-start | bytes 43204
  18.4 78.6 %copy-start.2 = (f32[60,60]{1,0:T(8,128)S(1)}, f32[60,60]{1,0:T(8,128)}, u32[]{:S(2)}) copy-start(f32[60,60]{1,0:T(8,128)} %param.24) | copy-start | bytes 43204
  18.4 79.4 %copy-start.5 = (bf16[64,16,32]{0,2,1:T(8,128)(2,1)S(1)}, bf16[64,16,32]{0,2,1:T(8,128)(2,1)}, u32[]{:S(2)}) copy-start(bf16[64,16,32]{0,2,1:T(8,128)(2,1)} %param.21) | copy-start | bytes 196612
  18.4 79.4 %copy-start.6 = (bf16[128,128]{1,0:T(8,128)(2,1)S(1)}, bf16[128,128]{1,0:T(8,128)(2,1)}, u32[]{:S(2)}) copy-start(bf16[128,128]{1,0:T(8,128)(2,1)} %param.28) | copy-start | bytes 98308
  18.4 79.4 %copy-start.7 = (bf16[128,64]{0,1:T(8,128)(2,1)S(1)}, bf16[128,64]{0,1:T(8,128)(2,1)}, u32[]{:S(2)}) copy-start(bf16[128,64]{0,1:T(8,128)(2,1)} %param.29) | copy-start | bytes 49156
  18.5 79.4 %copy-start.12 = (f32[128]{0:T(128)S(1)}, f32[128]{0:T(128)}, u32[]{:S(2)}) copy-start(f32[128]{0:T(128)} %param.26) | copy-start | bytes 1540
  97.0 1.3 %copy-start.8 = (bf16[64,64]{1,0:T(8,128)(2,1)S(1)}, bf16[64,64]{1,0:T(8,128)(2,1)}, u32[]{:S(2)}) copy-start(bf16[64,64]{1,0:T(8,128)(2,1)} %param.30) | copy-start | bytes 24580
  97.0 1.3 %copy-start.13 = (bf16[64]{0:T(256)(128)(2,1)S(1)}, bf16[64]{0:T(256)(128)(2,1)}, u32[]{:S(2)}) copy-start(bf16[64]{0:T(256)(128)(2,1)} %param.31) | copy-start | bytes 388
  97.9 0.9 copy-start.3
  98.3 27.9 %copy-start.14 = (u32[32]{0:T(128)S(1)}, u32[32]{0:T(128)}, u32[]{:S(2)}) copy-start(u32[32]{0:T(128)} %constant.64) | copy-start | bytes 388
where the time goes:
time: 129 us
  blocking collectives  118 us (91%)
  other arithmetic  4.41 us (3%)
  matrix products  2.42 us (2%)
  local copies, waits for them, and re-layouts  2.18 us (2%)
  between operations  1.57 us (1%)
    all_gather x1, blocking collectives, shards(): atom_table = lax.all_gather(own_table, ('row', 'col'), axis=1, tiled=True)  68 us
    unnamed x1, blocking collectives  17.6 us
    all_gather x1, blocking collectives, shards(): lax.all_gather(normed, 'col', axis=0, tiled=True)  14.8 us
    all_gather x1, blocking collectives, shards(): every_key = lax.all_gather(row_keys, 'row', axis=0, tiled=True)  9.45 us
    pmax x1, blocking collectives, shards(): global_max = lax.pmax(local_max, 'col')  8.52 us

commit v1 on v0

v1 whole, which is shorter than its diff:
```python
import functools
import math

import jax
import jax.numpy as jnp
from jax import lax
from jax.experimental import pallas as pl
from jax.experimental.pallas import tpu as pltpu
from jax.sharding import PartitionSpec as P

ln_epsilon = 1e-05
masked_fill = -1000000000.0
masked_below = -100000000.0
root_shift = 0.01
lanes = 128
f32 = jnp.float32
bf16 = jnp.bfloat16
nt = (((1,), (1,)), ((), ()))
tn = (((0,), (0,)), ((), ()))


def split3(x):
    hi = x.astype(bf16).astype(f32)
    mid = (x - hi).astype(bf16).astype(f32)
    return hi, mid, x - hi - mid


def iota(shape, axis):
    return lax.broadcasted_iota(jnp.int32, shape, axis)


def column(row):
    n = row.shape[1]
    square = jnp.where(iota((n, n), 0) == iota((n, n), 1), jnp.broadcast_to(row, (n, n)), 0.0)
    return jnp.sum(square, axis=1, keepdims=True)


def gelu(x):
    inner = x * (0.7978845608028654 + 0.035677408136300125 * (x * x))
    return (0.5 * x) * (1.0 + jnp.tanh(inner))


def node_rows(width, own):
    return -(-(width // lanes + 1) * own // 16) * 16


def pack_kernel(dims, nodes, coords, types, segments, mask, bias, *refs):
    own, cols, width, heads, keys, kinds = dims
    outs, held = refs[:cols], refs[cols]
    queries = own * cols
    me = lax.axis_index("col")
    pieces = own * keys // lanes
    lane, row = iota((own, lanes), 1), iota((own, lanes), 0)
    table = jnp.zeros((own, lanes), f32)
    for c in range(3):
        for n, part in enumerate(split3(column(coords[c : c + 1, :]))):
            table = jnp.where(lane == 3 * n + c, part, table)
    for t in range(own):
        kind = (types[t] + kinds // 2 * segments[t]).astype(f32)
        table = jnp.where((lane == 9) & (row == t), kind, table)
    full = nodes[...].astype(f32)
    blocks = [full[:, b * lanes : (b + 1) * lanes] for b in range(width // lanes)] + [table]
    used = len(blocks) * own
    blocks.append(jnp.zeros((node_rows(width, own) - used, lanes), f32))
    packed = jnp.concatenate(blocks, axis=0).astype(bf16)
    for out in outs:
        out[pieces * heads :, :] = packed
    kept = jnp.where(mask[...][None] == 1, bias[...].astype(f32), masked_fill)
    held[:, :keys] = kept.reshape(heads * queries, keys)
    blocks_of = refs[cols + 1]
    for d in range(cols):
        rows = [held[pl.ds(d * own + i, heads, stride=queries), :][:, :keys] for i in range(own)]
        wide = jnp.concatenate(rows, axis=1).astype(bf16)
        for b in range(pieces):
            blocks_of[d, b * heads : (b + 1) * heads, :] = wide[:, b * lanes : (b + 1) * lanes]
    for k in range(cols):
        outs[k][: pieces * heads, :] = blocks_of[me ^ k]


def gather_kernel(dims, *refs):
    own, cols, width, heads, keys, kinds = dims
    start = own * keys // lanes * heads
    out = refs[cols]
    blocks = [ref[start:, :].astype(f32) for ref in refs[:cols]]
    for b in range(width // lanes + 1):
        rows = jnp.concatenate([block[b * own : (b + 1) * own] for block in blocks], axis=0)
        out[:, b * lanes : (b + 1) * lanes] = rows.astype(bf16)


def arrange_kernel(dims, *refs):
    own, cols, width, heads, keys, kinds = dims
    out = refs[cols]
    atoms = out.shape[1]
    per_row = own * cols
    r, c = lax.axis_index("row"), lax.axis_index("col")
    wide = [
        jnp.concatenate(
            [ref[b * heads : (b + 1) * heads, :].astype(f32) for b in range(own * keys // lanes)],
            axis=1,
        )
        for ref in refs[:cols]
    ]
    blocks = [
        jnp.concatenate([w[:, i * keys : (i + 1) * keys] for i in range(own)], axis=0).astype(bf16)
        for w in wide
    ]
    step = max(lanes // keys, 1)
    for s in range(0, atoms, lanes):
        slot = s + iota((1, lanes), 1)
        source = ((r ^ (slot // per_row)) * cols + (c ^ (slot % per_row // own))) * own + slot % own
        total = jnp.zeros((own * heads, lanes), f32)
        for k in range(0, cols, step):
            place = iota((step * keys, 1), 0)
            atom = (c ^ (k + place // keys)) * keys + place % keys
            chosen = (atom == source).astype(f32).astype(bf16)
            taken = jnp.concatenate([blocks[k + n] for n in range(step)], axis=1)
            total = total + jnp.dot(taken, chosen, preferred_element_type=f32)
        out[:, s : s + lanes] = total.astype(bf16)


def attend_kernel(
    dims,
    near,
    far,
    bias,
    coords,
    ln_gain,
    w_qkv,
    gauss_mul,
    gauss_add,
    gauss_mean,
    gauss_width,
    w_gauss,
    w_heads,
    w_coord1,
    w_coord2,
    attended,
    moved,
    logits,
    values,
    places,
    strengths,
):
    own, cols, width, heads, keys, kinds = dims
    atoms = bias.shape[1]
    head_dim = width // heads
    half = near.shape[0]
    gain = ln_gain[...]

    def normed(x):
        features = x.astype(f32)
        centred = features - jnp.mean(features, axis=1, keepdims=True)
        spread = jnp.mean(centred * centred, axis=1, keepdims=True)
        return (centred * lax.rsqrt(spread + ln_epsilon) * gain).astype(bf16)

    own_table = near[:16, width:].astype(f32)
    own_columns = [
        (own_table[:, c : c + 1] + own_table[:, 3 + c : 4 + c]) + own_table[:, 6 + c : 7 + c]
        for c in range(3)
    ]
    own_kind = own_table[:, 9:10].astype(jnp.int32)
    query_onehot = (own_kind == iota((16, kinds), 1)).astype(f32).astype(bf16)
    looked = []
    for table in (gauss_mul, gauss_add):
        parts = [
            jnp.dot(query_onehot, part.astype(bf16), preferred_element_type=f32)
            for part in split3(table[...])
        ]
        looked.extend(part.astype(bf16) for part in parts)
    lookup = jnp.concatenate(looked, axis=0)
    inverse = 1.0 / column(gauss_width[...])
    centre = column(gauss_mean[...])
    sharp = inverse * math.sqrt(0.5 * math.log2(math.e))
    norming = jnp.log2(inverse * (1.0 / math.sqrt(2.0 * math.pi)))
    queries = jnp.dot(normed(near[:16, :width]), w_qkv[:, :width], preferred_element_type=f32)
    head_mask = iota((heads, width), 1) // head_dim == iota((heads, width), 0)
    spread_queries = jnp.concatenate(
        [
            jnp.where(head_mask, jnp.broadcast_to(queries[i : i + 1], (heads, width)), 0.0)
            for i in range(own)
        ],
        axis=0,
    ).astype(bf16)
    select_at, select_from = iota((16, lanes), 0), iota((16, lanes), 1)
    selector = (
        ((select_from < 9) & (select_from % 3 == select_at) & (select_at < 3))
        | ((select_from == 9) & (select_at == 3))
    ).astype(f32).astype(bf16)

    for s in range(0, atoms, lanes):
        if half < lanes:
            x = jnp.concatenate([near[...], far[...]], axis=0)
        elif s < half:
            x = near[s : s + lanes, :]
        else:
            x = far[s - half : s - half + lanes, :]
        block = normed(x[:, :width])
        both = jnp.dot(block, w_qkv[:, width:], preferred_element_type=f32).astype(bf16)
        values[s : s + lanes, :] = both[:, width:]
        table = lax.dot_general(selector, x[:, width:], nt, preferred_element_type=f32)
        places[:, s : s + lanes] = jnp.where(iota((16, lanes), 0) == 3, 1.0, table)
        offsets = [own_columns[c] - table[c : c + 1] for c in range(3)]
        squares = offsets[0] * offsets[0] + offsets[1] * offsets[1] + offsets[2] * offsets[2]
        distance = jnp.sqrt(squares + root_shift)
        key_onehot = (table[3:4].astype(jnp.int32) == iota((kinds, lanes), 0)).astype(f32).astype(bf16)
        found = jnp.dot(lookup, key_onehot, preferred_element_type=f32)
        scale = found[0:16] + found[16:32] + found[32:48]
        shift = found[48:64] + found[64:80] + found[80:96]
        expanded = scale * distance + shift
        features = []
        for i in range(own):
            scaled = (expanded[i : i + 1] - centre) * sharp
            features.append(jnp.exp2(norming - scaled * scaled).astype(bf16))
        hidden = lax.dot_general(
            w_gauss[...], jnp.concatenate(features, axis=1), tn, preferred_element_type=f32
        )
        geometry = lax.dot_general(
            w_heads[...], gelu(hidden).astype(bf16), tn, preferred_element_type=f32
        )
        affinity = lax.dot_general(spread_queries, both[:, :width], nt, preferred_element_type=f32)
        here = bias[:, s : s + lanes].astype(f32)
        rows = []
        for i in range(own):
            at = slice(i * heads, (i + 1) * heads)
            row = here[at] + geometry[:, i * lanes : (i + 1) * lanes]
            row = row + affinity[at] * (1.0 / math.sqrt(head_dim))
            logits[at, s : s + lanes] = jnp.where(here[at] < masked_below, masked_fill, row)
            rows.append(row.astype(bf16))
        mixed = lax.dot_general(
            w_coord1[...], jnp.concatenate(rows, axis=1), tn, preferred_element_type=f32
        )
        strength = jnp.dot(w_coord2[...], gelu(mixed).astype(bf16), preferred_element_type=f32)
        strengths[:, s : s + lanes] = jnp.concatenate(
            [
                jnp.where(
                    here[i * heads : i * heads + 1] < masked_below,
                    0.0,
                    strength[:, i * lanes : (i + 1) * lanes],
                )
                for i in range(own)
            ],
            axis=0,
        )

    masked = logits[...]
    weights = jnp.exp(masked - jnp.max(masked, axis=1, keepdims=True))
    share = 1.0 / jnp.sum(weights, axis=1, keepdims=True)
    taken = jnp.dot(weights.astype(bf16), values[...], preferred_element_type=f32) * share
    attended[...] = jnp.concatenate(
        [
            jnp.sum(
                jnp.where(head_mask, taken[i * heads : (i + 1) * heads], 0.0), axis=0, keepdims=True
            )
            for i in range(own)
        ],
        axis=0,
    ).astype(bf16)
    pulled = lax.dot_general(
        places[...],
        strengths[...],
        nt,
        precision=lax.Precision.HIGHEST,
        preferred_element_type=f32,
    )
    here = coords[...]
    moved[...] = here + (here * pulled[3:4] - pulled[0:3]) * (1.0 / atoms)


def shards(
    nodes,
    coords,
    atom_types,
    segment_ids,
    pair_mask,
    pair_bias,
    ln_gain,
    w_qkv,
    gauss_mul,
    gauss_add,
    gauss_mean,
    gauss_width,
    w_gauss,
    w_heads,
    w_coord1,
    w_coord2,
):
    cols, rows = lax.axis_size("col"), lax.axis_size("row")
    own, width = nodes.shape
    heads, queries, keys = pair_bias.shape
    kinds = gauss_mul.shape[0]
    atoms = own * rows * cols
    dims = (own, cols, width, heads, keys, kinds)
    payload = jax.ShapeDtypeStruct((own * keys // lanes * heads + node_rows(width, own), lanes), bf16)
    params = pltpu.CompilerParams(vmem_limit_bytes=(16 if atoms <= 128 else 56) * 2**20)
    vmem, smem = pl.BlockSpec(memory_space=pltpu.VMEM), pl.BlockSpec(memory_space=pltpu.SMEM)
    packed = pl.pallas_call(
        functools.partial(pack_kernel, dims),
        out_shape=[payload] * cols,
        in_specs=[vmem, vmem, smem, smem, vmem, vmem],
        out_specs=[vmem] * cols,
        scratch_shapes=[
            pltpu.VMEM((heads * queries, lanes), f32),
            pltpu.VMEM((cols, own * keys // lanes * heads, lanes), bf16),
        ],
        compiler_params=params,
        name="pack",
    )(nodes, coords, atom_types, segment_ids, pair_mask, pair_bias)
    arrived = [packed[0]] + [
        lax.ppermute(packed[k], "col", [(i, i ^ k) for i in range(cols)]) for k in range(1, cols)
    ]
    near = pl.pallas_call(
        functools.partial(gather_kernel, dims),
        out_shape=jax.ShapeDtypeStruct((own * cols, width + lanes), bf16),
        in_specs=[vmem] * cols,
        out_specs=vmem,
        compiler_params=params,
        name="gather",
    )(*arrived)
    bias = pl.pallas_call(
        functools.partial(arrange_kernel, dims),
        out_shape=jax.ShapeDtypeStruct((own * heads, atoms), bf16),
        in_specs=[vmem] * cols,
        out_specs=vmem,
        compiler_params=params,
        name="arrange",
    )(*arrived)
    step = 1
    while True:
        far = lax.ppermute(near, "row", [(i, i ^ step) for i in range(rows)])
        step *= 2
        if step == rows:
            break
        near = jnp.concatenate([near, far], axis=0)
    attended, moved = pl.pallas_call(
        functools.partial(attend_kernel, dims),
        out_shape=[
            jax.ShapeDtypeStruct((own, width), bf16),
            jax.ShapeDtypeStruct((3, own), f32),
        ],
        in_specs=[vmem] * 14,
        out_specs=[vmem] * 2,
        scratch_shapes=[
            pltpu.VMEM((own * heads, atoms), f32),
            pltpu.VMEM((atoms, width), bf16),
            pltpu.VMEM((16, atoms), f32),
            pltpu.VMEM((own, atoms), f32),
        ],
        compiler_params=params,
        name="attend",
    )(
        near,
        far,
        bias,
        coords,
        ln_gain[None, :],
        w_qkv,
        gauss_mul,
        gauss_add,
        gauss_mean[None, :],
        gauss_width[None, :],
        w_gauss,
        w_heads,
        w_coord1,
        w_coord2[None, :],
    )
    return attended, moved


def solution(mesh):
    own, tile, whole = P(("row", "col")), P("row", "col"), P()
    in_specs = (
        P(("row", "col"), None),
        P(None, ("row", "col")),
        own,
        own,
        tile,
        P(None, "row", "col"),
    ) + (whole,) * 10
    out_specs = (P(("row", "col"), None), P(None, ("row", "col")))
    return jax.shard_map(shards, mesh=mesh, in_specs=in_specs, out_specs=out_specs, check_vma=False)
```

time: 129 us -> 37.7 us (0.29)
  blocking collectives: 118 us -> 0 us
  waiting for transfers between devices: 0 us -> 11.1 us
  local copies, waits for them, and re-layouts: 2.18 us -> 13.1 us
  starting transfers between devices: 0 us -> 8.83 us
  other arithmetic: 4.41 us -> 0.01 us
  Pallas kernels: 0 us -> 3.38 us
  matrix products: 2.42 us -> 0 us
    all_gather x3 -> x0, blocking collectives: 92.2 us -> none  [the longest x1 68 us: shards(): atom_table = lax.all_gather(own_table, ('row', 'col'), axis=1, tiled=True)]
    unnamed x1 -> x0, blocking collectives: 17.6 us -> none
    unnamed x37 -> x32, local copies, waits for them, and re-layouts: 0.99 us -> 13.1 us
    ppermute x0 -> x6, waiting for transfers between devices: none -> 11.1 us  [the longest x3 5.62 us: shards(): lax.ppermute(packed[k], 'col', [(i, i ^ k) for i in range(cols)])]
    ppermute x0 -> x6, starting transfers between devices: none -> 8.83 us  [the longest x3 5.68 us: shards(): lax.ppermute(packed[k], 'col', [(i, i ^ k) for i in range(cols)])]
    pmax x1 -> x0, blocking collectives: 8.52 us -> none  [shards(): global_max = lax.pmax(local_max, 'col')]
    pallas_call x0 -> x4, Pallas kernels: none -> 3.38 us  [the longest x1 2.27 us: shards(): pl.pallas_call(functools.partial(attend_kernel, dims), out_shape=[jax.Sha...]
    dot_general x9 -> x0, matrix products: 2.42 us -> none  [the longest x1 0.42 us: shards(): jnp.einsum('gij,g->ij', mixed, w_coord2, preferred_element_type=jnp.float32)]
  transfers between devices with their start and end apart: 0 -> 6, of which waited for: 0 -> 5; matrix products, arithmetic and copies ran while one was open for 0% -> 2% of each run, Pallas kernels for 0% -> 1%
where the time goes in v1:
time: 37.7 us; the launch traced here: 37.1 us
  local copies, waits for them, and re-layouts  13.1 us (35%)
  waiting for transfers between devices  11.1 us (29%)
  starting transfers between devices  8.83 us (23%)
  Pallas kernels  3.38 us (9%)
  between operations  0.69 us (2%)
    unnamed x32, local copies, waits for them, and re-layouts  13.1 us
    ppermute x3, starting transfers between devices, shards(): lax.ppermute(packed[k], 'col', [(i, i ^ k) for i in range(cols)])  5.68 us
    ppermute x3, waiting for transfers between devices, shards(): lax.ppermute(packed[k], 'col', [(i, i ^ k) for i in range(cols)])  5.62 us
    ppermute x3, waiting for transfers between devices, shards(): far = lax.ppermute(near, 'row', [(i, i ^ step) for i in range(rows)])  5.47 us
    ppermute x3, starting transfers between devices, shards(): far = lax.ppermute(near, 'row', [(i, i ^ step) for i in range(rows)])  3.15 us
    pallas_call x1, Pallas kernels, shards(): pl.pallas_call(functools.partial(attend_kernel, dims), out_shape=[jax.Sha...  2.27 us
    pallas_call x1, Pallas kernels, shards(): pl.pallas_call(functools.partial(pack_kernel, dims), out_shape=[payload]...  0.79 us
  transfers between devices with their start and end apart: 6, of which 5 were waited for; matrix products, arithmetic and copies ran while one was open for 2% of the time, Pallas kernels for 1%

profile of v1, /device:TPU:0, one launch (start us, length us, event | category | flops | bytes accessed | tf_op | source)
XLA Modules:
  0.0 37.1 jit_solution(10463080404475969401)
XLA Ops:
  0.6 1.1 %copy.18.bias = bf16[64,16,32]{2,1,0:T(8,128)(2,1)S(1)} copy(bf16[64,16,32]{0,2,1:T(8,128)(2,1)} %param.21) | data formatting | bytes 131072 | tf_op args[5]
  1.8 0.0 copy-start.5
  1.8 0.7 %copy-done.5 = s32[16,32]{1,0:T(8,128)S(1)} copy-done((s32[16,32]{1,0:T(8,128)S(1)}, s32[16,32]{1,0:T(8,128)}, u32[]{:S(2)}) %copy-start.5) | copy-done | bytes 2072
  2.5 0.7 %copy-done.6 = f32[3,4]{1,0:T(4,128)S(1)} copy-done((f32[3,4]{1,0:T(4,128)S(1)}, f32[3,4]{1,0:T(4,128)}, u32[]{:S(2)}) %copy-start.6) | copy-done | bytes 72
  3.2 0.7 %copy-done.8 = bf16[4,512]{1,0:T(4,128)(2,1)S(1)} copy-done((bf16[4,512]{1,0:T(4,128)(2,1)S(1)}, bf16[4,512]{1,0:T(4,128)(2,1)}, u32[]{:S(2)}) %copy-start.8) | copy-done | bytes 4120
  3.9 0.7 %copy-done.10 = s32[4]{0:T(128)S(1)} copy-done((s32[4]{0:T(128)S(1)}, s32[4]{0:T(128)}, u32[]{:S(2)}) %copy-start.10) | copy-done | bytes 40
  4.5 0.7 %copy-done.11 = s32[4]{0:T(128)S(1)} copy-done((s32[4]{0:T(128)S(1)}, s32[4]{0:T(128)}, u32[]{:S(2)}) %copy-start.11) | copy-done | bytes 40
  5.2 0.8 %pack.1 = (bf16[96,128]{1,0:T(8,128)(2,1)S(1)}, bf16[96,128]{1,0:T(8,128)(2,1)S(1)}, bf16[96,128]{1,0:T(8,128)(2,1)S(1)}, bf16[96,128]{1,0:T(8,128)(2,1)S(1)}) custom-call(bf16[4,512]{1,0:T(4,128)(2,1)S(1)} %copy-done.8, f32[3,4]{1,0:T(4,128)S(1)} %copy-done.6, s32[4]{0:T(128)S(1)} %copy-done.10, s32[4]{0:T(128)S(1)} %copy-done.11, s32[16,32]{1,0:T(8,128)S(1)} %copy-done.5, ...), custom_call_target="tpu_custom_call" | custom-call | tf_op jit(solution)/shard_map/pack/pallas_call | solution.py:296
  6.0 3.1 %collective-permute-start = (bf16[96,128]{1,0:T(8,128)(2,1)S(1)}, bf16[96,128]{1,0:T(8,128)(2,1)S(1)}, u32[]{:S(2)}, u32[]{:S(2)}) collective-permute-start(bf16[96,128]{1,0:T(8,128)(2,1)S(1)} %get-tuple-element.7), channel_id=1, source_target_pairs={{0,1},{1,0},{2,3},{3,2},{4,5},{5,4},{6,7},{7,6},{8,9},{9,8},{10,11... | collective-permute-start | bytes 73736 | tf_op jit(solution)/shard_map/ppermute | solution.py:309
  9.0 2.6 %collective-permute-start.1 = (bf16[96,128]{1,0:T(8,128)(2,1)S(1)}, bf16[96,128]{1,0:T(8,128)(2,1)S(1)}, u32[]{:S(2)}, u32[]{:S(2)}) collective-permute-start(bf16[96,128]{1,0:T(8,128)(2,1)S(1)} %get-tuple-element.8), channel_id=1, source_target_pairs={{0,2},{1,3},{2,0},{3,1},{4,6},{5,7},{6,4},{7,5},{8,10},{9,11},{10,... | collective-permute-start | bytes 73736 | tf_op jit(solution)/shard_map/ppermute | solution.py:309
  11.6 0.0 collective-permute-start.2
  11.6 2.5 %collective-permute-done.1.refs_2_ = bf16[96,128]{1,0:T(8,128)(2,1)S(1)} collective-permute-done((bf16[96,128]{1,0:T(8,128)(2,1)S(1)}, bf16[96,128]{1,0:T(8,128)(2,1)S(1)}, u32[]{:S(2)}, u32[]{:S(2)}) %collective-permute-start.1) | collective-permute-done | bytes 24608 | tf_op jit(solution)/shard_map/ppermute | solution.py:309
  14.1 3.1 %collective-permute-done.2.refs_3_ = bf16[96,128]{1,0:T(8,128)(2,1)S(1)} collective-permute-done((bf16[96,128]{1,0:T(8,128)(2,1)S(1)}, bf16[96,128]{1,0:T(8,128)(2,1)S(1)}, u32[]{:S(2)}, u32[]{:S(2)}) %collective-permute-start.2) | collective-permute-done | bytes 24608 | tf_op jit(solution)/shard_map/ppermute | solution.py:309
  17.3 0.1 collective-permute-start.3
  17.4 1.2 %collective-permute-done.3 = bf16[16,640]{1,0:T(8,128)(2,1)S(1)} collective-permute-done((bf16[16,640]{1,0:T(8,128)(2,1)S(1)}, bf16[16,640]{1,0:T(8,128)(2,1)S(1)}, u32[]{:S(2)}, u32[]{:S(2)}) %collective-permute-start.3) | collective-permute-done | bytes 20512 | tf_op jit(solution)/shard_map/ppermute | solution.py:329
  18.5 1.5 %collective-permute-start.4 = (bf16[32,640]{1,0:T(8,128)(2,1)S(1)}, bf16[32,640]{1,0:T(8,128)(2,1)S(1)}, u32[]{:S(2)}, u32[]{:S(2)}) collective-permute-start(bf16[32,640]{1,0:T(8,128)(2,1)S(1)} %pad_maximum_fusion.1), channel_id=1, source_target_pairs={{0,8},{4,12},{8,0},{12,4},{16,24},{20,28},{24,16},{28,20},{1,9},{5... | collective-permute-start | bytes 122888 | tf_op jit(solution)/shard_map/ppermute | solution.py:329
  20.0 2.5 %collective-permute-done.4 = bf16[32,640]{1,0:T(8,128)(2,1)S(1)} collective-permute-done((bf16[32,640]{1,0:T(8,128)(2,1)S(1)}, bf16[32,640]{1,0:T(8,128)(2,1)S(1)}, u32[]{:S(2)}, u32[]{:S(2)}) %collective-permute-start.4) | collective-permute-done | bytes 40992 | tf_op jit(solution)/shard_map/ppermute | solution.py:329
  22.5 1.6 %collective-permute-start.5 = (bf16[64,640]{1,0:T(8,128)(2,1)S(1)}, bf16[64,640]{1,0:T(8,128)(2,1)S(1)}, u32[]{:S(2)}, u32[]{:S(2)}) collective-permute-start(bf16[64,640]{1,0:T(8,128)(2,1)S(1)} %pad_maximum_fusion.near), channel_id=1, source_target_pairs={{0,16},{4,20},{8,24},{12,28},{16,0},{20,4},{24,8},{28,12},{1,17},{... | collective-permute-start | bytes 245768 | tf_op jit(solution)/shard_map/ppermute | solution.py:329
  24.1 0.8 %copy.19.w_heads = bf16[128,64]{1,0:T(8,128)(2,1)S(1)} copy(bf16[128,64]{0,1:T(8,128)(2,1)} %param.29) | data formatting | bytes 32768 | tf_op args[13]
  25.0 0.3 arrange.1.bias
  25.3 1.8 %collective-permute-done.5.far = bf16[64,640]{1,0:T(8,128)(2,1)S(1)} collective-permute-done((bf16[64,640]{1,0:T(8,128)(2,1)S(1)}, bf16[64,640]{1,0:T(8,128)(2,1)S(1)}, u32[]{:S(2)}, u32[]{:S(2)}) %collective-permute-start.5) | collective-permute-done | bytes 81952 | tf_op jit(solution)/shard_map/ppermute | solution.py:329
  27.1 1.4 %copy-done = bf16[512,1536]{1,0:T(8,128)(2,1)S(1)} copy-done((bf16[512,1536]{1,0:T(8,128)(2,1)S(1)}, bf16[512,1536]{1,0:T(8,128)(2,1)}, u32[]{:S(2)}) %copy-start) | copy-done | bytes 1572888
  28.5 0.8 %copy-done.1 = f32[60,60]{1,0:T(8,128)S(1)} copy-done((f32[60,60]{1,0:T(8,128)S(1)}, f32[60,60]{1,0:T(8,128)}, u32[]{:S(2)}) %copy-start.1) | copy-done | bytes 14424
  29.2 0.8 %copy-done.2 = f32[60,60]{1,0:T(8,128)S(1)} copy-done((f32[60,60]{1,0:T(8,128)S(1)}, f32[60,60]{1,0:T(8,128)}, u32[]{:S(2)}) %copy-start.2) | copy-done | bytes 14424
  30.0 0.8 %copy-done.3 = bf16[128,128]{1,0:T(8,128)(2,1)S(1)} copy-done((bf16[128,128]{1,0:T(8,128)(2,1)S(1)}, bf16[128,128]{1,0:T(8,128)(2,1)}, u32[]{:S(2)}) %copy-start.3) | copy-done | bytes 32792
  30.7 0.7 %copy-done.4 = bf16[64,64]{1,0:T(8,128)(2,1)S(1)} copy-done((bf16[64,64]{1,0:T(8,128)(2,1)S(1)}, bf16[64,64]{1,0:T(8,128)(2,1)}, u32[]{:S(2)}) %copy-start.4) | copy-done | bytes 8216
  31.5 0.7 %copy-done.7 = f32[3,4]{1,0:T(4,128)S(1)} copy-done((f32[3,4]{1,0:T(4,128)S(1)}, f32[3,4]{1,0:T(4,128)}, u32[]{:S(2)}) %copy-start.7) | copy-done | bytes 72
  32.1 0.7 %copy-done.9 = f32[512]{0:T(512)S(1)} copy-done((f32[512]{0:T(512)S(1)}, f32[512]{0:T(512)}, u32[]{:S(2)}) %copy-start.9) | copy-done | bytes 2072
  32.8 0.7 %copy-done.12 = f32[128]{0:T(128)S(1)} copy-done((f32[128]{0:T(128)S(1)}, f32[128]{0:T(128)}, u32[]{:S(2)}) %copy-start.12) | copy-done | bytes 536
  33.5 0.7 %copy-done.13 = f32[128]{0:T(128)S(1)} copy-done((f32[128]{0:T(128)S(1)}, f32[128]{0:T(128)}, u32[]{:S(2)}) %copy-start.13) | copy-done | bytes 536
  34.1 0.7 %copy-done.14 = bf16[64]{0:T(256)(128)(2,1)S(1)} copy-done((bf16[64]{0:T(256)(128)(2,1)S(1)}, bf16[64]{0:T(256)(128)(2,1)}, u32[]{:S(2)}) %copy-start.14) | copy-done | bytes 152
  34.8 2.3 %attend.1 = (bf16[4,512]{1,0:T(4,128)(2,1)}, f32[3,4]{1,0:T(4,128)}) custom-call(bf16[64,640]{1,0:T(8,128)(2,1)S(1)} %pad_maximum_fusion.near, bf16[64,640]{1,0:T(8,128)(2,1)S(1)} %collective-permute-done.5.far, bf16[256,128]{1,0:T(8,128)(2,1)S(1)} %arrange.1.bias, f32[3,4]{1,0:T(4,128)S(1)} %copy-done.7, f32[1,512]{1,0:T(1,128)S(1)} %bitcast.4, ...), custom_call_target="tpu_custom_call" | custom-call | tf_op jit(solution)/shard_map/attend/pallas_call | solution.py:334
  (18 shorter events, 0.0 us)
Async XLA Ops:
  1.8 0.7 %copy-start.5 = (s32[16,32]{1,0:T(8,128)S(1)}, s32[16,32]{1,0:T(8,128)}, u32[]{:S(2)}) copy-start(s32[16,32]{1,0:T(8,128)} %mask.1) | copy-start | bytes 6148
  2.5 0.7 %copy-start.6 = (f32[3,4]{1,0:T(4,128)S(1)}, f32[3,4]{1,0:T(4,128)}, u32[]{:S(2)}) copy-start(f32[3,4]{1,0:T(4,128)} %coords.3) | copy-start | bytes 148
  3.2 0.7 %copy-start.8 = (bf16[4,512]{1,0:T(4,128)(2,1)S(1)}, bf16[4,512]{1,0:T(4,128)(2,1)}, u32[]{:S(2)}) copy-start(bf16[4,512]{1,0:T(4,128)(2,1)} %nodes.1) | copy-start | bytes 12292
  3.9 0.7 %copy-start.10 = (s32[4]{0:T(128)S(1)}, s32[4]{0:T(128)}, u32[]{:S(2)}) copy-start(s32[4]{0:T(128)} %types.1) | copy-start | bytes 52
  4.5 0.7 %copy-start.11 = (s32[4]{0:T(128)S(1)}, s32[4]{0:T(128)}, u32[]{:S(2)}) copy-start(s32[4]{0:T(128)} %segments.1) | copy-start | bytes 52
  6.0 5.7 %collective-permute-start = (bf16[96,128]{1,0:T(8,128)(2,1)S(1)}, bf16[96,128]{1,0:T(8,128)(2,1)S(1)}, u32[]{:S(2)}, u32[]{:S(2)}) collective-permute-start(bf16[96,128]{1,0:T(8,128)(2,1)S(1)} %get-tuple-element.7), channel_id=1, source_target_pairs={{0,1},{1,0},{2,3},{3,2},{4,5},{5,4},{6,7},{7,6},{8,9},{9,8},{10,11... | collective-permute-start | bytes 73736 | tf_op jit(solution)/shard_map/ppermute | solution.py:309
  9.0 5.1 %collective-permute-start.1 = (bf16[96,128]{1,0:T(8,128)(2,1)S(1)}, bf16[96,128]{1,0:T(8,128)(2,1)S(1)}, u32[]{:S(2)}, u32[]{:S(2)}) collective-permute-start(bf16[96,128]{1,0:T(8,128)(2,1)S(1)} %get-tuple-element.8), channel_id=1, source_target_pairs={{0,2},{1,3},{2,0},{3,1},{4,6},{5,7},{6,4},{7,5},{8,10},{9,11},{10,... | collective-permute-start | bytes 73736 | tf_op jit(solution)/shard_map/ppermute | solution.py:309
  11.6 5.6 %collective-permute-start.2 = (bf16[96,128]{1,0:T(8,128)(2,1)S(1)}, bf16[96,128]{1,0:T(8,128)(2,1)S(1)}, u32[]{:S(2)}, u32[]{:S(2)}) collective-permute-start(bf16[96,128]{1,0:T(8,128)(2,1)S(1)} %get-tuple-element.9), channel_id=1, source_target_pairs={{0,3},{1,2},{2,1},{3,0},{4,7},{5,6},{6,5},{7,4},{8,11},{9,10},{10,... | collective-permute-start | bytes 73736 | tf_op jit(solution)/shard_map/ppermute | solution.py:309
  17.3 1.3 %collective-permute-start.3 = (bf16[16,640]{1,0:T(8,128)(2,1)S(1)}, bf16[16,640]{1,0:T(8,128)(2,1)S(1)}, u32[]{:S(2)}, u32[]{:S(2)}) collective-permute-start(bf16[16,640]{1,0:T(8,128)(2,1)S(1)} %gather.1), channel_id=1, source_target_pairs={{0,4},{4,0},{8,12},{12,8},{16,20},{20,16},{24,28},{28,24},{1,5},{5... | collective-permute-start | bytes 61448 | tf_op jit(solution)/shard_map/ppermute | solution.py:329
  18.5 4.0 %collective-permute-start.4 = (bf16[32,640]{1,0:T(8,128)(2,1)S(1)}, bf16[32,640]{1,0:T(8,128)(2,1)S(1)}, u32[]{:S(2)}, u32[]{:S(2)}) collective-permute-start(bf16[32,640]{1,0:T(8,128)(2,1)S(1)} %pad_maximum_fusion.1), channel_id=1, source_target_pairs={{0,8},{4,12},{8,0},{12,4},{16,24},{20,28},{24,16},{28,20},{1,9},{5... | collective-permute-start | bytes 122888 | tf_op jit(solution)/shard_map/ppermute | solution.py:329
  22.5 4.5 %collective-permute-start.5 = (bf16[64,640]{1,0:T(8,128)(2,1)S(1)}, bf16[64,640]{1,0:T(8,128)(2,1)S(1)}, u32[]{:S(2)}, u32[]{:S(2)}) collective-permute-start(bf16[64,640]{1,0:T(8,128)(2,1)S(1)} %pad_maximum_fusion.near), channel_id=1, source_target_pairs={{0,16},{4,20},{8,24},{12,28},{16,0},{20,4},{24,8},{28,12},{1,17},{... | collective-permute-start | bytes 245768 | tf_op jit(solution)/shard_map/ppermute | solution.py:329
  27.1 1.4 %copy-start = (bf16[512,1536]{1,0:T(8,128)(2,1)S(1)}, bf16[512,1536]{1,0:T(8,128)(2,1)}, u32[]{:S(2)}) copy-start(bf16[512,1536]{1,0:T(8,128)(2,1)} %w_qkv.1) | copy-start | bytes 4718596
  28.5 0.8 %copy-start.1 = (f32[60,60]{1,0:T(8,128)S(1)}, f32[60,60]{1,0:T(8,128)}, u32[]{:S(2)}) copy-start(f32[60,60]{1,0:T(8,128)} %gauss_mul.1) | copy-start | bytes 43204
  29.2 0.8 %copy-start.2 = (f32[60,60]{1,0:T(8,128)S(1)}, f32[60,60]{1,0:T(8,128)}, u32[]{:S(2)}) copy-start(f32[60,60]{1,0:T(8,128)} %gauss_add.1) | copy-start | bytes 43204
  30.0 0.8 %copy-start.3 = (bf16[128,128]{1,0:T(8,128)(2,1)S(1)}, bf16[128,128]{1,0:T(8,128)(2,1)}, u32[]{:S(2)}) copy-start(bf16[128,128]{1,0:T(8,128)(2,1)} %w_gauss.1) | copy-start | bytes 98308
  30.7 0.7 %copy-start.4 = (bf16[64,64]{1,0:T(8,128)(2,1)S(1)}, bf16[64,64]{1,0:T(8,128)(2,1)}, u32[]{:S(2)}) copy-start(bf16[64,64]{1,0:T(8,128)(2,1)} %w_coord1.1) | copy-start | bytes 24580
  31.5 0.7 %copy-start.7 = (f32[3,4]{1,0:T(4,128)S(1)}, f32[3,4]{1,0:T(4,128)}, u32[]{:S(2)}) copy-start(f32[3,4]{1,0:T(4,128)} %coords.3) | copy-start | bytes 148
  32.1 0.7 %copy-start.9 = (f32[512]{0:T(512)S(1)}, f32[512]{0:T(512)}, u32[]{:S(2)}) copy-start(f32[512]{0:T(512)} %param.22) | copy-start | bytes 6148
  32.8 0.7 %copy-start.12 = (f32[128]{0:T(128)S(1)}, f32[128]{0:T(128)}, u32[]{:S(2)}) copy-start(f32[128]{0:T(128)} %param.26) | copy-start | bytes 1540
  33.5 0.7 %copy-start.13 = (f32[128]{0:T(128)S(1)}, f32[128]{0:T(128)}, u32[]{:S(2)}) copy-start(f32[128]{0:T(128)} %param.27) | copy-start | bytes 1540
  34.1 0.7 %copy-start.14 = (bf16[64]{0:T(256)(128)(2,1)S(1)}, bf16[64]{0:T(256)(128)(2,1)}, u32[]{:S(2)}) copy-start(bf16[64]{0:T(256)(128)(2,1)} %param.31) | copy-start | bytes 388

commit v2 on v1

v2 whole, which is shorter than its diff:
```python
import functools
import math

import jax
import jax.numpy as jnp
from jax import lax
from jax.experimental import pallas as pl
from jax.experimental.pallas import tpu as pltpu
from jax.sharding import PartitionSpec as P

ln_epsilon = 1e-05
masked_fill = -1000000000.0
masked_below = -100000000.0
root_shift = 0.01
lanes = 128
f32 = jnp.float32
bf16 = jnp.bfloat16
nt = (((1,), (1,)), ((), ()))
tn = (((0,), (0,)), ((), ()))


def split3(x):
    hi = x.astype(bf16).astype(f32)
    mid = (x - hi).astype(bf16).astype(f32)
    return hi, mid, x - hi - mid


def iota(shape, axis):
    return lax.broadcasted_iota(jnp.int32, shape, axis)


def column(row):
    n = row.shape[1]
    square = jnp.where(iota((n, n), 0) == iota((n, n), 1), jnp.broadcast_to(row, (n, n)), 0.0)
    return jnp.sum(square, axis=1, keepdims=True)


def gelu(x):
    inner = x * (0.7978845608028654 + 0.035677408136300125 * (x * x))
    return (0.5 * x) * (1.0 + jnp.tanh(inner))


def node_rows(width, own):
    return width // lanes * own + own


def payload_rows(dims):
    own, cols, width, heads, keys, kinds = dims
    pairs = own * keys
    used = pairs * heads // lanes + node_rows(width, own) + pairs // lanes
    return -(-used // 16) * 16


def in_hbm(x):
    return pltpu.with_memory_space_constraint(x, pltpu.HBM)


def fetch(sources, targets, semaphores):
    copies = [
        pltpu.make_async_copy(source, target, semaphores.at[n])
        for n, (source, target) in enumerate(zip(sources, targets, strict=True))
    ]
    for copy in copies:
        copy.start()
    return copies


def pack_kernel(dims, *refs):
    own, cols, width, heads, keys, kinds = dims
    sources, outs, held = refs[:6], refs[6 : 6 + cols], refs[6 + cols : 12 + cols]
    masks, semaphores = refs[12 + cols :]
    copies = fetch(sources, held, semaphores)
    nodes, coords, types, segments, mask, bias = held
    me = lax.axis_index("col")
    pairs, fold = own * keys, lanes // heads
    bias_rows = pairs // fold
    for copy in copies[:4]:
        copy.wait()
    lane = iota((own, lanes), 1)
    table = jnp.zeros((own, lanes), f32)
    for c in range(3):
        for n, part in enumerate(split3(column(coords[c : c + 1, :]))):
            table = jnp.where(lane == 3 * n + c, part, table)
    kind = (types[...] + kinds // 2 * segments[...]).astype(f32)
    table = jnp.where(lane == 9, column(kind), table)
    full = nodes[...].astype(f32)
    blocks = [full[:, b * lanes : (b + 1) * lanes] for b in range(width // lanes)] + [table]
    copies[4].wait()
    wide_mask = mask[...].astype(f32)
    for d in range(cols):
        row = jnp.concatenate([wide_mask[d * own + i : d * own + i + 1] for i in range(own)], axis=1)
        for n in range(pairs // lanes):
            masks[d, n : n + 1, :] = row[:, n * lanes : (n + 1) * lanes]
    rest = payload_rows(dims) - bias_rows - node_rows(width, own) - pairs // lanes
    if rest:
        filler = [jnp.zeros((rest, lanes), f32)]
    else:
        filler = []
    copies[5].wait()
    for k in range(cols):
        target = me ^ k
        tail = jnp.concatenate(blocks + [masks[target]] + filler, axis=0)
        outs[k][bias_rows:, :] = tail.astype(bf16)
        tile = bias[pl.ds(target * own, own)].astype(f32).reshape(pairs, heads)
        wide = [tile[n * bias_rows : (n + 1) * bias_rows] for n in range(fold)]
        outs[k][:bias_rows, :] = jnp.concatenate(wide, axis=1).astype(bf16)


def gather_kernel(dims, *refs):
    own, cols, width, heads, keys, kinds = dims
    start = own * keys * heads // lanes
    out = refs[cols]
    blocks = [ref[start:, :].astype(f32) for ref in refs[:cols]]
    for b in range(width // lanes + 1):
        rows = jnp.concatenate([block[b * own : (b + 1) * own] for block in blocks], axis=0)
        out[:, b * lanes : (b + 1) * lanes] = rows.astype(bf16)


def arrange_kernel(dims, steps, *refs):
    own, cols, width, heads, keys, kinds = dims
    out = refs[cols]
    atoms = out.shape[1]
    pairs, fold = own * keys, lanes // heads
    bias_rows, each = pairs // fold, own // fold
    mask_at = bias_rows + node_rows(width, own)
    per_row = own * cols
    r, c = lax.axis_index("row"), lax.axis_index("col")
    blocks = [
        jnp.concatenate([ref[b * keys : (b + 1) * keys, :] for ref in refs[:cols]], axis=0)
        for b in range(each)
    ]
    mask_rows = []
    for i in range(own):
        parts = []
        for ref in refs[:cols]:
            tail = ref[bias_rows:, :].astype(f32)
            first = mask_at - bias_rows + i * keys // lanes
            parts.append(tail[first : first + 1, i * keys % lanes : i * keys % lanes + keys])
        mask_rows.append(jnp.concatenate(parts, axis=1))
    mask_rows = jnp.concatenate(mask_rows + [jnp.zeros((16 - own, atoms), f32)], axis=0).astype(bf16)
    place = iota((atoms, 1), 0)
    atom = (c ^ (place // keys)) * keys + place % keys
    for s in range(0, atoms, lanes):
        slot = s + iota((1, lanes), 1)
        bits = slot // per_row
        row = r
        for n, step in enumerate(steps):
            row = row ^ (((bits >> n) & 1) * step)
        source = (row * cols + (c ^ (slot % per_row // own))) * own + slot % own
        chosen = (atom == source).astype(f32).astype(bf16)
        valid = jnp.dot(mask_rows, chosen, preferred_element_type=f32)
        for b in range(each):
            moved = lax.dot_general(blocks[b], chosen, tn, preferred_element_type=f32)
            for a in range(fold):
                i = a * each + b
                kept = jnp.where(valid[i : i + 1] > 0.5, moved[a * heads : (a + 1) * heads], masked_fill)
                out[i * heads : (i + 1) * heads, s : s + lanes] = kept.astype(bf16)


def normed(x, gain):
    features = x.astype(f32)
    centred = features - jnp.mean(features, axis=1, keepdims=True)
    spread = jnp.mean(centred * centred, axis=1, keepdims=True)
    return (centred * lax.rsqrt(spread + ln_epsilon) * gain).astype(bf16)


def prepare_kernel(dims, near, *refs):
    own, cols, width, heads, keys, kinds = dims
    sources = refs[:11]
    w_qkv, w_heads, ln_gain, w_coord2, coords = refs[11:16]
    w_gauss, w_coord1, spread_queries, lookup, own_columns, kernels = refs[16:22]
    mul_held, add_held, mean_held, width_held, gauss_held, coord1_held, semaphores = refs[22:]
    copies = fetch(
        sources,
        (w_qkv, w_heads, ln_gain, w_coord2, coords)
        + (mul_held, add_held, mean_held, width_held, gauss_held, coord1_held),
        semaphores,
    )
    x = near[:16, :]
    own_table = x[:, width:].astype(f32)
    for c in range(3):
        parts = (own_table[:, c : c + 1] + own_table[:, 3 + c : 4 + c]) + own_table[:, 6 + c : 7 + c]
        own_columns[c * 8 : c * 8 + 8, :] = jnp.broadcast_to(parts[:8], (8, lanes))
    own_kind = own_table[:, 9:10].astype(jnp.int32)
    query_onehot = (own_kind == iota((16, kinds), 1)).astype(f32).astype(bf16)
    for copy in copies[5:]:
        copy.wait()
    inverse = 1.0 / column(width_held[...])
    gauss = inverse.shape[0]
    kernels[0] = jnp.broadcast_to(column(mean_held[...]), (gauss, lanes))
    kernels[1] = jnp.broadcast_to(inverse * math.sqrt(0.5 * math.log2(math.e)), (gauss, lanes))
    kernels[2] = jnp.broadcast_to(jnp.log2(inverse * (1.0 / math.sqrt(2.0 * math.pi))), (gauss, lanes))
    at = 0
    for table in (mul_held, add_held):
        for part in split3(table[...]):
            found = jnp.dot(query_onehot, part.astype(bf16), preferred_element_type=f32)
            lookup[at : at + 16, :] = found.astype(bf16)
            at += 16
    w_gauss[...] = gauss_held[...].astype(f32).T.astype(bf16)
    w_coord1[...] = coord1_held[...].astype(f32).T.astype(bf16)
    for copy in copies[:5]:
        copy.wait()
    queries = jnp.dot(
        normed(x[:, :width], ln_gain[...]), w_qkv[:, :width], preferred_element_type=f32
    )
    head_mask = iota((heads, width), 1) // (width // heads) == iota((heads, width), 0)
    for i in range(own):
        spread = jnp.where(head_mask, jnp.broadcast_to(queries[i : i + 1], (heads, width)), 0.0)
        spread_queries[i * heads : (i + 1) * heads, :] = spread.astype(bf16)


def attend_kernel(
    dims,
    near,
    far,
    bias,
    w_qkv,
    w_heads,
    ln_gain,
    w_coord2,
    coords,
    w_gauss,
    w_coord1,
    spread_queries,
    lookup,
    own_columns,
    kernels,
    attended,
    moved,
    logits,
    values,
    places,
    strengths,
):
    own, cols, width, heads, keys, kinds = dims
    atoms = bias.shape[1]
    head_dim = width // heads
    half = near.shape[0]
    gain = ln_gain[...]
    select_at, select_from = iota((16, lanes), 0), iota((16, lanes), 1)
    selector = (
        ((select_from < 9) & (select_from % 3 == select_at) & (select_at < 3))
        | ((select_from == 9) & (select_at == 3))
    ).astype(f32).astype(bf16)
    centre, sharp, norming = kernels[0], kernels[1], kernels[2]

    for s in range(0, atoms, lanes):
        if half < lanes:
            x = jnp.concatenate([near[...], far[...]], axis=0)
        elif s < half:
            x = near[s : s + lanes, :]
        else:
            x = far[s - half : s - half + lanes, :]
        table = lax.dot_general(selector, x[:, width:], nt, preferred_element_type=f32)
        places[:, s : s + lanes] = jnp.where(iota((16, lanes), 0) == 3, 1.0, table)
        offsets = [own_columns[c * 8 : c * 8 + own, :] - table[c : c + 1] for c in range(3)]
        squares = offsets[0] * offsets[0] + offsets[1] * offsets[1] + offsets[2] * offsets[2]
        distance = jnp.sqrt(squares + root_shift)
        key_onehot = (table[3:4].astype(jnp.int32) == iota((kinds, lanes), 0)).astype(f32).astype(bf16)
        found = jnp.dot(lookup[...], key_onehot, preferred_element_type=f32)
        scale = found[0:16] + found[16:32] + found[32:48]
        shift = found[48:64] + found[64:80] + found[80:96]
        expanded = scale[:own] * distance + shift[:own]
        features = []
        for i in range(own):
            scaled = (expanded[i : i + 1] - centre) * sharp
            features.append(jnp.exp2(norming - scaled * scaled).astype(bf16))
        hidden = jnp.dot(w_gauss[...], jnp.concatenate(features, axis=1), preferred_element_type=f32)
        geometry = jnp.dot(w_heads[...], gelu(hidden).astype(bf16), preferred_element_type=f32)
        block = normed(x[:, :width], gain)
        both = jnp.dot(block, w_qkv[:, width:], preferred_element_type=f32).astype(bf16)
        values[s : s + lanes, :] = both[:, width:]
        affinity = lax.dot_general(
            spread_queries[...], both[:, :width], nt, preferred_element_type=f32
        )
        here = bias[:, s : s + lanes].astype(f32)
        rows = []
        for i in range(own):
            at = slice(i * heads, (i + 1) * heads)
            row = here[at] + geometry[:, i * lanes : (i + 1) * lanes]
            row = row + affinity[at] * (1.0 / math.sqrt(head_dim))
            logits[at, s : s + lanes] = jnp.where(here[at] < masked_below, masked_fill, row)
            rows.append(row.astype(bf16))
        mixed = jnp.dot(w_coord1[...], jnp.concatenate(rows, axis=1), preferred_element_type=f32)
        strength = jnp.dot(w_coord2[...], gelu(mixed).astype(bf16), preferred_element_type=f32)
        strengths[:, s : s + lanes] = jnp.concatenate(
            [
                jnp.where(
                    here[i * heads : i * heads + 1] < masked_below,
                    0.0,
                    strength[:, i * lanes : (i + 1) * lanes],
                )
                for i in range(own)
            ],
            axis=0,
        )

    masked = logits[...]
    weights = jnp.exp(masked - jnp.max(masked, axis=1, keepdims=True))
    share = 1.0 / jnp.sum(weights, axis=1, keepdims=True)
    taken = jnp.dot(weights.astype(bf16), values[...], preferred_element_type=f32) * share
    head_mask = iota((heads, width), 1) // head_dim == iota((heads, width), 0)
    attended[...] = jnp.concatenate(
        [
            jnp.sum(
                jnp.where(head_mask, taken[i * heads : (i + 1) * heads], 0.0), axis=0, keepdims=True
            )
            for i in range(own)
        ],
        axis=0,
    ).astype(bf16)
    pulled = lax.dot_general(
        places[...],
        strengths[...],
        nt,
        precision=lax.Precision.HIGHEST,
        preferred_element_type=f32,
    )
    here = coords[...]
    moved[...] = here + (here * pulled[3:4] - pulled[0:3]) * (1.0 / atoms)


def shards(
    nodes,
    coords,
    atom_types,
    segment_ids,
    pair_mask,
    pair_bias,
    ln_gain,
    w_qkv,
    gauss_mul,
    gauss_add,
    gauss_mean,
    gauss_width,
    w_gauss,
    w_heads,
    w_coord1,
    w_coord2,
):
    cols, rows = lax.axis_size("col"), lax.axis_size("row")
    own, width = nodes.shape
    heads, queries, keys = pair_bias.shape
    kinds, gauss = gauss_mul.shape[0], gauss_mean.shape[0]
    atoms = own * rows * cols
    dims = (own, cols, width, heads, keys, kinds)
    shape = jax.ShapeDtypeStruct
    params = pltpu.CompilerParams(vmem_limit_bytes=(16 if atoms <= 128 else 56) * 2**20)
    vmem, anywhere = pl.BlockSpec(memory_space=pltpu.VMEM), pl.BlockSpec(memory_space=pl.ANY)
    sources = (
        nodes,
        coords,
        atom_types[None, :],
        segment_ids[None, :],
        pair_mask,
        pair_bias.transpose(1, 2, 0),
    )
    packed = pl.pallas_call(
        functools.partial(pack_kernel, dims),
        out_shape=[shape((payload_rows(dims), lanes), bf16)] * cols,
        in_specs=[anywhere] * 6,
        out_specs=[vmem] * cols,
        scratch_shapes=[pltpu.VMEM(x.shape, x.dtype) for x in sources]
        + [pltpu.VMEM((cols, own * keys // lanes, lanes), f32), pltpu.SemaphoreType.DMA((6,))],
        compiler_params=params,
        name="pack",
    )(*map(in_hbm, sources))
    arrived = [packed[0]] + [
        lax.ppermute(packed[k], "col", [(i, i ^ k) for i in range(cols)]) for k in range(1, cols)
    ]
    near = pl.pallas_call(
        functools.partial(gather_kernel, dims),
        out_shape=shape((own * cols, width + lanes), bf16),
        in_specs=[vmem] * cols,
        out_specs=vmem,
        compiler_params=params,
        name="gather",
    )(*arrived)
    steps = [2**n for n in range(1, rows.bit_length() - 1)] + [1]
    bias = pl.pallas_call(
        functools.partial(arrange_kernel, dims, steps),
        out_shape=shape((own * heads, atoms), bf16),
        in_specs=[vmem] * cols,
        out_specs=vmem,
        compiler_params=params,
        name="arrange",
    )(*arrived)
    weights = (w_qkv, w_heads.T, ln_gain[None, :], w_coord2[None, :], coords)
    tables = (gauss_mul, gauss_add, gauss_mean[None, :], gauss_width[None, :], w_gauss, w_coord1)
    prepared = pl.pallas_call(
        functools.partial(prepare_kernel, dims),
        out_shape=[shape(x.shape, x.dtype) for x in weights]
        + [
            shape((gauss, gauss), bf16),
            shape(w_coord1.shape, bf16),
            shape((own * heads, width), bf16),
            shape((96, kinds), bf16),
            shape((24, lanes), f32),
            shape((3, gauss, lanes), f32),
        ],
        in_specs=[vmem] + [anywhere] * 11,
        out_specs=[vmem] * 11,
        scratch_shapes=[pltpu.VMEM(x.shape, x.dtype) for x in tables]
        + [pltpu.SemaphoreType.DMA((11,))],
        compiler_params=params,
        name="prepare",
    )(near, *map(in_hbm, weights + tables))
    for n, step in enumerate(steps):
        far = lax.ppermute(near, "row", [(i, i ^ step) for i in range(rows)])
        if n < len(steps) - 1:
            near = jnp.concatenate([near, far], axis=0)
    attended, moved = pl.pallas_call(
        functools.partial(attend_kernel, dims),
        out_shape=[shape((own, width), bf16), shape((3, own), f32)],
        in_specs=[vmem] * 14,
        out_specs=[vmem] * 2,
        scratch_shapes=[
            pltpu.VMEM((own * heads, atoms), f32),
            pltpu.VMEM((atoms, width), bf16),
            pltpu.VMEM((16, atoms), f32),
            pltpu.VMEM((own, atoms), f32),
        ],
        compiler_params=params,
        name="attend",
    )(near, far, bias, *prepared)
    return attended, moved


def solution(mesh):
    own, tile, whole = P(("row", "col")), P("row", "col"), P()
    in_specs = (
        P(("row", "col"), None),
        P(None, ("row", "col")),
        own,
        own,
        tile,
        P(None, "row", "col"),
    ) + (whole,) * 10
    out_specs = (P(("row", "col"), None), P(None, ("row", "col")))
    return jax.shard_map(shards, mesh=mesh, in_specs=in_specs, out_specs=out_specs, check_vma=False)
```

time: 37.7 us -> 25.4 us (0.67); the launches traced: 37.1 us -> 25.2 us
  local copies, waits for them, and re-layouts: 13.1 us -> 0 us
  Pallas kernels: 3.38 us -> 5.31 us
  waiting for transfers between devices: 11.1 us -> 10.4 us
    unnamed x32 -> x0, local copies, waits for them, and re-layouts: 13.1 us -> none
    pallas_call x4 -> x5, Pallas kernels: 3.38 us -> 5.31 us  [the longest x1 1.98 us: shards(): pl.pallas_call(functools.partial(attend_kernel, dims), out_shape=[shape((...]
    ppermute x3, waiting for transfers between devices: 5.47 us -> 4.78 us  [shards(): far = lax.ppermute(near, 'row', [(i, i ^ step) for i in range(rows)])]
  transfers between devices with their start and end apart: 6 -> 6, of which waited for: 5 -> 4; matrix products, arithmetic and copies ran while one was open for 2% -> 0% of each run, Pallas kernels for 1% -> 9%
where the time goes in v2:
time: 25.4 us; the launch traced here: 25.2 us
  waiting for transfers between devices  10.4 us (41%)
  starting transfers between devices  8.83 us (35%)
  Pallas kernels  5.31 us (21%)
  between operations  0.67 us (3%)
    ppermute x3, starting transfers between devices, shards(): lax.ppermute(packed[k], 'col', [(i, i ^ k) for i in range(cols)])  5.68 us
    ppermute x3, waiting for transfers between devices, shards(): lax.ppermute(packed[k], 'col', [(i, i ^ k) for i in range(cols)])  5.62 us
    ppermute x3, waiting for transfers between devices, shards(): far = lax.ppermute(near, 'row', [(i, i ^ step) for i in range(rows)])  4.78 us
    ppermute x3, starting transfers between devices, shards(): far = lax.ppermute(near, 'row', [(i, i ^ step) for i in range(rows)])  3.15 us
    pallas_call x1, Pallas kernels, shards(): pl.pallas_call(functools.partial(attend_kernel, dims), out_shape=[shape((...  1.98 us
    pallas_call x1, Pallas kernels, shards(): pl.pallas_call(functools.partial(prepare_kernel, dims), out_shape=[shape(...  1.97 us
    pallas_call x1, Pallas kernels, shards(): pl.pallas_call(functools.partial(pack_kernel, dims), out_shape=[shape((pa...  1.13 us
  transfers between devices with their start and end apart: 6, of which 4 were waited for; matrix products, arithmetic and copies ran while one was open for 0% of the time, Pallas kernels for 9%

profile of v2, /device:TPU:0, one launch (start us, length us, event | category | flops | bytes accessed | tf_op | source)
XLA Modules:
  0.0 25.2 jit_solution(16907250251325102591)
XLA Ops:
  0.6 1.1 %pack.1 = (bf16[96,128]{1,0:T(8,128)(2,1)S(1)}, bf16[96,128]{1,0:T(8,128)(2,1)S(1)}, bf16[96,128]{1,0:T(8,128)(2,1)S(1)}, bf16[96,128]{1,0:T(8,128)(2,1)S(1)}) custom-call(bf16[4,512]{1,0:T(4,128)(2,1)} %refs_0_.2, f32[3,4]{1,0:T(4,128)} %refs_4_.3, s32[1,4]{1,0:T(1,128)} %bitcast.11, s32[1,4]{1,0:T(1,128)} %bitcast.12, s32[16,32]{1,0:T(8,128)} %refs_4_.2, ...), custom_call_target="tpu_custom_call" | custom-call | tf_op jit(solution)/shard_map/pack/pallas_call | solution.py:358
  1.8 3.1 %collective-permute-start = (bf16[96,128]{1,0:T(8,128)(2,1)S(1)}, bf16[96,128]{1,0:T(8,128)(2,1)S(1)}, u32[]{:S(2)}, u32[]{:S(2)}) collective-permute-start(bf16[96,128]{1,0:T(8,128)(2,1)S(1)} %get-tuple-element.18), channel_id=1, source_target_pairs={{0,1},{1,0},{2,3},{3,2},{4,5},{5,4},{6,7},{7,6},{8,9},{9,8},{10,11... | collective-permute-start | bytes 73736 | tf_op jit(solution)/shard_map/ppermute | solution.py:369
  4.9 2.6 %collective-permute-start.1 = (bf16[96,128]{1,0:T(8,128)(2,1)S(1)}, bf16[96,128]{1,0:T(8,128)(2,1)S(1)}, u32[]{:S(2)}, u32[]{:S(2)}) collective-permute-start(bf16[96,128]{1,0:T(8,128)(2,1)S(1)} %get-tuple-element.19), channel_id=1, source_target_pairs={{0,2},{1,3},{2,0},{3,1},{4,6},{5,7},{6,4},{7,5},{8,10},{9,11},{10,... | collective-permute-start | bytes 73736 | tf_op jit(solution)/shard_map/ppermute | solution.py:369
  7.4 0.0 collective-permute-start.2
  7.4 0.0 collective-permute-done.refs_1_
  7.5 2.5 %collective-permute-done.1.refs_2_ = bf16[96,128]{1,0:T(8,128)(2,1)S(1)} collective-permute-done((bf16[96,128]{1,0:T(8,128)(2,1)S(1)}, bf16[96,128]{1,0:T(8,128)(2,1)S(1)}, u32[]{:S(2)}, u32[]{:S(2)}) %collective-permute-start.1) | collective-permute-done | bytes 24608 | tf_op jit(solution)/shard_map/ppermute | solution.py:369
  9.9 3.1 %collective-permute-done.2.refs_3_ = bf16[96,128]{1,0:T(8,128)(2,1)S(1)} collective-permute-done((bf16[96,128]{1,0:T(8,128)(2,1)S(1)}, bf16[96,128]{1,0:T(8,128)(2,1)S(1)}, u32[]{:S(2)}, u32[]{:S(2)}) %collective-permute-start.2) | collective-permute-done | bytes 24608 | tf_op jit(solution)/shard_map/ppermute | solution.py:369
  13.1 1.6 %collective-permute-start.3 = (bf16[16,640]{1,0:T(8,128)(2,1)S(1)}, bf16[16,640]{1,0:T(8,128)(2,1)S(1)}, u32[]{:S(2)}, u32[]{:S(2)}) collective-permute-start(bf16[16,640]{1,0:T(8,128)(2,1)S(1)} %gather.1.near), channel_id=1, source_target_pairs={{0,8},{4,12},{8,0},{12,4},{16,24},{20,28},{24,16},{28,20},{1,9},{5... | collective-permute-start | bytes 61448 | tf_op jit(solution)/shard_map/ppermute | solution.py:409
  14.6 2.3 %collective-permute-done.3 = bf16[16,640]{1,0:T(8,128)(2,1)S(1)} collective-permute-done((bf16[16,640]{1,0:T(8,128)(2,1)S(1)}, bf16[16,640]{1,0:T(8,128)(2,1)S(1)}, u32[]{:S(2)}, u32[]{:S(2)}) %collective-permute-start.3) | collective-permute-done | bytes 20512 | tf_op jit(solution)/shard_map/ppermute | solution.py:409
  16.9 1.5 %collective-permute-start.4 = (bf16[32,640]{1,0:T(8,128)(2,1)S(1)}, bf16[32,640]{1,0:T(8,128)(2,1)S(1)}, u32[]{:S(2)}, u32[]{:S(2)}) collective-permute-start(bf16[32,640]{1,0:T(8,128)(2,1)S(1)} %pad_maximum_fusion.1), channel_id=1, source_target_pairs={{0,16},{4,20},{8,24},{12,28},{16,0},{20,4},{24,8},{28,12},{1,17},{... | collective-permute-start | bytes 122888 | tf_op jit(solution)/shard_map/ppermute | solution.py:409
  18.5 2.5 %collective-permute-done.4 = bf16[32,640]{1,0:T(8,128)(2,1)S(1)} collective-permute-done((bf16[32,640]{1,0:T(8,128)(2,1)S(1)}, bf16[32,640]{1,0:T(8,128)(2,1)S(1)}, u32[]{:S(2)}, u32[]{:S(2)}) %collective-permute-start.4) | collective-permute-done | bytes 40992 | tf_op jit(solution)/shard_map/ppermute | solution.py:409
  21.0 0.1 collective-permute-start.5
  21.0 2.0 %prepare.1 = (bf16[512,1536]{1,0:T(8,128)(2,1)S(1)}, bf16[64,128]{1,0:T(8,128)(2,1)S(1)}, f32[1,512]{1,0:T(1,128)S(1)}, bf16[1,64]{1,0:T(2,128)(2,1)S(1)}, f32[3...) custom-call(bf16[16,640]{1,0:T(8,128)(2,1)S(1)} %gather.1.near, ...), custom_call_target="tpu_custom_call" | custom-call | tf_op jit(solution)/shard_map/prepare/pallas_call | solution.py:390
  23.0 0.2 arrange.1.bias
  23.2 0.0 collective-permute-done.5.far
  23.2 2.0 %attend.1 = (bf16[4,512]{1,0:T(4,128)(2,1)}, f32[3,4]{1,0:T(4,128)}) custom-call(bf16[64,640]{1,0:T(8,128)(2,1)S(1)} %pad_maximum_fusion.near, bf16[64,640]{1,0:T(8,128)(2,1)S(1)} %collective-permute-done.5.far, bf16[256,128]{1,0:T(8,128)(2,1)S(1)} %arrange.1.bias, bf16[512,1536]{1,0:T(8,128)(2,1)S(1)} %get-tuple-element.21.w_qkv, ...), custom_call_target="tpu_custom_call" | custom-call | tf_op jit(solution)/shard_map/attend/pallas_call | solution.py:412
  (3 shorter events, 0.0 us)
Async XLA Ops:
  1.8 5.7 %collective-permute-start = (bf16[96,128]{1,0:T(8,128)(2,1)S(1)}, bf16[96,128]{1,0:T(8,128)(2,1)S(1)}, u32[]{:S(2)}, u32[]{:S(2)}) collective-permute-start(bf16[96,128]{1,0:T(8,128)(2,1)S(1)} %get-tuple-element.18), channel_id=1, source_target_pairs={{0,1},{1,0},{2,3},{3,2},{4,5},{5,4},{6,7},{7,6},{8,9},{9,8},{10,11... | collective-permute-start | bytes 73736 | tf_op jit(solution)/shard_map/ppermute | solution.py:369
  4.9 5.1 %collective-permute-start.1 = (bf16[96,128]{1,0:T(8,128)(2,1)S(1)}, bf16[96,128]{1,0:T(8,128)(2,1)S(1)}, u32[]{:S(2)}, u32[]{:S(2)}) collective-permute-start(bf16[96,128]{1,0:T(8,128)(2,1)S(1)} %get-tuple-element.19), channel_id=1, source_target_pairs={{0,2},{1,3},{2,0},{3,1},{4,6},{5,7},{6,4},{7,5},{8,10},{9,11},{10,... | collective-permute-start | bytes 73736 | tf_op jit(solution)/shard_map/ppermute | solution.py:369
  7.4 5.6 %collective-permute-start.2 = (bf16[96,128]{1,0:T(8,128)(2,1)S(1)}, bf16[96,128]{1,0:T(8,128)(2,1)S(1)}, u32[]{:S(2)}, u32[]{:S(2)}) collective-permute-start(bf16[96,128]{1,0:T(8,128)(2,1)S(1)} %get-tuple-element.20), channel_id=1, source_target_pairs={{0,3},{1,2},{2,1},{3,0},{4,7},{5,6},{6,5},{7,4},{8,11},{9,10},{10,... | collective-permute-start | bytes 73736 | tf_op jit(solution)/shard_map/ppermute | solution.py:369
  13.1 3.8 %collective-permute-start.3 = (bf16[16,640]{1,0:T(8,128)(2,1)S(1)}, bf16[16,640]{1,0:T(8,128)(2,1)S(1)}, u32[]{:S(2)}, u32[]{:S(2)}) collective-permute-start(bf16[16,640]{1,0:T(8,128)(2,1)S(1)} %gather.1.near), channel_id=1, source_target_pairs={{0,8},{4,12},{8,0},{12,4},{16,24},{20,28},{24,16},{28,20},{1,9},{5... | collective-permute-start | bytes 61448 | tf_op jit(solution)/shard_map/ppermute | solution.py:409
  16.9 4.0 %collective-permute-start.4 = (bf16[32,640]{1,0:T(8,128)(2,1)S(1)}, bf16[32,640]{1,0:T(8,128)(2,1)S(1)}, u32[]{:S(2)}, u32[]{:S(2)}) collective-permute-start(bf16[32,640]{1,0:T(8,128)(2,1)S(1)} %pad_maximum_fusion.1), channel_id=1, source_target_pairs={{0,16},{4,20},{8,24},{12,28},{16,0},{20,4},{24,8},{28,12},{1,17},{... | collective-permute-start | bytes 122888 | tf_op jit(solution)/shard_map/ppermute | solution.py:409
  21.0 2.3 %collective-permute-start.5 = (bf16[64,640]{1,0:T(8,128)(2,1)S(1)}, bf16[64,640]{1,0:T(8,128)(2,1)S(1)}, u32[]{:S(2)}, u32[]{:S(2)}) collective-permute-start(bf16[64,640]{1,0:T(8,128)(2,1)S(1)} %pad_maximum_fusion.near), channel_id=1, source_target_pairs={{0,4},{4,0},{8,12},{12,8},{16,20},{20,16},{24,28},{28,24},{1,5},{5... | collective-permute-start | bytes 245768 | tf_op jit(solution)/shard_map/ppermute | solution.py:409

commit v3 on v2

--- a/solution.py
+++ b/solution.py
@@ -41,14 +41,15 @@
 
 
 def node_rows(width, own):
-    return width // lanes * own + own
-
-
-def payload_rows(dims):
-    own, cols, width, heads, keys, kinds = dims
-    pairs = own * keys
-    used = pairs * heads // lanes + node_rows(width, own) + pairs // lanes
-    return -(-used // 16) * 16
+    return (width // lanes + 1) * own
+
+
+def sizes(dims):
+    own, cols, width, heads, keys, kinds = dims
+    bias_rows, mask_rows = own * keys * heads // lanes, own * keys // lanes
+    first = node_rows(width, own) + (cols - 1) * (bias_rows + mask_rows)
+    second = bias_rows + 2 * node_rows(width, own) + mask_rows
+    return bias_rows, mask_rows, -(-first // 16) * 16, -(-second // 16) * 16
 
 
 def in_hbm(x):
@@ -65,15 +66,19 @@
     return copies
 
 
+def filled(blocks, rows):
+    rest = rows - sum(block.shape[0] for block in blocks)
+    return jnp.concatenate(blocks + ([jnp.zeros((rest, lanes), f32)] if rest else []), axis=0)
+
+
 def pack_kernel(dims, *refs):
     own, cols, width, heads, keys, kinds = dims
-    sources, outs, held = refs[:6], refs[6 : 6 + cols], refs[6 + cols : 12 + cols]
-    masks, semaphores = refs[12 + cols :]
+    bias_rows, mask_rows, first_rows, second_rows = sizes(dims)
+    sources, first, kept, held, masks, semaphores = refs[:6], refs[6], refs[7], refs[8:14], refs[14], refs[15]
     copies = fetch(sources, held, semaphores)
     nodes, coords, types, segments, mask, bias = held
     me = lax.axis_index("col")
     pairs, fold = own * keys, lanes // heads
-    bias_rows = pairs // fold
     for copy in copies[:4]:
         copy.wait()
     lane = iota((own, lanes), 1)
@@ -89,72 +94,92 @@
     wide_mask = mask[...].astype(f32)
     for d in range(cols):
         row = jnp.concatenate([wide_mask[d * own + i : d * own + i + 1] for i in range(own)], axis=1)
-        for n in range(pairs // lanes):
+        for n in range(mask_rows):
             masks[d, n : n + 1, :] = row[:, n * lanes : (n + 1) * lanes]
-    rest = payload_rows(dims) - bias_rows - node_rows(width, own) - pairs // lanes
-    if rest:
-        filler = [jnp.zeros((rest, lanes), f32)]
-    else:
-        filler = []
+    start = (cols - 1) * bias_rows
+    tail = filled(blocks + [masks[me ^ k] for k in range(1, cols)], first_rows - start)
+    first[start:, :] = tail.astype(bf16)
+    kept[bias_rows:, :] = filled([masks[me]], kept.shape[0] - bias_rows).astype(bf16)
     copies[5].wait()
     for k in range(cols):
-        target = me ^ k
-        tail = jnp.concatenate(blocks + [masks[target]] + filler, axis=0)
-        outs[k][bias_rows:, :] = tail.astype(bf16)
-        tile = bias[pl.ds(target * own, own)].astype(f32).reshape(pairs, heads)
+        tile = bias[pl.ds((me ^ k) * own, own)].astype(f32).reshape(pairs, heads)
         wide = [tile[n * bias_rows : (n + 1) * bias_rows] for n in range(fold)]
-        outs[k][:bias_rows, :] = jnp.concatenate(wide, axis=1).astype(bf16)
-
-
-def gather_kernel(dims, *refs):
-    own, cols, width, heads, keys, kinds = dims
-    start = own * keys * heads // lanes
-    out = refs[cols]
-    blocks = [ref[start:, :].astype(f32) for ref in refs[:cols]]
+        block = jnp.concatenate(wide, axis=1).astype(bf16)
+        if k:
+            first[(k - 1) * bias_rows : k * bias_rows, :] = block
+        else:
+            kept[:bias_rows, :] = block
+
+
+def regroup_kernel(dims, order, mine, other, *outs):
+    own, cols, width, heads, keys, kinds = dims
+    bias_rows, mask_rows, first_rows, second_rows = sizes(dims)
+    start, rows = (cols - 1) * bias_rows, node_rows(width, own)
+    here, there = mine[start:, :].astype(f32), other[start:, :].astype(f32)
+    for n, k in enumerate(order):
+        outs[n][:bias_rows, :] = other[(k - 1) * bias_rows : k * bias_rows, :]
+        at = rows + (k - 1) * mask_rows
+        tail = filled([here[:rows], there[:rows], there[at : at + mask_rows]], second_rows - bias_rows)
+        outs[n][bias_rows:, :] = tail.astype(bf16)
+
+
+def gather_kernel(dims, order, mine, other, *refs):
+    own, cols, width, heads, keys, kinds = dims
+    bias_rows, mask_rows, first_rows, second_rows = sizes(dims)
+    start, rows = (cols - 1) * bias_rows, node_rows(width, own)
+    out = refs[cols - 1]
+    blocks = [mine[start:, :].astype(f32)[:rows], other[start:, :].astype(f32)[:rows]]
+    for k in range(1, cols):
+        tail = refs[order.index(k)][bias_rows:, :].astype(f32)
+        blocks += [tail[rows : 2 * rows], tail[:rows]]
     for b in range(width // lanes + 1):
-        rows = jnp.concatenate([block[b * own : (b + 1) * own] for block in blocks], axis=0)
-        out[:, b * lanes : (b + 1) * lanes] = rows.astype(bf16)
-
-
-def arrange_kernel(dims, steps, *refs):
-    own, cols, width, heads, keys, kinds = dims
-    out = refs[cols]
+        taken = jnp.concatenate([block[b * own : (b + 1) * own] for block in blocks], axis=0)
+        out[:, b * lanes : (b + 1) * lanes] = taken.astype(bf16)
+
+
+def arrange_kernel(dims, order, steps, kept, *refs):
+    own, cols, width, heads, keys, kinds = dims
+    bias_rows, mask_rows, first_rows, second_rows = sizes(dims)
+    received = [refs[order.index(k)] for k in range(1, cols)]
+    spread_queries, w_qkv, out, keyed = refs[cols - 1 :]
+    keyed[...] = lax.dot_general(
+        spread_queries[...], w_qkv[:, width : 2 * width], nt, preferred_element_type=f32
+    ).astype(bf16)
     atoms = out.shape[1]
-    pairs, fold = own * keys, lanes // heads
-    bias_rows, each = pairs // fold, own // fold
-    mask_at = bias_rows + node_rows(width, own)
-    per_row = own * cols
+    fold = lanes // heads
+    each = own // fold
+    mask_at = 2 * node_rows(width, own)
+    per_row = 2 * own * cols
     r, c = lax.axis_index("row"), lax.axis_index("col")
     blocks = [
-        jnp.concatenate([ref[b * keys : (b + 1) * keys, :] for ref in refs[:cols]], axis=0)
+        jnp.concatenate([ref[b * keys : (b + 1) * keys, :] for ref in [kept] + received], axis=0)
         for b in range(each)
     ]
-    mask_rows = []
+    tails = [kept[bias_rows:, :].astype(f32)[:mask_rows]]
+    tails += [ref[bias_rows:, :].astype(f32)[mask_at : mask_at + mask_rows] for ref in received]
+    masks = []
     for i in range(own):
-        parts = []
-        for ref in refs[:cols]:
-            tail = ref[bias_rows:, :].astype(f32)
-            first = mask_at - bias_rows + i * keys // lanes
-            parts.append(tail[first : first + 1, i * keys % lanes : i * keys % lanes + keys])
-        mask_rows.append(jnp.concatenate(parts, axis=1))
-    mask_rows = jnp.concatenate(mask_rows + [jnp.zeros((16 - own, atoms), f32)], axis=0).astype(bf16)
+        n, lane = i * keys // lanes, i * keys % lanes
+        masks.append(jnp.concatenate([tail[n : n + 1, lane : lane + keys] for tail in tails], axis=1))
+    masks = jnp.concatenate(masks + [jnp.zeros((16 - own, atoms), f32)], axis=0).astype(bf16)
     place = iota((atoms, 1), 0)
     atom = (c ^ (place // keys)) * keys + place % keys
     for s in range(0, atoms, lanes):
         slot = s + iota((1, lanes), 1)
-        bits = slot // per_row
-        row = r
-        for n, step in enumerate(steps):
-            row = row ^ (((bits >> n) & 1) * step)
-        source = (row * cols + (c ^ (slot % per_row // own))) * own + slot % own
+        piece, inner = slot // per_row, slot % per_row
+        step = jnp.zeros((1, lanes), jnp.int32)
+        for n, value in enumerate(steps):
+            step = jnp.where(piece == n, value, step)
+        row = r ^ step ^ (inner // own % 2)
+        source = (row * cols + (c ^ (inner // (2 * own)))) * own + inner % own
         chosen = (atom == source).astype(f32).astype(bf16)
-        valid = jnp.dot(mask_rows, chosen, preferred_element_type=f32)
+        valid = jnp.dot(masks, chosen, preferred_element_type=f32)
         for b in range(each):
             moved = lax.dot_general(blocks[b], chosen, tn, preferred_element_type=f32)
             for a in range(fold):
                 i = a * each + b
-                kept = jnp.where(valid[i : i + 1] > 0.5, moved[a * heads : (a + 1) * heads], masked_fill)
-                out[i * heads : (i + 1) * heads, s : s + lanes] = kept.astype(bf16)
+                taken = jnp.where(valid[i : i + 1] > 0.5, moved[a * heads : (a + 1) * heads], masked_fill)
+                out[i * heads : (i + 1) * heads, s : s + lanes] = taken.astype(bf16)
 
 
 def normed(x, gain):
@@ -164,8 +189,9 @@
     return (centred * lax.rsqrt(spread + ln_epsilon) * gain).astype(bf16)
 
 
-def prepare_kernel(dims, near, *refs):
-    own, cols, width, heads, keys, kinds = dims
+def prepare_kernel(dims, mine, *refs):
+    own, cols, width, heads, keys, kinds = dims
+    bias_rows, mask_rows, first_rows, second_rows = sizes(dims)
     sources = refs[:11]
     w_qkv, w_heads, ln_gain, w_coord2, coords = refs[11:16]
     w_gauss, w_coord1, spread_queries, lookup, own_columns, kernels = refs[16:22]
@@ -176,8 +202,13 @@
         + (mul_held, add_held, mean_held, width_held, gauss_held, coord1_held),
         semaphores,
     )
-    x = near[:16, :]
-    own_table = x[:, width:].astype(f32)
+    rows = mine[(cols - 1) * bias_rows :, :].astype(f32)[: node_rows(width, own)]
+    filler = jnp.zeros((16 - own, lanes), f32)
+    x = [
+        jnp.concatenate([rows[b * own : (b + 1) * own], filler], axis=0)
+        for b in range(width // lanes + 1)
+    ]
+    own_table = x[width // lanes]
     for c in range(3):
         parts = (own_table[:, c : c + 1] + own_table[:, 3 + c : 4 + c]) + own_table[:, 6 + c : 7 + c]
         own_columns[c * 8 : c * 8 + 8, :] = jnp.broadcast_to(parts[:8], (8, lanes))
@@ -201,7 +232,9 @@
     for copy in copies[:5]:
         copy.wait()
     queries = jnp.dot(
-        normed(x[:, :width], ln_gain[...]), w_qkv[:, :width], preferred_element_type=f32
+        normed(jnp.concatenate(x[:-1], axis=1), ln_gain[...]),
+        w_qkv[:, :width],
+        preferred_element_type=f32,
     )
     head_mask = iota((heads, width), 1) // (width // heads) == iota((heads, width), 0)
     for i in range(own):
@@ -209,33 +242,15 @@
         spread_queries[i * heads : (i + 1) * heads, :] = spread.astype(bf16)
 
 
-def attend_kernel(
-    dims,
-    near,
-    far,
-    bias,
-    w_qkv,
-    w_heads,
-    ln_gain,
-    w_coord2,
-    coords,
-    w_gauss,
-    w_coord1,
-    spread_queries,
-    lookup,
-    own_columns,
-    kernels,
-    attended,
-    moved,
-    logits,
-    values,
-    places,
-    strengths,
-):
-    own, cols, width, heads, keys, kinds = dims
+def attend_kernel(dims, count, *refs):
+    own, cols, width, heads, keys, kinds = dims
+    pieces = refs[:count]
+    bias, keyed, w_qkv, w_heads, ln_gain, w_coord2, coords = refs[count : count + 7]
+    w_gauss, w_coord1, lookup, own_columns, kernels, attended, moved = refs[count + 7 : count + 14]
+    logits, values, places, strengths = refs[count + 14 :]
     atoms = bias.shape[1]
     head_dim = width // heads
-    half = near.shape[0]
+    each = lanes // pieces[0].shape[0]
     gain = ln_gain[...]
     select_at, select_from = iota((16, lanes), 0), iota((16, lanes), 1)
     selector = (
@@ -245,12 +260,12 @@
     centre, sharp, norming = kernels[0], kernels[1], kernels[2]
 
     for s in range(0, atoms, lanes):
-        if half < lanes:
-            x = jnp.concatenate([near[...], far[...]], axis=0)
-        elif s < half:
-            x = near[s : s + lanes, :]
+        if each:
+            first = s // lanes * each
+            x = jnp.concatenate([ref[...] for ref in pieces[first : first + each]], axis=0)
         else:
-            x = far[s - half : s - half + lanes, :]
+            rows = pieces[0].shape[0]
+            x = pieces[s // rows][s % rows : s % rows + lanes, :]
         table = lax.dot_general(selector, x[:, width:], nt, preferred_element_type=f32)
         places[:, s : s + lanes] = jnp.where(iota((16, lanes), 0) == 3, 1.0, table)
         offsets = [own_columns[c * 8 : c * 8 + own, :] - table[c : c + 1] for c in range(3)]
@@ -268,11 +283,10 @@
         hidden = jnp.dot(w_gauss[...], jnp.concatenate(features, axis=1), preferred_element_type=f32)
         geometry = jnp.dot(w_heads[...], gelu(hidden).astype(bf16), preferred_element_type=f32)
         block = normed(x[:, :width], gain)
-        both = jnp.dot(block, w_qkv[:, width:], preferred_element_type=f32).astype(bf16)
-        values[s : s + lanes, :] = both[:, width:]
-        affinity = lax.dot_general(
-            spread_queries[...], both[:, :width], nt, preferred_element_type=f32
-        )
+        values[s : s + lanes, :] = jnp.dot(
+            block, w_qkv[:, 2 * width :], preferred_element_type=f32
+        ).astype(bf16)
+        affinity = lax.dot_general(keyed[...], block, nt, preferred_element_type=f32)
         here = bias[:, s : s + lanes].astype(f32)
         rows = []
         for i in range(own):
@@ -318,6 +332,14 @@
     )
     here = coords[...]
     moved[...] = here + (here * pulled[3:4] - pulled[0:3]) * (1.0 / atoms)
+
+
+def exchange(x, step, distance):
+    rows, cols = lax.axis_size("row"), lax.axis_size("col")
+    pairs = [
+        (r * cols + c, (r ^ step) * cols + (c ^ distance)) for r in range(rows) for c in range(cols)
+    ]
+    return lax.ppermute(x, ("row", "col"), pairs)
 
 
 def shards(
@@ -344,9 +366,23 @@
     kinds, gauss = gauss_mul.shape[0], gauss_mean.shape[0]
     atoms = own * rows * cols
     dims = (own, cols, width, heads, keys, kinds)
+    bias_rows, mask_rows, first_rows, second_rows = sizes(dims)
     shape = jax.ShapeDtypeStruct
     params = pltpu.CompilerParams(vmem_limit_bytes=(16 if atoms <= 128 else 56) * 2**20)
     vmem, anywhere = pl.BlockSpec(memory_space=pltpu.VMEM), pl.BlockSpec(memory_space=pl.ANY)
+
+    def call(kernel, name, out_shape, inputs, remote=(), scratch=()):
+        single = not isinstance(out_shape, list)
+        return pl.pallas_call(
+            kernel,
+            out_shape=out_shape,
+            in_specs=[vmem] * len(inputs) + [anywhere] * len(remote),
+            out_specs=vmem if single else [vmem] * len(out_shape),
+            scratch_shapes=list(scratch),
+            compiler_params=params,
+            name=name,
+        )(*inputs, *map(in_hbm, remote))
+
     sources = (
         nodes,
         coords,
@@ -355,41 +391,39 @@
         pair_mask,
         pair_bias.transpose(1, 2, 0),
     )
-    packed = pl.pallas_call(
+    mine, kept = call(
         functools.partial(pack_kernel, dims),
-        out_shape=[shape((payload_rows(dims), lanes), bf16)] * cols,
-        in_specs=[anywhere] * 6,
-        out_specs=[vmem] * cols,
-        scratch_shapes=[pltpu.VMEM(x.shape, x.dtype) for x in sources]
-        + [pltpu.VMEM((cols, own * keys // lanes, lanes), f32), pltpu.SemaphoreType.DMA((6,))],
-        compiler_params=params,
-        name="pack",
-    )(*map(in_hbm, sources))
-    arrived = [packed[0]] + [
-        lax.ppermute(packed[k], "col", [(i, i ^ k) for i in range(cols)]) for k in range(1, cols)
-    ]
-    near = pl.pallas_call(
-        functools.partial(gather_kernel, dims),
-        out_shape=shape((own * cols, width + lanes), bf16),
-        in_specs=[vmem] * cols,
-        out_specs=vmem,
-        compiler_params=params,
-        name="gather",
-    )(*arrived)
-    steps = [2**n for n in range(1, rows.bit_length() - 1)] + [1]
-    bias = pl.pallas_call(
-        functools.partial(arrange_kernel, dims, steps),
-        out_shape=shape((own * heads, atoms), bf16),
-        in_specs=[vmem] * cols,
-        out_specs=vmem,
-        compiler_params=params,
-        name="arrange",
-    )(*arrived)
+        "pack",
+        [
+            shape((first_rows, lanes), bf16),
+            shape((-(-(bias_rows + mask_rows) // 16) * 16, lanes), bf16),
+        ],
+        (),
+        sources,
+        [pltpu.VMEM(x.shape, x.dtype) for x in sources]
+        + [pltpu.VMEM((cols, mask_rows, lanes), f32), pltpu.SemaphoreType.DMA((6,))],
+    )
+    order = (cols - 1, *range(1, cols - 1))
+    other = exchange(mine, 1, 0)
+    grouped = call(
+        functools.partial(regroup_kernel, dims, order),
+        "regroup",
+        [shape((second_rows, lanes), bf16)] * (cols - 1),
+        (mine, other),
+    )
+    received = [exchange(x, 1, k) for x, k in zip(grouped, order, strict=True)]
+    near = call(
+        functools.partial(gather_kernel, dims, order),
+        "gather",
+        shape((2 * own * cols, width + lanes), bf16),
+        (mine, other, *received),
+    )
     weights = (w_qkv, w_heads.T, ln_gain[None, :], w_coord2[None, :], coords)
     tables = (gauss_mul, gauss_add, gauss_mean[None, :], gauss_width[None, :], w_gauss, w_coord1)
-    prepared = pl.pallas_call(
+    prepared = call(
         functools.partial(prepare_kernel, dims),
-        out_shape=[shape(x.shape, x.dtype) for x in weights]
+        "prepare",
+        [shape(x.shape, x.dtype) for x in weights]
         + [
             shape((gauss, gauss), bf16),
             shape(w_coord1.shape, bf16),
@@ -398,31 +432,35 @@
             shape((24, lanes), f32),
             shape((3, gauss, lanes), f32),
         ],
-        in_specs=[vmem] + [anywhere] * 11,
-        out_specs=[vmem] * 11,
-        scratch_shapes=[pltpu.VMEM(x.shape, x.dtype) for x in tables]
-        + [pltpu.SemaphoreType.DMA((11,))],
-        compiler_params=params,
-        name="prepare",
-    )(near, *map(in_hbm, weights + tables))
-    for n, step in enumerate(steps):
-        far = lax.ppermute(near, "row", [(i, i ^ step) for i in range(rows)])
-        if n < len(steps) - 1:
-            near = jnp.concatenate([near, far], axis=0)
-    attended, moved = pl.pallas_call(
-        functools.partial(attend_kernel, dims),
-        out_shape=[shape((own, width), bf16), shape((3, own), f32)],
-        in_specs=[vmem] * 14,
-        out_specs=[vmem] * 2,
-        scratch_shapes=[
+        (lax.optimization_barrier((mine, other))[0],),
+        weights + tables,
+        [pltpu.VMEM(x.shape, x.dtype) for x in tables] + [pltpu.SemaphoreType.DMA((11,))],
+    )
+    near, prepared = lax.optimization_barrier((near, prepared))
+    w_qkv, w_heads, ln_gain, w_coord2, coords, w_gauss, w_coord1, spread_queries, lookup = prepared[:9]
+    own_columns, kernels = prepared[9:]
+    steps = [0] + [step + 1 for step in range(2, rows, 2)]
+    pieces = [near] + [exchange(near, step, 0) for step in steps[1:]]
+    bias, keyed = call(
+        functools.partial(arrange_kernel, dims, order, steps),
+        "arrange",
+        [shape((own * heads, atoms), bf16), shape((own * heads, width), bf16)],
+        (kept, *received, spread_queries, w_qkv),
+    )
+    attended, moved = call(
+        functools.partial(attend_kernel, dims, len(pieces)),
+        "attend",
+        [shape((own, width), bf16), shape((3, own), f32)],
+        (*pieces, bias, keyed, w_qkv, w_heads, ln_gain, w_coord2, coords)
+        + (w_gauss, w_coord1, lookup, own_columns, kernels),
+        (),
+        [
             pltpu.VMEM((own * heads, atoms), f32),
             pltpu.VMEM((atoms, width), bf16),
             pltpu.VMEM((16, atoms), f32),
             pltpu.VMEM((own, atoms), f32),
         ],
-        compiler_params=params,
-        name="attend",
-    )(near, far, bias, *prepared)
+    )
     return attended, moved
 
 

time: 25.4 us -> 20.4 us (0.80)
  waiting for transfers between devices: 10.4 us -> 5.08 us
  starting transfers between devices: 8.83 us -> 9.12 us
    ppermute x6 -> x7, waiting for transfers between devices: 10.4 us -> 5.08 us  [exchange(): return lax.ppermute(x, ('row', 'col'), pairs)]
    ppermute x6 -> x7, starting transfers between devices: 8.83 us -> 9.12 us  [exchange(): return lax.ppermute(x, ('row', 'col'), pairs)]
    pallas_call x5 -> x6, Pallas kernels: 5.31 us -> 5.29 us  [call(): pl.pallas_call(kernel, out_shape=out_shape, in_specs=[vmem] * len(inputs)...]
  transfers between devices with their start and end apart: 6 -> 7, of which waited for: 4 -> 6; matrix products, arithmetic and copies ran while one was open for 0% -> 0% of each run, Pallas kernels for 9% -> 11%
where the time goes in v3:
time: 20.4 us; the launch traced here: 20.2 us
  starting transfers between devices  9.12 us (45%)
  Pallas kernels  5.29 us (26%)
  waiting for transfers between devices  5.08 us (25%)
  between operations  0.68 us (3%)
    ppermute x7, starting transfers between devices, exchange(): return lax.ppermute(x, ('row', 'col'), pairs)  9.12 us
    pallas_call x6, Pallas kernels, call(): pl.pallas_call(kernel, out_shape=out_shape, in_specs=[vmem] * len(inputs)...  5.29 us
    ppermute x7, waiting for transfers between devices, exchange(): return lax.ppermute(x, ('row', 'col'), pairs)  5.08 us
  transfers between devices with their start and end apart: 7, of which 6 were waited for; matrix products, arithmetic and copies ran while one was open for 0% of the time, Pallas kernels for 11%

profile of v3, /device:TPU:0, one launch (start us, length us, event | category | flops | bytes accessed | tf_op | source)
XLA Modules:
  0.0 20.2 jit_solution(4536217108407845969)
XLA Ops:
  0.6 1.1 %pack.1 = (bf16[224,128]{1,0:T(8,128)(2,1)S(1)}, bf16[80,128]{1,0:T(8,128)(2,1)S(1)}) custom-call(bf16[4,512]{1,0:T(4,128)(2,1)} %refs_0_.2, f32[3,4]{1,0:T(4,128)} %refs_4_.3, s32[1,4]{1,0:T(1,128)} %bitcast.11, s32[1,4]{1,0:T(1,128)} %bitcast.12, s32[16,32]{1,0:T(8,128)} %refs_4_.2, bf16[16,32,64]{2,1,0:T(8,128)(2,1)} %bitcast.8), custom_call_target="tpu_custom_call" | custom-call | tf_op jit(solution)/shard_map/pack/pallas_call | solution.py:376
  1.8 0.5 %collective-permute-start = (bf16[224,128]{1,0:T(8,128)(2,1)S(1)}, bf16[224,128]{1,0:T(8,128)(2,1)S(1)}, u32[]{:S(2)}, u32[]{:S(2)}) collective-permute-start(bf16[224,128]{1,0:T(8,128)(2,1)S(1)} %get-tuple-element.37.mine), channel_id=1, source_target_pairs={{0,4},{1,5},{2,6},{3,7},{4,0},{5,1},{6,2},{7,3},{8,12},{9,13},{10,... | collective-permute-start | bytes 172040 | tf_op jit(solution)/shard_map/ppermute | solution.py:342
  2.3 0.9 %collective-permute-done.other = bf16[224,128]{1,0:T(8,128)(2,1)S(1)} collective-permute-done((bf16[224,128]{1,0:T(8,128)(2,1)S(1)}, bf16[224,128]{1,0:T(8,128)(2,1)S(1)}, u32[]{:S(2)}, u32[]{:S(2)}) %collective-permute-start) | collective-permute-done | bytes 57376 | tf_op jit(solution)/shard_map/ppermute | solution.py:342
  3.2 4.8 %collective-permute-start.1 = (bf16[112,128]{1,0:T(8,128)(2,1)S(1)}, bf16[112,128]{1,0:T(8,128)(2,1)S(1)}, u32[]{:S(2)}, u32[]{:S(2)}) collective-permute-start(bf16[112,128]{1,0:T(8,128)(2,1)S(1)} %get-tuple-element.34), channel_id=1, source_target_pairs={{0,7},{1,6},{2,5},{3,4},{4,3},{5,2},{6,1},{7,0},{8,15},{9,14},{10,... | collective-permute-start | bytes 86024 | tf_op jit(solution)/shard_map/ppermute | solution.py:342
  8.0 0.0 collective-permute-start.2
  8.0 0.6 %collective-permute-start.3 = (bf16[112,128]{1,0:T(8,128)(2,1)S(1)}, bf16[112,128]{1,0:T(8,128)(2,1)S(1)}, u32[]{:S(2)}, u32[]{:S(2)}) collective-permute-start(bf16[112,128]{1,0:T(8,128)(2,1)S(1)} %get-tuple-element.36), channel_id=1, source_target_pairs={{0,6},{1,7},{2,4},{3,5},{4,2},{5,3},{6,0},{7,1},{8,14},{9,15},{10,... | collective-permute-start | bytes 86024 | tf_op jit(solution)/shard_map/ppermute | solution.py:342
  8.6 2.0 %prepare.1 = (bf16[512,1536]{1,0:T(8,128)(2,1)S(1)}, bf16[64,128]{1,0:T(8,128)(2,1)S(1)}, f32[1,512]{1,0:T(1,128)S(1)}, bf16[1,64]{1,0:T(2,128)(2,1)S(1)}, f32[3...) custom-call(bf16[224,128]{1,0:T(8,128)(2,1)S(1)} %get-tuple-element., ...), custom_call_target="tpu_custom_call" | custom-call | tf_op jit(solution)/shard_map/prepare/pallas_call | solution.py:376
  10.5 0.0 collective-permute-done.1.refs_0_
  10.5 0.7 %collective-permute-done.2.refs_1_ = bf16[112,128]{1,0:T(8,128)(2,1)S(1)} collective-permute-done((bf16[112,128]{1,0:T(8,128)(2,1)S(1)}, bf16[112,128]{1,0:T(8,128)(2,1)S(1)}, u32[]{:S(2)}, u32[]{:S(2)}) %collective-permute-start.2) | collective-permute-done | bytes 28704 | tf_op jit(solution)/shard_map/ppermute | solution.py:342
  11.3 0.9 %collective-permute-done.3.refs_2_ = bf16[112,128]{1,0:T(8,128)(2,1)S(1)} collective-permute-done((bf16[112,128]{1,0:T(8,128)(2,1)S(1)}, bf16[112,128]{1,0:T(8,128)(2,1)S(1)}, u32[]{:S(2)}, u32[]{:S(2)}) %collective-permute-start.3) | collective-permute-done | bytes 28704 | tf_op jit(solution)/shard_map/ppermute | solution.py:342
  12.2 2.5 %collective-permute-start.6 = (bf16[32,640]{1,0:T(8,128)(2,1)S(1)}, bf16[32,640]{1,0:T(8,128)(2,1)S(1)}, u32[]{:S(2)}, u32[]{:S(2)}) collective-permute-start(bf16[32,640]{1,0:T(8,128)(2,1)S(1)} %gather.1.refs_0_), channel_id=1, source_target_pairs={{0,28},{1,29},{2,30},{3,31},{4,24},{5,25},{6,26},{7,27},{8,20},{9,... | collective-permute-start | bytes 122888 | tf_op jit(solution)/shard_map/ppermute | solution.py:342
  14.6 0.3 %collective-permute-start.5 = (bf16[32,640]{1,0:T(8,128)(2,1)S(1)}, bf16[32,640]{1,0:T(8,128)(2,1)S(1)}, u32[]{:S(2)}, u32[]{:S(2)}) collective-permute-start(bf16[32,640]{1,0:T(8,128)(2,1)S(1)} %gather.1.refs_0_), channel_id=1, source_target_pairs={{0,20},{1,21},{2,22},{3,23},{4,16},{5,17},{6,18},{7,19},{8,28},{9,... | collective-permute-start | bytes 122888 | tf_op jit(solution)/shard_map/ppermute | solution.py:342
  14.9 0.5 %collective-permute-start.4 = (bf16[32,640]{1,0:T(8,128)(2,1)S(1)}, bf16[32,640]{1,0:T(8,128)(2,1)S(1)}, u32[]{:S(2)}, u32[]{:S(2)}) collective-permute-start(bf16[32,640]{1,0:T(8,128)(2,1)S(1)} %gather.1.refs_0_), channel_id=1, source_target_pairs={{0,12},{1,13},{2,14},{3,15},{4,8},{5,9},{6,10},{7,11},{8,4},{9,5},... | collective-permute-start | bytes 122888 | tf_op jit(solution)/shard_map/ppermute | solution.py:342
  15.4 0.4 %arrange.1 = (bf16[256,128]{1,0:T(8,128)(2,1)S(1)}, bf16[256,512]{1,0:T(8,128)(2,1)S(1)}) custom-call(bf16[80,128]{1,0:T(8,128)(2,1)S(1)} %get-tuple-element.50.kept, bf16[112,128]{1,0:T(8,128)(2,1)S(1)} %collective-permute-done.1.refs_0_, bf16[112,128]{1,0:T(8,128)(2,1)S(1)} %collective-permute-done.2.refs_1_, ...), custom_call_target="tpu_custom_call" | custom-call | tf_op jit(solution)/shard_map/arrange/pallas_call | solution.py:376
  15.8 0.8 %collective-permute-done.6.refs_3_ = bf16[32,640]{1,0:T(8,128)(2,1)S(1)} collective-permute-done((bf16[32,640]{1,0:T(8,128)(2,1)S(1)}, bf16[32,640]{1,0:T(8,128)(2,1)S(1)}, u32[]{:S(2)}, u32[]{:S(2)}) %collective-permute-start.6) | collective-permute-done | bytes 40992 | tf_op jit(solution)/shard_map/ppermute | solution.py:342
  16.6 1.6 %collective-permute-done.5.refs_2_ = bf16[32,640]{1,0:T(8,128)(2,1)S(1)} collective-permute-done((bf16[32,640]{1,0:T(8,128)(2,1)S(1)}, bf16[32,640]{1,0:T(8,128)(2,1)S(1)}, u32[]{:S(2)}, u32[]{:S(2)}) %collective-permute-start.5) | collective-permute-done | bytes 40992 | tf_op jit(solution)/shard_map/ppermute | solution.py:342
  18.2 0.2 collective-permute-done.4.refs_1_
  18.3 1.8 %attend.1 = (bf16[4,512]{1,0:T(4,128)(2,1)}, f32[3,4]{1,0:T(4,128)}) custom-call(bf16[32,640]{1,0:T(8,128)(2,1)S(1)} %gather.1.refs_0_, bf16[32,640]{1,0:T(8,128)(2,1)S(1)} %collective-permute-done.4.refs_1_, bf16[32,640]{1,0:T(8,128)(2,1)S(1)} %collective-permute-done.5.refs_2_, bf16[32,640]{1,0:T(8,128)(2,1)S(1)} %collective-permute-done.6.refs_3_, ...), custom_call_target="tpu_custom_call" | custom-call | tf_op jit(solution)/shard_map/attend/pallas_call | solution.py:376
  (2 shorter events, 0.0 us)
Async XLA Ops:
  1.8 1.4 %collective-permute-start = (bf16[224,128]{1,0:T(8,128)(2,1)S(1)}, bf16[224,128]{1,0:T(8,128)(2,1)S(1)}, u32[]{:S(2)}, u32[]{:S(2)}) collective-permute-start(bf16[224,128]{1,0:T(8,128)(2,1)S(1)} %get-tuple-element.37.mine), channel_id=1, source_target_pairs={{0,4},{1,5},{2,6},{3,7},{4,0},{5,1},{6,2},{7,3},{8,12},{9,13},{10,... | collective-permute-start | bytes 172040 | tf_op jit(solution)/shard_map/ppermute | solution.py:342
  3.2 7.3 %collective-permute-start.1 = (bf16[112,128]{1,0:T(8,128)(2,1)S(1)}, bf16[112,128]{1,0:T(8,128)(2,1)S(1)}, u32[]{:S(2)}, u32[]{:S(2)}) collective-permute-start(bf16[112,128]{1,0:T(8,128)(2,1)S(1)} %get-tuple-element.34), channel_id=1, source_target_pairs={{0,7},{1,6},{2,5},{3,4},{4,3},{5,2},{6,1},{7,0},{8,15},{9,14},{10,... | collective-permute-start | bytes 86024 | tf_op jit(solution)/shard_map/ppermute | solution.py:342
  8.0 3.3 %collective-permute-start.2 = (bf16[112,128]{1,0:T(8,128)(2,1)S(1)}, bf16[112,128]{1,0:T(8,128)(2,1)S(1)}, u32[]{:S(2)}, u32[]{:S(2)}) collective-permute-start(bf16[112,128]{1,0:T(8,128)(2,1)S(1)} %get-tuple-element.35), channel_id=1, source_target_pairs={{0,5},{1,4},{2,7},{3,6},{4,1},{5,0},{6,3},{7,2},{8,13},{9,12},{10,... | collective-permute-start | bytes 86024 | tf_op jit(solution)/shard_map/ppermute | solution.py:342
  8.0 4.2 %collective-permute-start.3 = (bf16[112,128]{1,0:T(8,128)(2,1)S(1)}, bf16[112,128]{1,0:T(8,128)(2,1)S(1)}, u32[]{:S(2)}, u32[]{:S(2)}) collective-permute-start(bf16[112,128]{1,0:T(8,128)(2,1)S(1)} %get-tuple-element.36), channel_id=1, source_target_pairs={{0,6},{1,7},{2,4},{3,5},{4,2},{5,3},{6,0},{7,1},{8,14},{9,15},{10,... | collective-permute-start | bytes 86024 | tf_op jit(solution)/shard_map/ppermute | solution.py:342
  12.2 4.4 %collective-permute-start.6 = (bf16[32,640]{1,0:T(8,128)(2,1)S(1)}, bf16[32,640]{1,0:T(8,128)(2,1)S(1)}, u32[]{:S(2)}, u32[]{:S(2)}) collective-permute-start(bf16[32,640]{1,0:T(8,128)(2,1)S(1)} %gather.1.refs_0_), channel_id=1, source_target_pairs={{0,28},{1,29},{2,30},{3,31},{4,24},{5,25},{6,26},{7,27},{8,20},{9,... | collective-permute-start | bytes 122888 | tf_op jit(solution)/shard_map/ppermute | solution.py:342
  14.6 3.5 %collective-permute-start.5 = (bf16[32,640]{1,0:T(8,128)(2,1)S(1)}, bf16[32,640]{1,0:T(8,128)(2,1)S(1)}, u32[]{:S(2)}, u32[]{:S(2)}) collective-permute-start(bf16[32,640]{1,0:T(8,128)(2,1)S(1)} %gather.1.refs_0_), channel_id=1, source_target_pairs={{0,20},{1,21},{2,22},{3,23},{4,16},{5,17},{6,18},{7,19},{8,28},{9,... | collective-permute-start | bytes 122888 | tf_op jit(solution)/shard_map/ppermute | solution.py:342
  14.9 3.4 %collective-permute-start.4 = (bf16[32,640]{1,0:T(8,128)(2,1)S(1)}, bf16[32,640]{1,0:T(8,128)(2,1)S(1)}, u32[]{:S(2)}, u32[]{:S(2)}) collective-permute-start(bf16[32,640]{1,0:T(8,128)(2,1)S(1)} %gather.1.refs_0_), channel_id=1, source_target_pairs={{0,12},{1,13},{2,14},{3,15},{4,8},{5,9},{6,10},{7,11},{8,4},{9,5},... | collective-permute-start | bytes 122888 | tf_op jit(solution)/shard_map/ppermute | solution.py:342

commit v4 on v3

--- a/solution.py
+++ b/solution.py
@@ -40,15 +40,18 @@
     return (0.5 * x) * (1.0 + jnp.tanh(inner))
 
 
+table_rows = 16
+
+
 def node_rows(width, own):
-    return (width // lanes + 1) * own
+    return width // lanes * own
 
 
 def sizes(dims):
     own, cols, width, heads, keys, kinds = dims
     bias_rows, mask_rows = own * keys * heads // lanes, own * keys // lanes
-    first = node_rows(width, own) + (cols - 1) * (bias_rows + mask_rows)
-    second = bias_rows + 2 * node_rows(width, own) + mask_rows
+    first = table_rows + node_rows(width, own) + (cols - 1) * (bias_rows + mask_rows)
+    second = bias_rows + table_rows + 2 * node_rows(width, own) + mask_rows
     return bias_rows, mask_rows, -(-first // 16) * 16, -(-second // 16) * 16
 
 
@@ -81,15 +84,13 @@
     pairs, fold = own * keys, lanes // heads
     for copy in copies[:4]:
         copy.wait()
-    lane = iota((own, lanes), 1)
-    table = jnp.zeros((own, lanes), f32)
-    for c in range(3):
-        for n, part in enumerate(split3(column(coords[c : c + 1, :]))):
-            table = jnp.where(lane == 3 * n + c, part, table)
+    high, middle, low = split3(coords[...])
     kind = (types[...] + kinds // 2 * segments[...]).astype(f32)
-    table = jnp.where(lane == 9, column(kind), table)
+    blank = jnp.zeros((1, own), f32)
+    table = jnp.concatenate([high, kind, low, blank, middle] + [blank] * 5, axis=0)
+    table = jnp.concatenate([table, jnp.zeros((table_rows, lanes - own), f32)], axis=1)
     full = nodes[...].astype(f32)
-    blocks = [full[:, b * lanes : (b + 1) * lanes] for b in range(width // lanes)] + [table]
+    blocks = [table] + [full[:, b * lanes : (b + 1) * lanes] for b in range(width // lanes)]
     copies[4].wait()
     wide_mask = mask[...].astype(f32)
     for d in range(cols):
@@ -114,12 +115,14 @@
 def regroup_kernel(dims, order, mine, other, *outs):
     own, cols, width, heads, keys, kinds = dims
     bias_rows, mask_rows, first_rows, second_rows = sizes(dims)
-    start, rows = (cols - 1) * bias_rows, node_rows(width, own)
+    start, rows = (cols - 1) * bias_rows, table_rows + node_rows(width, own)
     here, there = mine[start:, :].astype(f32), other[start:, :].astype(f32)
+    table = here[:table_rows] + pltpu.roll(there[:table_rows], own, 1)
     for n, k in enumerate(order):
         outs[n][:bias_rows, :] = other[(k - 1) * bias_rows : k * bias_rows, :]
         at = rows + (k - 1) * mask_rows
-        tail = filled([here[:rows], there[:rows], there[at : at + mask_rows]], second_rows - bias_rows)
+        tail = [table, here[table_rows:rows], there[table_rows:rows], there[at : at + mask_rows]]
+        tail = filled(tail, second_rows - bias_rows)
         outs[n][bias_rows:, :] = tail.astype(bf16)
 
 
@@ -128,13 +131,19 @@
     bias_rows, mask_rows, first_rows, second_rows = sizes(dims)
     start, rows = (cols - 1) * bias_rows, node_rows(width, own)
     out = refs[cols - 1]
-    blocks = [mine[start:, :].astype(f32)[:rows], other[start:, :].astype(f32)[:rows]]
-    for k in range(1, cols):
-        tail = refs[order.index(k)][bias_rows:, :].astype(f32)
-        blocks += [tail[rows : 2 * rows], tail[:rows]]
-    for b in range(width // lanes + 1):
+    here, there = mine[start:, :].astype(f32), other[start:, :].astype(f32)
+    tails = [refs[order.index(k)][bias_rows:, :].astype(f32) for k in range(1, cols)]
+    table = here[:table_rows] + pltpu.roll(there[:table_rows], own, 1)
+    for k, tail in enumerate(tails, 1):
+        table = table + pltpu.roll(tail[:table_rows], 2 * own * k, 1)
+    out[:table_rows, :] = table.astype(bf16)
+    blocks = [here[table_rows:], there[table_rows:]]
+    for tail in tails:
+        blocks += [tail[table_rows : table_rows + rows], tail[table_rows + rows :]]
+    each = 2 * own * cols
+    for b in range(width // lanes):
         taken = jnp.concatenate([block[b * own : (b + 1) * own] for block in blocks], axis=0)
-        out[:, b * lanes : (b + 1) * lanes] = taken.astype(bf16)
+        out[table_rows + b * each : table_rows + (b + 1) * each, :] = taken.astype(bf16)
 
 
 def arrange_kernel(dims, order, steps, kept, *refs):
@@ -142,13 +151,14 @@
     bias_rows, mask_rows, first_rows, second_rows = sizes(dims)
     received = [refs[order.index(k)] for k in range(1, cols)]
     spread_queries, w_qkv, out, keyed = refs[cols - 1 :]
-    keyed[...] = lax.dot_general(
+    through_keys = lax.dot_general(
         spread_queries[...], w_qkv[:, width : 2 * width], nt, preferred_element_type=f32
-    ).astype(bf16)
+    )
+    keyed[...] = (through_keys * (1.0 / math.sqrt(width // heads))).astype(bf16)
     atoms = out.shape[1]
     fold = lanes // heads
     each = own // fold
-    mask_at = 2 * node_rows(width, own)
+    mask_at = table_rows + 2 * node_rows(width, own)
     per_row = 2 * own * cols
     r, c = lax.axis_index("row"), lax.axis_index("col")
     blocks = [
@@ -170,8 +180,9 @@
         step = jnp.zeros((1, lanes), jnp.int32)
         for n, value in enumerate(steps):
             step = jnp.where(piece == n, value, step)
-        row = r ^ step ^ (inner // own % 2)
-        source = (row * cols + (c ^ (inner // (2 * own)))) * own + inner % own
+        distance = inner // (2 * own)
+        row = r ^ step ^ (inner // own % 2) ^ (distance > 0).astype(jnp.int32)
+        source = (row * cols + (c ^ distance)) * own + inner % own
         chosen = (atom == source).astype(f32).astype(bf16)
         valid = jnp.dot(masks, chosen, preferred_element_type=f32)
         for b in range(each):
@@ -193,49 +204,50 @@
     own, cols, width, heads, keys, kinds = dims
     bias_rows, mask_rows, first_rows, second_rows = sizes(dims)
     sources = refs[:11]
-    w_qkv, w_heads, ln_gain, w_coord2, coords = refs[11:16]
-    w_gauss, w_coord1, spread_queries, lookup, own_columns, kernels = refs[16:22]
-    mul_held, add_held, mean_held, width_held, gauss_held, coord1_held, semaphores = refs[22:]
+    w_qkv, w_heads, ln_gain, coords, w_gauss, w_coord1, w_coord2, spread_queries = refs[11:19]
+    lookup, own_columns, kernels = refs[19:22]
+    mul_held, add_held, mean_held, width_held, gauss_held, coord1_held, coord2_held = refs[22:29]
+    semaphores = refs[29]
     copies = fetch(
         sources,
-        (w_qkv, w_heads, ln_gain, w_coord2, coords)
-        + (mul_held, add_held, mean_held, width_held, gauss_held, coord1_held),
+        (w_qkv, w_heads, ln_gain, coords, mul_held, add_held, mean_held, width_held)
+        + (gauss_held, coord1_held, coord2_held),
         semaphores,
     )
-    rows = mine[(cols - 1) * bias_rows :, :].astype(f32)[: node_rows(width, own)]
-    filler = jnp.zeros((16 - own, lanes), f32)
-    x = [
-        jnp.concatenate([rows[b * own : (b + 1) * own], filler], axis=0)
-        for b in range(width // lanes + 1)
-    ]
-    own_table = x[width // lanes]
+    tail = mine[(cols - 1) * bias_rows :, :].astype(f32)
+    table, rows = tail[:table_rows], tail[table_rows : table_rows + node_rows(width, own)]
+    places = (table[0:3] + table[8:11]) + table[4:7]
     for c in range(3):
-        parts = (own_table[:, c : c + 1] + own_table[:, 3 + c : 4 + c]) + own_table[:, 6 + c : 7 + c]
-        own_columns[c * 8 : c * 8 + 8, :] = jnp.broadcast_to(parts[:8], (8, lanes))
-    own_kind = own_table[:, 9:10].astype(jnp.int32)
+        own_columns[c * 8 : c * 8 + own, :] = jnp.broadcast_to(
+            column(places[c : c + 1, :own]), (own, lanes)
+        )
+    own_kind = column(table[3:4, :own]).astype(jnp.int32)
+    own_kind = jnp.concatenate([own_kind, jnp.zeros((16 - own, 1), jnp.int32)], axis=0)
     query_onehot = (own_kind == iota((16, kinds), 1)).astype(f32).astype(bf16)
-    for copy in copies[5:]:
+    for copy in copies[4:]:
         copy.wait()
     inverse = 1.0 / column(width_held[...])
     gauss = inverse.shape[0]
     kernels[0] = jnp.broadcast_to(column(mean_held[...]), (gauss, lanes))
     kernels[1] = jnp.broadcast_to(inverse * math.sqrt(0.5 * math.log2(math.e)), (gauss, lanes))
     kernels[2] = jnp.broadcast_to(jnp.log2(inverse * (1.0 / math.sqrt(2.0 * math.pi))), (gauss, lanes))
-    at = 0
+    found = []
     for table in (mul_held, add_held):
-        for part in split3(table[...]):
-            found = jnp.dot(query_onehot, part.astype(bf16), preferred_element_type=f32)
-            lookup[at : at + 16, :] = found.astype(bf16)
-            at += 16
+        parts = [
+            jnp.dot(query_onehot, part.astype(bf16), preferred_element_type=f32)
+            for part in split3(table[...])
+        ]
+        found.append((parts[0] + parts[1] + parts[2])[:own])
+    found = jnp.concatenate(found, axis=0)
+    lookup[...] = jnp.concatenate([found, jnp.zeros((2 * own, lanes - kinds), f32)], axis=1)
     w_gauss[...] = gauss_held[...].astype(f32).T.astype(bf16)
     w_coord1[...] = coord1_held[...].astype(f32).T.astype(bf16)
-    for copy in copies[:5]:
+    w_coord2[...] = jnp.broadcast_to(column(coord2_held[...].astype(f32)), (heads, lanes))
+    for copy in copies[:4]:
         copy.wait()
-    queries = jnp.dot(
-        normed(jnp.concatenate(x[:-1], axis=1), ln_gain[...]),
-        w_qkv[:, :width],
-        preferred_element_type=f32,
-    )
+    x = jnp.concatenate([rows[b * own : (b + 1) * own] for b in range(width // lanes)], axis=1)
+    x = jnp.concatenate([x, jnp.zeros((16 - own, width), f32)], axis=0)
+    queries = jnp.dot(normed(x, ln_gain[...]), w_qkv[:, :width], preferred_element_type=f32)
     head_mask = iota((heads, width), 1) // (width // heads) == iota((heads, width), 0)
     for i in range(own):
         spread = jnp.where(head_mask, jnp.broadcast_to(queries[i : i + 1], (heads, width)), 0.0)
@@ -245,44 +257,43 @@
 def attend_kernel(dims, count, *refs):
     own, cols, width, heads, keys, kinds = dims
     pieces = refs[:count]
-    bias, keyed, w_qkv, w_heads, ln_gain, w_coord2, coords = refs[count : count + 7]
-    w_gauss, w_coord1, lookup, own_columns, kernels, attended, moved = refs[count + 7 : count + 14]
-    logits, values, places, strengths = refs[count + 14 :]
+    bias, keyed, w_qkv, w_heads, ln_gain, coords = refs[count : count + 6]
+    w_gauss, w_coord1, w_coord2, lookup, own_columns, kernels = refs[count + 6 : count + 12]
+    attended, moved, logits, values, places, strengths = refs[count + 12 :]
     atoms = bias.shape[1]
-    head_dim = width // heads
-    each = lanes // pieces[0].shape[0]
+    each = 2 * own * cols
     gain = ln_gain[...]
-    select_at, select_from = iota((16, lanes), 0), iota((16, lanes), 1)
-    selector = (
-        ((select_from < 9) & (select_from % 3 == select_at) & (select_at < 3))
-        | ((select_from == 9) & (select_at == 3))
-    ).astype(f32).astype(bf16)
     centre, sharp, norming = kernels[0], kernels[1], kernels[2]
+    found = lookup[...]
 
     for s in range(0, atoms, lanes):
-        if each:
-            first = s // lanes * each
-            x = jnp.concatenate([ref[...] for ref in pieces[first : first + each]], axis=0)
-        else:
-            rows = pieces[0].shape[0]
-            x = pieces[s // rows][s % rows : s % rows + lanes, :]
-        table = lax.dot_general(selector, x[:, width:], nt, preferred_element_type=f32)
-        places[:, s : s + lanes] = jnp.where(iota((16, lanes), 0) == 3, 1.0, table)
-        offsets = [own_columns[c * 8 : c * 8 + own, :] - table[c : c + 1] for c in range(3)]
+        taken = pieces[s // each : (s + lanes) // each]
+        table = jnp.concatenate([ref[:table_rows, :].astype(f32)[:, :each] for ref in taken], axis=1)
+        place = (table[0:3] + table[8:11]) + table[4:7]
+        places[0:3, s : s + lanes] = place
+        offsets = [own_columns[c * 8 : c * 8 + own, :] - place[c : c + 1] for c in range(3)]
         squares = offsets[0] * offsets[0] + offsets[1] * offsets[1] + offsets[2] * offsets[2]
         distance = jnp.sqrt(squares + root_shift)
-        key_onehot = (table[3:4].astype(jnp.int32) == iota((kinds, lanes), 0)).astype(f32).astype(bf16)
-        found = jnp.dot(lookup[...], key_onehot, preferred_element_type=f32)
-        scale = found[0:16] + found[16:32] + found[32:48]
-        shift = found[48:64] + found[64:80] + found[80:96]
-        expanded = scale[:own] * distance + shift[:own]
+        kind = jnp.broadcast_to(table[3:4].astype(jnp.int32), (2 * own, lanes))
+        pair = jnp.take_along_axis(found, kind, axis=1)
+        expanded = pair[:own] * distance + pair[own:]
         features = []
         for i in range(own):
             scaled = (expanded[i : i + 1] - centre) * sharp
             features.append(jnp.exp2(norming - scaled * scaled).astype(bf16))
         hidden = jnp.dot(w_gauss[...], jnp.concatenate(features, axis=1), preferred_element_type=f32)
         geometry = jnp.dot(w_heads[...], gelu(hidden).astype(bf16), preferred_element_type=f32)
-        block = normed(x[:, :width], gain)
+        x = [
+            jnp.concatenate(
+                [
+                    ref[table_rows + b * each : table_rows + (b + 1) * each, :]
+                    for b in range(width // lanes)
+                ],
+                axis=1,
+            )
+            for ref in taken
+        ]
+        block = normed(jnp.concatenate(x, axis=0), gain)
         values[s : s + lanes, :] = jnp.dot(
             block, w_qkv[:, 2 * width :], preferred_element_type=f32
         ).astype(bf16)
@@ -291,29 +302,23 @@
         rows = []
         for i in range(own):
             at = slice(i * heads, (i + 1) * heads)
-            row = here[at] + geometry[:, i * lanes : (i + 1) * lanes]
-            row = row + affinity[at] * (1.0 / math.sqrt(head_dim))
+            row = (here[at] + affinity[at]) + geometry[:, i * lanes : (i + 1) * lanes]
             logits[at, s : s + lanes] = jnp.where(here[at] < masked_below, masked_fill, row)
             rows.append(row.astype(bf16))
         mixed = jnp.dot(w_coord1[...], jnp.concatenate(rows, axis=1), preferred_element_type=f32)
-        strength = jnp.dot(w_coord2[...], gelu(mixed).astype(bf16), preferred_element_type=f32)
-        strengths[:, s : s + lanes] = jnp.concatenate(
-            [
-                jnp.where(
-                    here[i * heads : i * heads + 1] < masked_below,
-                    0.0,
-                    strength[:, i * lanes : (i + 1) * lanes],
-                )
-                for i in range(own)
-            ],
-            axis=0,
-        )
+        mixed = gelu(mixed)
+        for i in range(own):
+            strength = jnp.sum(
+                mixed[:, i * lanes : (i + 1) * lanes] * w_coord2[...], axis=0, keepdims=True
+            )
+            masked = here[i * heads : i * heads + 1] < masked_below
+            strengths[i : i + 1, s : s + lanes] = jnp.where(masked, 0.0, strength)
 
     masked = logits[...]
     weights = jnp.exp(masked - jnp.max(masked, axis=1, keepdims=True))
     share = 1.0 / jnp.sum(weights, axis=1, keepdims=True)
     taken = jnp.dot(weights.astype(bf16), values[...], preferred_element_type=f32) * share
-    head_mask = iota((heads, width), 1) // head_dim == iota((heads, width), 0)
+    head_mask = iota((heads, width), 1) // (width // heads) == iota((heads, width), 0)
     attended[...] = jnp.concatenate(
         [
             jnp.sum(
@@ -323,15 +328,12 @@
         ],
         axis=0,
     ).astype(bf16)
-    pulled = lax.dot_general(
-        places[...],
-        strengths[...],
-        nt,
-        precision=lax.Precision.HIGHEST,
-        preferred_element_type=f32,
-    )
     here = coords[...]
-    moved[...] = here + (here * pulled[3:4] - pulled[0:3]) * (1.0 / atoms)
+    shift = jnp.zeros((3, own), f32)
+    for i in range(own):
+        pulls = (here[:, i : i + 1] - places[0:3, :]) * strengths[i : i + 1, :]
+        shift = jnp.where(iota((3, own), 1) == i, jnp.sum(pulls, axis=1, keepdims=True), shift)
+    moved[...] = here + shift * (1.0 / atoms)
 
 
 def exchange(x, step, distance):
@@ -415,11 +417,12 @@
     near = call(
         functools.partial(gather_kernel, dims, order),
         "gather",
-        shape((2 * own * cols, width + lanes), bf16),
+        shape((table_rows + 2 * node_rows(width, own) * cols, lanes), bf16),
         (mine, other, *received),
     )
-    weights = (w_qkv, w_heads.T, ln_gain[None, :], w_coord2[None, :], coords)
+    weights = (w_qkv, w_heads.T, ln_gain[None, :], coords)
     tables = (gauss_mul, gauss_add, gauss_mean[None, :], gauss_width[None, :], w_gauss, w_coord1)
+    tables += (w_coord2[None, :],)
     prepared = call(
         functools.partial(prepare_kernel, dims),
         "prepare",
@@ -427,8 +430,9 @@
         + [
             shape((gauss, gauss), bf16),
             shape(w_coord1.shape, bf16),
+            shape((heads, lanes), f32),
             shape((own * heads, width), bf16),
-            shape((96, kinds), bf16),
+            shape((2 * own, lanes), f32),
             shape((24, lanes), f32),
             shape((3, gauss, lanes), f32),
         ],
@@ -437,8 +441,8 @@
         [pltpu.VMEM(x.shape, x.dtype) for x in tables] + [pltpu.SemaphoreType.DMA((11,))],
     )
     near, prepared = lax.optimization_barrier((near, prepared))
-    w_qkv, w_heads, ln_gain, w_coord2, coords, w_gauss, w_coord1, spread_queries, lookup = prepared[:9]
-    own_columns, kernels = prepared[9:]
+    w_qkv, w_heads, ln_gain, coords, w_gauss, w_coord1, w_coord2, spread_queries = prepared[:8]
+    lookup, own_columns, kernels = prepared[8:]
     steps = [0] + [step + 1 for step in range(2, rows, 2)]
     pieces = [near] + [exchange(near, step, 0) for step in steps[1:]]
     bias, keyed = call(
@@ -451,14 +455,14 @@
         functools.partial(attend_kernel, dims, len(pieces)),
         "attend",
         [shape((own, width), bf16), shape((3, own), f32)],
-        (*pieces, bias, keyed, w_qkv, w_heads, ln_gain, w_coord2, coords)
-        + (w_gauss, w_coord1, lookup, own_columns, kernels),
+        (*pieces, bias, keyed, w_qkv, w_heads, ln_gain, coords)
+        + (w_gauss, w_coord1, w_coord2, lookup, own_columns, kernels),
         (),
         [
             pltpu.VMEM((own * heads, atoms), f32),
             pltpu.VMEM((atoms, width), bf16),
-            pltpu.VMEM((16, atoms), f32),
-            pltpu.VMEM((own, atoms), f32),
+            pltpu.VMEM((8, atoms), f32),
+            pltpu.VMEM((8, atoms), f32),
         ],
     )
     return attended, moved

time: 20.4 us -> 20.2 us (level)
  transfers between devices with their start and end apart: 7 -> 7, of which waited for: 6 -> 6; matrix products, arithmetic and copies ran while one was open for 0% -> 0% of each run, Pallas kernels for 11% -> 12%
where the time goes in v4:
time: 20.2 us; the launch traced here: 20 us
  starting transfers between devices  9.01 us (45%)
  Pallas kernels  5.22 us (26%)
  waiting for transfers between devices  5.07 us (25%)
  between operations  0.67 us (3%)
    ppermute x7, starting transfers between devices, exchange(): return lax.ppermute(x, ('row', 'col'), pairs)  9.01 us
    pallas_call x6, Pallas kernels, call(): pl.pallas_call(kernel, out_shape=out_shape, in_specs=[vmem] * len(inputs)...  5.22 us
    ppermute x7, waiting for transfers between devices, exchange(): return lax.ppermute(x, ('row', 'col'), pairs)  5.07 us
  transfers between devices with their start and end apart: 7, of which 6 were waited for; matrix products, arithmetic and copies ran while one was open for 0% of the time, Pallas kernels for 12%

profile of v4, /device:TPU:0, one launch (start us, length us, event | category | flops | bytes accessed | tf_op | source)
XLA Modules:
  0.0 20.0 jit_solution(15933462058314129992)
XLA Ops:
  0.6 1.1 %pack.1 = (bf16[240,128]{1,0:T(8,128)(2,1)S(1)}, bf16[80,128]{1,0:T(8,128)(2,1)S(1)}) custom-call(bf16[4,512]{1,0:T(4,128)(2,1)} %refs_0_.2, f32[3,4]{1,0:T(4,128)} %refs_3_.1, s32[1,4]{1,0:T(1,128)} %bitcast.11, s32[1,4]{1,0:T(1,128)} %bitcast.12, s32[16,32]{1,0:T(8,128)} %refs_4_.2, bf16[16,32,64]{2,1,0:T(8,128)(2,1)} %bitcast.8), custom_call_target="tpu_custom_call" | custom-call | tf_op jit(solution)/shard_map/pack/pallas_call | solution.py:378
  1.8 0.5 %collective-permute-start = (bf16[240,128]{1,0:T(8,128)(2,1)S(1)}, bf16[240,128]{1,0:T(8,128)(2,1)S(1)}, u32[]{:S(2)}, u32[]{:S(2)}) collective-permute-start(bf16[240,128]{1,0:T(8,128)(2,1)S(1)} %get-tuple-element.37.mine), channel_id=1, source_target_pairs={{0,4},{1,5},{2,6},{3,7},{4,0},{5,1},{6,2},{7,3},{8,12},{9,13},{10,... | collective-permute-start | bytes 184328 | tf_op jit(solution)/shard_map/ppermute | solution.py:344
  2.3 0.9 %collective-permute-done.other = bf16[240,128]{1,0:T(8,128)(2,1)S(1)} collective-permute-done((bf16[240,128]{1,0:T(8,128)(2,1)S(1)}, bf16[240,128]{1,0:T(8,128)(2,1)S(1)}, u32[]{:S(2)}, u32[]{:S(2)}) %collective-permute-start) | collective-permute-done | bytes 61472 | tf_op jit(solution)/shard_map/ppermute | solution.py:344
  3.2 0.1 regroup.1
  3.3 4.7 %collective-permute-start.1 = (bf16[128,128]{1,0:T(8,128)(2,1)S(1)}, bf16[128,128]{1,0:T(8,128)(2,1)S(1)}, u32[]{:S(2)}, u32[]{:S(2)}) collective-permute-start(bf16[128,128]{1,0:T(8,128)(2,1)S(1)} %get-tuple-element.34), channel_id=1, source_target_pairs={{0,7},{1,6},{2,5},{3,4},{4,3},{5,2},{6,1},{7,0},{8,15},{9,14},{10,... | collective-permute-start | bytes 98312 | tf_op jit(solution)/shard_map/ppermute | solution.py:344
  8.0 0.0 collective-permute-start.2
  8.0 0.6 %collective-permute-start.3 = (bf16[128,128]{1,0:T(8,128)(2,1)S(1)}, bf16[128,128]{1,0:T(8,128)(2,1)S(1)}, u32[]{:S(2)}, u32[]{:S(2)}) collective-permute-start(bf16[128,128]{1,0:T(8,128)(2,1)S(1)} %get-tuple-element.36), channel_id=1, source_target_pairs={{0,6},{1,7},{2,4},{3,5},{4,2},{5,3},{6,0},{7,1},{8,14},{9,15},{10,... | collective-permute-start | bytes 98312 | tf_op jit(solution)/shard_map/ppermute | solution.py:344
  8.6 2.0 %prepare.1 = (bf16[512,1536]{1,0:T(8,128)(2,1)S(1)}, bf16[64,128]{1,0:T(8,128)(2,1)S(1)}, f32[1,512]{1,0:T(1,128)S(1)}, f32[3,4]{1,0:T(4,128)S(1)}, bf16[128,128...) custom-call(bf16[240,128]{1,0:T(8,128)(2,1)S(1)} %get-tuple-element., ...), custom_call_target="tpu_custom_call" | custom-call | tf_op jit(solution)/shard_map/prepare/pallas_call | solution.py:378
  10.5 0.0 collective-permute-done.1.refs_0_
  10.6 0.8 %collective-permute-done.2.refs_1_ = bf16[128,128]{1,0:T(8,128)(2,1)S(1)} collective-permute-done((bf16[128,128]{1,0:T(8,128)(2,1)S(1)}, bf16[128,128]{1,0:T(8,128)(2,1)S(1)}, u32[]{:S(2)}, u32[]{:S(2)}) %collective-permute-start.2) | collective-permute-done | bytes 32800 | tf_op jit(solution)/shard_map/ppermute | solution.py:344
  11.3 0.9 %collective-permute-done.3.refs_2_ = bf16[128,128]{1,0:T(8,128)(2,1)S(1)} collective-permute-done((bf16[128,128]{1,0:T(8,128)(2,1)S(1)}, bf16[128,128]{1,0:T(8,128)(2,1)S(1)}, u32[]{:S(2)}, u32[]{:S(2)}) %collective-permute-start.3) | collective-permute-done | bytes 32800 | tf_op jit(solution)/shard_map/ppermute | solution.py:344
  12.2 0.1 gather.1.refs_0_
  12.3 2.4 %collective-permute-start.6 = (bf16[144,128]{1,0:T(8,128)(2,1)S(1)}, bf16[144,128]{1,0:T(8,128)(2,1)S(1)}, u32[]{:S(2)}, u32[]{:S(2)}) collective-permute-start(bf16[144,128]{1,0:T(8,128)(2,1)S(1)} %gather.1.refs_0_), channel_id=1, source_target_pairs={{0,28},{1,29},{2,30},{3,31},{4,24},{5,25},{6,26},{7,27},{8,20},{9,... | collective-permute-start | bytes 110600 | tf_op jit(solution)/shard_map/ppermute | solution.py:344
  14.7 0.3 %collective-permute-start.5 = (bf16[144,128]{1,0:T(8,128)(2,1)S(1)}, bf16[144,128]{1,0:T(8,128)(2,1)S(1)}, u32[]{:S(2)}, u32[]{:S(2)}) collective-permute-start(bf16[144,128]{1,0:T(8,128)(2,1)S(1)} %gather.1.refs_0_), channel_id=1, source_target_pairs={{0,20},{1,21},{2,22},{3,23},{4,16},{5,17},{6,18},{7,19},{8,28},{9,... | collective-permute-start | bytes 110600 | tf_op jit(solution)/shard_map/ppermute | solution.py:344
  15.0 0.5 %collective-permute-start.4 = (bf16[144,128]{1,0:T(8,128)(2,1)S(1)}, bf16[144,128]{1,0:T(8,128)(2,1)S(1)}, u32[]{:S(2)}, u32[]{:S(2)}) collective-permute-start(bf16[144,128]{1,0:T(8,128)(2,1)S(1)} %gather.1.refs_0_), channel_id=1, source_target_pairs={{0,12},{1,13},{2,14},{3,15},{4,8},{5,9},{6,10},{7,11},{8,4},{9,5},... | collective-permute-start | bytes 110600 | tf_op jit(solution)/shard_map/ppermute | solution.py:344
  15.5 0.4 %arrange.1 = (bf16[256,128]{1,0:T(8,128)(2,1)S(1)}, bf16[256,512]{1,0:T(8,128)(2,1)S(1)}) custom-call(bf16[80,128]{1,0:T(8,128)(2,1)S(1)} %get-tuple-element.50.kept, bf16[128,128]{1,0:T(8,128)(2,1)S(1)} %collective-permute-done.1.refs_0_, bf16[128,128]{1,0:T(8,128)(2,1)S(1)} %collective-permute-done.2.refs_1_, ...), custom_call_target="tpu_custom_call" | custom-call | tf_op jit(solution)/shard_map/arrange/pallas_call | solution.py:378
  15.8 0.7 %collective-permute-done.6.refs_3_ = bf16[144,128]{1,0:T(8,128)(2,1)S(1)} collective-permute-done((bf16[144,128]{1,0:T(8,128)(2,1)S(1)}, bf16[144,128]{1,0:T(8,128)(2,1)S(1)}, u32[]{:S(2)}, u32[]{:S(2)}) %collective-permute-start.6) | collective-permute-done | bytes 36896 | tf_op jit(solution)/shard_map/ppermute | solution.py:344
  16.6 1.6 %collective-permute-done.5.refs_2_ = bf16[144,128]{1,0:T(8,128)(2,1)S(1)} collective-permute-done((bf16[144,128]{1,0:T(8,128)(2,1)S(1)}, bf16[144,128]{1,0:T(8,128)(2,1)S(1)}, u32[]{:S(2)}, u32[]{:S(2)}) %collective-permute-start.5) | collective-permute-done | bytes 36896 | tf_op jit(solution)/shard_map/ppermute | solution.py:344
  18.1 0.2 %collective-permute-done.4.refs_1_ = bf16[144,128]{1,0:T(8,128)(2,1)S(1)} collective-permute-done((bf16[144,128]{1,0:T(8,128)(2,1)S(1)}, bf16[144,128]{1,0:T(8,128)(2,1)S(1)}, u32[]{:S(2)}, u32[]{:S(2)}) %collective-permute-start.4) | collective-permute-done | bytes 36896 | tf_op jit(solution)/shard_map/ppermute | solution.py:344
  18.4 1.6 %attend.1 = (bf16[4,512]{1,0:T(4,128)(2,1)}, f32[3,4]{1,0:T(4,128)}) custom-call(bf16[144,128]{1,0:T(8,128)(2,1)S(1)} %gather.1.refs_0_, bf16[144,128]{1,0:T(8,128)(2,1)S(1)} %collective-permute-done.4.refs_1_, bf16[144,128]{1,0:T(8,128)(2,1)S(1)} %collective-permute-done.5.refs_2_, bf16[144,128]{1,0:T(8,128)(2,1)S(1)} %collective-permute-done.6.refs_3_, ...), custom_call_target="tpu_custom_call" | custom-call | tf_op jit(solution)/shard_map/attend/pallas_call | solution.py:378
Async XLA Ops:
  1.8 1.4 %collective-permute-start = (bf16[240,128]{1,0:T(8,128)(2,1)S(1)}, bf16[240,128]{1,0:T(8,128)(2,1)S(1)}, u32[]{:S(2)}, u32[]{:S(2)}) collective-permute-start(bf16[240,128]{1,0:T(8,128)(2,1)S(1)} %get-tuple-element.37.mine), channel_id=1, source_target_pairs={{0,4},{1,5},{2,6},{3,7},{4,0},{5,1},{6,2},{7,3},{8,12},{9,13},{10,... | collective-permute-start | bytes 184328 | tf_op jit(solution)/shard_map/ppermute | solution.py:344
  3.3 7.3 %collective-permute-start.1 = (bf16[128,128]{1,0:T(8,128)(2,1)S(1)}, bf16[128,128]{1,0:T(8,128)(2,1)S(1)}, u32[]{:S(2)}, u32[]{:S(2)}) collective-permute-start(bf16[128,128]{1,0:T(8,128)(2,1)S(1)} %get-tuple-element.34), channel_id=1, source_target_pairs={{0,7},{1,6},{2,5},{3,4},{4,3},{5,2},{6,1},{7,0},{8,15},{9,14},{10,... | collective-permute-start | bytes 98312 | tf_op jit(solution)/shard_map/ppermute | solution.py:344
  8.0 3.3 %collective-permute-start.2 = (bf16[128,128]{1,0:T(8,128)(2,1)S(1)}, bf16[128,128]{1,0:T(8,128)(2,1)S(1)}, u32[]{:S(2)}, u32[]{:S(2)}) collective-permute-start(bf16[128,128]{1,0:T(8,128)(2,1)S(1)} %get-tuple-element.35), channel_id=1, source_target_pairs={{0,5},{1,4},{2,7},{3,6},{4,1},{5,0},{6,3},{7,2},{8,13},{9,12},{10,... | collective-permute-start | bytes 98312 | tf_op jit(solution)/shard_map/ppermute | solution.py:344
  8.0 4.2 %collective-permute-start.3 = (bf16[128,128]{1,0:T(8,128)(2,1)S(1)}, bf16[128,128]{1,0:T(8,128)(2,1)S(1)}, u32[]{:S(2)}, u32[]{:S(2)}) collective-permute-start(bf16[128,128]{1,0:T(8,128)(2,1)S(1)} %get-tuple-element.36), channel_id=1, source_target_pairs={{0,6},{1,7},{2,4},{3,5},{4,2},{5,3},{6,0},{7,1},{8,14},{9,15},{10,... | collective-permute-start | bytes 98312 | tf_op jit(solution)/shard_map/ppermute | solution.py:344
  12.3 4.3 %collective-permute-start.6 = (bf16[144,128]{1,0:T(8,128)(2,1)S(1)}, bf16[144,128]{1,0:T(8,128)(2,1)S(1)}, u32[]{:S(2)}, u32[]{:S(2)}) collective-permute-start(bf16[144,128]{1,0:T(8,128)(2,1)S(1)} %gather.1.refs_0_), channel_id=1, source_target_pairs={{0,28},{1,29},{2,30},{3,31},{4,24},{5,25},{6,26},{7,27},{8,20},{9,... | collective-permute-start | bytes 110600 | tf_op jit(solution)/shard_map/ppermute | solution.py:344
  14.7 3.4 %collective-permute-start.5 = (bf16[144,128]{1,0:T(8,128)(2,1)S(1)}, bf16[144,128]{1,0:T(8,128)(2,1)S(1)}, u32[]{:S(2)}, u32[]{:S(2)}) collective-permute-start(bf16[144,128]{1,0:T(8,128)(2,1)S(1)} %gather.1.refs_0_), channel_id=1, source_target_pairs={{0,20},{1,21},{2,22},{3,23},{4,16},{5,17},{6,18},{7,19},{8,28},{9,... | collective-permute-start | bytes 110600 | tf_op jit(solution)/shard_map/ppermute | solution.py:344
  15.0 3.4 %collective-permute-start.4 = (bf16[144,128]{1,0:T(8,128)(2,1)S(1)}, bf16[144,128]{1,0:T(8,128)(2,1)S(1)}, u32[]{:S(2)}, u32[]{:S(2)}) collective-permute-start(bf16[144,128]{1,0:T(8,128)(2,1)S(1)} %gather.1.refs_0_), channel_id=1, source_target_pairs={{0,12},{1,13},{2,14},{3,15},{4,8},{5,9},{6,10},{7,11},{8,4},{9,5},... | collective-permute-start | bytes 110600 | tf_op jit(solution)/shard_map/ppermute | solution.py:344

commit v5 on v4

--- a/solution.py
+++ b/solution.py
@@ -40,7 +40,7 @@
     return (0.5 * x) * (1.0 + jnp.tanh(inner))
 
 
-table_rows = 16
+table_rows, table_used = 16, 11
 
 
 def node_rows(width, own):
@@ -51,8 +51,18 @@
     own, cols, width, heads, keys, kinds = dims
     bias_rows, mask_rows = own * keys * heads // lanes, own * keys // lanes
     first = table_rows + node_rows(width, own) + (cols - 1) * (bias_rows + mask_rows)
-    second = bias_rows + table_rows + 2 * node_rows(width, own) + mask_rows
-    return bias_rows, mask_rows, -(-first // 16) * 16, -(-second // 16) * 16
+    wide_table = -(-(table_used + 2 * mask_rows) // 16) * 16
+    second = 2 * bias_rows + wide_table + 2 * node_rows(width, own)
+    return bias_rows, mask_rows, -(-first // 16) * 16, wide_table, second
+
+
+def paired(steps):
+    return [(steps[n + 1], steps[n]) for n in range(0, len(steps) - 1, 2)] + [(steps[-1], steps[-1])]
+
+
+def sources(transfers):
+    direct = [(odd, even, 1) for even, odd in transfers]
+    return [(0, 0, 0)] + direct + [(even, odd, 0) for even, odd in transfers[:-1]]
 
 
 def in_hbm(x):
@@ -76,9 +86,9 @@
 
 def pack_kernel(dims, *refs):
     own, cols, width, heads, keys, kinds = dims
-    bias_rows, mask_rows, first_rows, second_rows = sizes(dims)
-    sources, first, kept, held, masks, semaphores = refs[:6], refs[6], refs[7], refs[8:14], refs[14], refs[15]
-    copies = fetch(sources, held, semaphores)
+    bias_rows, mask_rows, first_rows, wide_table, second_rows = sizes(dims)
+    first, kept, held, masks, semaphores = refs[6], refs[7], refs[8:14], refs[14], refs[15]
+    copies = fetch(refs[:6], held, semaphores)
     nodes, coords, types, segments, mask, bias = held
     me = lax.axis_index("col")
     pairs, fold = own * keys, lanes // heads
@@ -98,12 +108,12 @@
         for n in range(mask_rows):
             masks[d, n : n + 1, :] = row[:, n * lanes : (n + 1) * lanes]
     start = (cols - 1) * bias_rows
-    tail = filled(blocks + [masks[me ^ k] for k in range(1, cols)], first_rows - start)
+    tail = filled(blocks + [masks[(me + k) % cols] for k in range(1, cols)], first_rows - start)
     first[start:, :] = tail.astype(bf16)
     kept[bias_rows:, :] = filled([masks[me]], kept.shape[0] - bias_rows).astype(bf16)
     copies[5].wait()
     for k in range(cols):
-        tile = bias[pl.ds((me ^ k) * own, own)].astype(f32).reshape(pairs, heads)
+        tile = bias[pl.ds((me + k) % cols * own, own)].astype(f32).reshape(pairs, heads)
         wide = [tile[n * bias_rows : (n + 1) * bias_rows] for n in range(fold)]
         block = jnp.concatenate(wide, axis=1).astype(bf16)
         if k:
@@ -112,77 +122,105 @@
             kept[:bias_rows, :] = block
 
 
-def regroup_kernel(dims, order, mine, other, *outs):
-    own, cols, width, heads, keys, kinds = dims
-    bias_rows, mask_rows, first_rows, second_rows = sizes(dims)
+def regroup_kernel(dims, transfers, mine, other, *outs):
+    own, cols, width, heads, keys, kinds = dims
+    bias_rows, mask_rows, first_rows, wide_table, second_rows = sizes(dims)
+    odd = lax.axis_index("row") % 2 == 1
     start, rows = (cols - 1) * bias_rows, table_rows + node_rows(width, own)
     here, there = mine[start:, :].astype(f32), other[start:, :].astype(f32)
-    table = here[:table_rows] + pltpu.roll(there[:table_rows], own, 1)
-    for n, k in enumerate(order):
-        outs[n][:bias_rows, :] = other[(k - 1) * bias_rows : k * bias_rows, :]
-        at = rows + (k - 1) * mask_rows
-        tail = [table, here[table_rows:rows], there[table_rows:rows], there[at : at + mask_rows]]
-        tail = filled(tail, second_rows - bias_rows)
-        outs[n][bias_rows:, :] = tail.astype(bf16)
-
-
-def gather_kernel(dims, order, mine, other, *refs):
-    own, cols, width, heads, keys, kinds = dims
-    bias_rows, mask_rows, first_rows, second_rows = sizes(dims)
+    table = (here[:table_rows] + pltpu.roll(there[:table_rows], own, 1))[:table_used]
+    nodes = [here[table_rows:rows], there[table_rows:rows]]
+    for out, (for_even, for_odd) in zip(outs, transfers, strict=True):
+
+        def chosen(x, first, count):
+            even_block = x[first + (for_even - 1) * count : first + for_even * count]
+            if for_even == for_odd:
+                return even_block
+            return jnp.where(odd, x[first + (for_odd - 1) * count : first + for_odd * count], even_block)
+
+        for n, ref in enumerate((mine, other)):
+            out[n * bias_rows : (n + 1) * bias_rows, :] = chosen(ref, 0, bias_rows)
+        masks = [chosen(x, rows, mask_rows) for x in (here, there)]
+        tail = filled([table] + masks, wide_table)
+        out[2 * bias_rows :, :] = jnp.concatenate([tail] + nodes, axis=0).astype(bf16)
+
+
+def gather_kernel(dims, mine, other, *refs):
+    own, cols, width, heads, keys, kinds = dims
+    bias_rows, mask_rows, first_rows, wide_table, second_rows = sizes(dims)
     start, rows = (cols - 1) * bias_rows, node_rows(width, own)
     out = refs[cols - 1]
     here, there = mine[start:, :].astype(f32), other[start:, :].astype(f32)
-    tails = [refs[order.index(k)][bias_rows:, :].astype(f32) for k in range(1, cols)]
+    tails = [ref[2 * bias_rows :, :].astype(f32) for ref in refs[: cols - 1]]
     table = here[:table_rows] + pltpu.roll(there[:table_rows], own, 1)
     for k, tail in enumerate(tails, 1):
-        table = table + pltpu.roll(tail[:table_rows], 2 * own * k, 1)
+        part = jnp.where(iota((table_rows, lanes), 0) < table_used, tail[:table_rows], 0.0)
+        table = table + pltpu.roll(part, 2 * own * k, 1)
     out[:table_rows, :] = table.astype(bf16)
     blocks = [here[table_rows:], there[table_rows:]]
     for tail in tails:
-        blocks += [tail[table_rows : table_rows + rows], tail[table_rows + rows :]]
+        blocks += [tail[wide_table : wide_table + rows], tail[wide_table + rows :]]
     each = 2 * own * cols
     for b in range(width // lanes):
         taken = jnp.concatenate([block[b * own : (b + 1) * own] for block in blocks], axis=0)
         out[table_rows + b * each : table_rows + (b + 1) * each, :] = taken.astype(bf16)
 
 
-def arrange_kernel(dims, order, steps, kept, *refs):
-    own, cols, width, heads, keys, kinds = dims
-    bias_rows, mask_rows, first_rows, second_rows = sizes(dims)
-    received = [refs[order.index(k)] for k in range(1, cols)]
-    spread_queries, w_qkv, out, keyed = refs[cols - 1 :]
-    through_keys = lax.dot_general(
-        spread_queries[...], w_qkv[:, width : 2 * width], nt, preferred_element_type=f32
-    )
-    keyed[...] = (through_keys * (1.0 / math.sqrt(width // heads))).astype(bf16)
+def normed(x, gain):
+    features = x.astype(f32)
+    centred = features - jnp.mean(features, axis=1, keepdims=True)
+    spread = jnp.mean(centred * centred, axis=1, keepdims=True)
+    return (centred * lax.rsqrt(spread + ln_epsilon) * gain).astype(bf16)
+
+
+def arrange_kernel(dims, column_parts, row_parts, mine, kept, *refs):
+    own, cols, width, heads, keys, kinds = dims
+    bias_rows, mask_rows, first_rows, wide_table, second_rows = sizes(dims)
+    received = refs[: cols - 1]
+    ln_gain, w_source, out, keyed, w_qkv, semaphores = refs[cols - 1 :]
+    copies = fetch((w_source,), (w_qkv,), semaphores)
     atoms = out.shape[1]
     fold = lanes // heads
     each = own // fold
-    mask_at = table_rows + 2 * node_rows(width, own)
     per_row = 2 * own * cols
     r, c = lax.axis_index("row"), lax.axis_index("col")
-    blocks = [
-        jnp.concatenate([ref[b * keys : (b + 1) * keys, :] for ref in [kept] + received], axis=0)
-        for b in range(each)
-    ]
+
+    def by_core(odd, part):
+        return jnp.where(odd, part[1], part[0])
+
+    blocks, masks = [], []
+    for b in range(each):
+        rows = [kept[b * keys : (b + 1) * keys, :]]
+        for ref, part in zip(received, column_parts[1:], strict=True):
+            first = part[2] * bias_rows + b * keys
+            rows.append(ref[first : first + keys, :])
+        blocks.append(jnp.concatenate(rows, axis=0))
     tails = [kept[bias_rows:, :].astype(f32)[:mask_rows]]
-    tails += [ref[bias_rows:, :].astype(f32)[mask_at : mask_at + mask_rows] for ref in received]
-    masks = []
+    for ref, part in zip(received, column_parts[1:], strict=True):
+        first = table_used + part[2] * mask_rows
+        tails.append(ref[2 * bias_rows : 2 * bias_rows + wide_table, :].astype(f32)[first : first + mask_rows])
     for i in range(own):
         n, lane = i * keys // lanes, i * keys % lanes
         masks.append(jnp.concatenate([tail[n : n + 1, lane : lane + keys] for tail in tails], axis=1))
     masks = jnp.concatenate(masks + [jnp.zeros((16 - own, atoms), f32)], axis=0).astype(bf16)
     place = iota((atoms, 1), 0)
-    atom = (c ^ (place // keys)) * keys + place % keys
+    step = jnp.zeros((atoms, 1), jnp.int32)
+    for n, part in enumerate(column_parts):
+        step = jnp.where(place // keys == n, by_core(r % 2 == 1, part), step)
+    atom = (c + cols - step) % cols * keys + place % keys
     for s in range(0, atoms, lanes):
         slot = s + iota((1, lanes), 1)
         piece, inner = slot // per_row, slot % per_row
-        step = jnp.zeros((1, lanes), jnp.int32)
-        for n, value in enumerate(steps):
-            step = jnp.where(piece == n, value, step)
-        distance = inner // (2 * own)
-        row = r ^ step ^ (inner // own % 2) ^ (distance > 0).astype(jnp.int32)
-        source = (row * cols + (c ^ distance)) * own + inner % own
+        row = jnp.zeros((1, lanes), jnp.int32) + r
+        for n, part in enumerate(row_parts):
+            row = jnp.where(piece == n, r ^ by_core(r % 2 == 1, part), row)
+        step, flip = jnp.zeros((1, lanes), jnp.int32), jnp.zeros((1, lanes), jnp.int32)
+        for n, part in enumerate(column_parts):
+            here = inner // (2 * own) == n
+            step = jnp.where(here, by_core(row % 2 == 1, part), step)
+            flip = jnp.where(here, part[2], flip)
+        row = row ^ flip ^ (inner // own % 2)
+        source = (row * cols + (c + cols - step) % cols) * own + inner % own
         chosen = (atom == source).astype(f32).astype(bf16)
         valid = jnp.dot(masks, chosen, preferred_element_type=f32)
         for b in range(each):
@@ -191,31 +229,36 @@
                 i = a * each + b
                 taken = jnp.where(valid[i : i + 1] > 0.5, moved[a * heads : (a + 1) * heads], masked_fill)
                 out[i * heads : (i + 1) * heads, s : s + lanes] = taken.astype(bf16)
-
-
-def normed(x, gain):
-    features = x.astype(f32)
-    centred = features - jnp.mean(features, axis=1, keepdims=True)
-    spread = jnp.mean(centred * centred, axis=1, keepdims=True)
-    return (centred * lax.rsqrt(spread + ln_epsilon) * gain).astype(bf16)
+    rows = mine[(cols - 1) * bias_rows :, :].astype(f32)[table_rows : table_rows + node_rows(width, own)]
+    x = jnp.concatenate([rows[b * own : (b + 1) * own] for b in range(width // lanes)], axis=1)
+    x = normed(jnp.concatenate([x, jnp.zeros((16 - own, width), f32)], axis=0), ln_gain[...])
+    copies[0].wait()
+    queries = jnp.dot(x, w_qkv[:, :width], preferred_element_type=f32)
+    head_mask = iota((heads, width), 1) // (width // heads) == iota((heads, width), 0)
+    spread = [
+        jnp.where(head_mask, jnp.broadcast_to(queries[i : i + 1], (heads, width)), 0.0)
+        for i in range(own)
+    ]
+    spread = jnp.concatenate(spread, axis=0).astype(bf16)
+    through_keys = lax.dot_general(
+        spread, w_qkv[:, width : 2 * width], nt, preferred_element_type=f32
+    )
+    keyed[...] = (through_keys * (1.0 / math.sqrt(width // heads))).astype(bf16)
 
 
 def prepare_kernel(dims, mine, *refs):
     own, cols, width, heads, keys, kinds = dims
-    bias_rows, mask_rows, first_rows, second_rows = sizes(dims)
-    sources = refs[:11]
-    w_qkv, w_heads, ln_gain, coords, w_gauss, w_coord1, w_coord2, spread_queries = refs[11:19]
-    lookup, own_columns, kernels = refs[19:22]
-    mul_held, add_held, mean_held, width_held, gauss_held, coord1_held, coord2_held = refs[22:29]
-    semaphores = refs[29]
+    bias_rows, mask_rows, first_rows, wide_table, second_rows = sizes(dims)
+    w_heads, ln_gain, coords, w_gauss, w_coord1, w_coord2 = refs[10:16]
+    lookup, own_columns, kernels = refs[16:19]
+    mul_held, add_held, mean_held, width_held, gauss_held, coord1_held, coord2_held = refs[19:26]
     copies = fetch(
-        sources,
-        (w_qkv, w_heads, ln_gain, coords, mul_held, add_held, mean_held, width_held)
+        refs[:10],
+        (w_heads, ln_gain, coords, mul_held, add_held, mean_held, width_held)
         + (gauss_held, coord1_held, coord2_held),
-        semaphores,
-    )
-    tail = mine[(cols - 1) * bias_rows :, :].astype(f32)
-    table, rows = tail[:table_rows], tail[table_rows : table_rows + node_rows(width, own)]
+        refs[26],
+    )
+    table = mine[(cols - 1) * bias_rows :, :].astype(f32)[:table_rows]
     places = (table[0:3] + table[8:11]) + table[4:7]
     for c in range(3):
         own_columns[c * 8 : c * 8 + own, :] = jnp.broadcast_to(
@@ -224,7 +267,7 @@
     own_kind = column(table[3:4, :own]).astype(jnp.int32)
     own_kind = jnp.concatenate([own_kind, jnp.zeros((16 - own, 1), jnp.int32)], axis=0)
     query_onehot = (own_kind == iota((16, kinds), 1)).astype(f32).astype(bf16)
-    for copy in copies[4:]:
+    for copy in copies:
         copy.wait()
     inverse = 1.0 / column(width_held[...])
     gauss = inverse.shape[0]
@@ -243,15 +286,6 @@
     w_gauss[...] = gauss_held[...].astype(f32).T.astype(bf16)
     w_coord1[...] = coord1_held[...].astype(f32).T.astype(bf16)
     w_coord2[...] = jnp.broadcast_to(column(coord2_held[...].astype(f32)), (heads, lanes))
-    for copy in copies[:4]:
-        copy.wait()
-    x = jnp.concatenate([rows[b * own : (b + 1) * own] for b in range(width // lanes)], axis=1)
-    x = jnp.concatenate([x, jnp.zeros((16 - own, width), f32)], axis=0)
-    queries = jnp.dot(normed(x, ln_gain[...]), w_qkv[:, :width], preferred_element_type=f32)
-    head_mask = iota((heads, width), 1) // (width // heads) == iota((heads, width), 0)
-    for i in range(own):
-        spread = jnp.where(head_mask, jnp.broadcast_to(queries[i : i + 1], (heads, width)), 0.0)
-        spread_queries[i * heads : (i + 1) * heads, :] = spread.astype(bf16)
 
 
 def attend_kernel(dims, count, *refs):
@@ -336,10 +370,12 @@
     moved[...] = here + shift * (1.0 / atoms)
 
 
-def exchange(x, step, distance):
+def exchange(x, steps, distances):
     rows, cols = lax.axis_size("row"), lax.axis_size("col")
     pairs = [
-        (r * cols + c, (r ^ step) * cols + (c ^ distance)) for r in range(rows) for c in range(cols)
+        (r * cols + c, (r ^ steps[r % 2]) * cols + (c + distances[r % 2]) % cols)
+        for r in range(rows)
+        for c in range(cols)
     ]
     return lax.ppermute(x, ("row", "col"), pairs)
 
@@ -368,7 +404,12 @@
     kinds, gauss = gauss_mul.shape[0], gauss_mean.shape[0]
     atoms = own * rows * cols
     dims = (own, cols, width, heads, keys, kinds)
-    bias_rows, mask_rows, first_rows, second_rows = sizes(dims)
+    bias_rows, mask_rows, first_rows, wide_table, second_rows = sizes(dims)
+    near_step, still = (1, 1), (0, 0)
+    along_col = paired(list(range(1, cols)))
+    along_row = [(even, odd) for odd, even in paired(list(range(3, rows, 2)))]
+    column_parts, row_parts = sources(along_col), sources(along_row)
+    row_parts = [(even ^ (1 - other), odd ^ (1 - other), other) if n else (0, 0, 0) for n, (even, odd, other) in enumerate(row_parts)]
     shape = jax.ShapeDtypeStruct
     params = pltpu.CompilerParams(vmem_limit_bytes=(16 if atoms <= 128 else 56) * 2**20)
     vmem, anywhere = pl.BlockSpec(memory_space=pltpu.VMEM), pl.BlockSpec(memory_space=pl.ANY)
@@ -385,7 +426,7 @@
             name=name,
         )(*inputs, *map(in_hbm, remote))
 
-    sources = (
+    own_arrays = (
         nodes,
         coords,
         atom_types[None, :],
@@ -401,55 +442,59 @@
             shape((-(-(bias_rows + mask_rows) // 16) * 16, lanes), bf16),
         ],
         (),
-        sources,
-        [pltpu.VMEM(x.shape, x.dtype) for x in sources]
+        own_arrays,
+        [pltpu.VMEM(x.shape, x.dtype) for x in own_arrays]
         + [pltpu.VMEM((cols, mask_rows, lanes), f32), pltpu.SemaphoreType.DMA((6,))],
     )
-    order = (cols - 1, *range(1, cols - 1))
-    other = exchange(mine, 1, 0)
+    other = exchange(mine, near_step, still)
     grouped = call(
-        functools.partial(regroup_kernel, dims, order),
+        functools.partial(regroup_kernel, dims, along_col),
         "regroup",
-        [shape((second_rows, lanes), bf16)] * (cols - 1),
+        [shape((second_rows, lanes), bf16)] * len(along_col),
         (mine, other),
     )
-    received = [exchange(x, 1, k) for x, k in zip(grouped, order, strict=True)]
-    near = call(
-        functools.partial(gather_kernel, dims, order),
-        "gather",
-        shape((table_rows + 2 * node_rows(width, own) * cols, lanes), bf16),
-        (mine, other, *received),
-    )
-    weights = (w_qkv, w_heads.T, ln_gain[None, :], coords)
+    received = [exchange(x, near_step, shift) for x, shift in zip(grouped, along_col, strict=True)]
+    small = (w_heads.T, ln_gain[None, :], coords)
     tables = (gauss_mul, gauss_add, gauss_mean[None, :], gauss_width[None, :], w_gauss, w_coord1)
     tables += (w_coord2[None, :],)
     prepared = call(
         functools.partial(prepare_kernel, dims),
         "prepare",
-        [shape(x.shape, x.dtype) for x in weights]
+        [shape(x.shape, x.dtype) for x in small]
         + [
             shape((gauss, gauss), bf16),
             shape(w_coord1.shape, bf16),
             shape((heads, lanes), f32),
-            shape((own * heads, width), bf16),
             shape((2 * own, lanes), f32),
             shape((24, lanes), f32),
             shape((3, gauss, lanes), f32),
         ],
-        (lax.optimization_barrier((mine, other))[0],),
-        weights + tables,
-        [pltpu.VMEM(x.shape, x.dtype) for x in tables] + [pltpu.SemaphoreType.DMA((11,))],
-    )
-    near, prepared = lax.optimization_barrier((near, prepared))
-    w_qkv, w_heads, ln_gain, coords, w_gauss, w_coord1, w_coord2, spread_queries = prepared[:8]
-    lookup, own_columns, kernels = prepared[8:]
-    steps = [0] + [step + 1 for step in range(2, rows, 2)]
-    pieces = [near] + [exchange(near, step, 0) for step in steps[1:]]
-    bias, keyed = call(
-        functools.partial(arrange_kernel, dims, order, steps),
+        (lax.optimization_barrier((mine, grouped[0]))[0],),
+        small + tables,
+        [pltpu.VMEM(x.shape, x.dtype) for x in tables] + [pltpu.SemaphoreType.DMA((10,))],
+    )
+    received[0], prepared = lax.optimization_barrier((received[0], prepared))
+    received += [exchange(x, near_step, still) for x in received[:-1]]
+    w_heads, ln_gain, coords, w_gauss, w_coord1, w_coord2, lookup, own_columns, kernels = prepared
+    near = call(
+        functools.partial(gather_kernel, dims),
+        "gather",
+        shape((table_rows + 2 * node_rows(width, own) * cols, lanes), bf16),
+        (mine, other, *received),
+    )
+    pieces = [near] + [exchange(near, step, still) for step in along_row]
+    pieces += [exchange(x, near_step, still) for x in pieces[1 : len(along_row)]]
+    bias, keyed, w_qkv = call(
+        functools.partial(arrange_kernel, dims, column_parts, row_parts),
         "arrange",
-        [shape((own * heads, atoms), bf16), shape((own * heads, width), bf16)],
-        (kept, *received, spread_queries, w_qkv),
+        [
+            shape((own * heads, atoms), bf16),
+            shape((own * heads, width), bf16),
+            shape(w_qkv.shape, bf16),
+        ],
+        (lax.optimization_barrier((mine, pieces[1]))[0], kept, *received, ln_gain),
+        (w_qkv,),
+        [pltpu.SemaphoreType.DMA((1,))],
     )
     attended, moved = call(
         functools.partial(attend_kernel, dims, len(pieces)),

time: 20.2 us -> 18.8 us (0.931)
  waiting for transfers between devices: 5.07 us -> 3.46 us
  Pallas kernels: 5.22 us -> 5.93 us
  starting transfers between devices: 9.01 us -> 8.41 us
    ppermute x7, waiting for transfers between devices: 5.07 us -> 3.46 us  [exchange(): return lax.ppermute(x, ('row', 'col'), pairs)]
    pallas_call x6, Pallas kernels: 5.22 us -> 5.93 us  [call(): pl.pallas_call(kernel, out_shape=out_shape, in_specs=[vmem] * len(inputs)...]
    ppermute x7, starting transfers between devices: 9.01 us -> 8.41 us  [exchange(): return lax.ppermute(x, ('row', 'col'), pairs)]
  transfers between devices with their start and end apart: 7 -> 7, of which waited for: 6 -> 6; matrix products, arithmetic and copies ran while one was open for 0% -> 0% of each run, Pallas kernels for 12% -> 16%
where the time goes in v5:
time: 18.8 us; the launch traced here: 18.5 us
  starting transfers between devices  8.41 us (45%)
  Pallas kernels  5.93 us (32%)
  waiting for transfers between devices  3.46 us (18%)
  between operations  0.66 us (4%)
    ppermute x7, starting transfers between devices, exchange(): return lax.ppermute(x, ('row', 'col'), pairs)  8.41 us
    pallas_call x6, Pallas kernels, call(): pl.pallas_call(kernel, out_shape=out_shape, in_specs=[vmem] * len(inputs)...  5.93 us
    ppermute x7, waiting for transfers between devices, exchange(): return lax.ppermute(x, ('row', 'col'), pairs)  3.46 us
  transfers between devices with their start and end apart: 7, of which 6 were waited for; matrix products, arithmetic and copies ran while one was open for 0% of the time, Pallas kernels for 16%

profile of v5, /device:TPU:0, one launch (start us, length us, event | category | flops | bytes accessed | tf_op | source)
XLA Modules:
  0.0 18.5 jit_solution(8394116897369656732)
XLA Ops:
  0.6 1.1 %pack.1 = (bf16[240,128]{1,0:T(8,128)(2,1)S(1)}, bf16[80,128]{1,0:T(8,128)(2,1)S(1)}) custom-call(bf16[4,512]{1,0:T(4,128)(2,1)} %refs_0_.1, f32[3,4]{1,0:T(4,128)} %refs_2_.1, s32[1,4]{1,0:T(1,128)} %bitcast.11, s32[1,4]{1,0:T(1,128)} %bitcast.12, s32[16,32]{1,0:T(8,128)} %refs_4_.3, bf16[16,32,64]{2,1,0:T(8,128)(2,1)} %bitcast.8), custom_call_target="tpu_custom_call" | custom-call | tf_op jit(solution)/shard_map/pack/pallas_call | solution.py:419
  1.8 0.5 %collective-permute-start = (bf16[240,128]{1,0:T(8,128)(2,1)S(1)}, bf16[240,128]{1,0:T(8,128)(2,1)S(1)}, u32[]{:S(2)}, u32[]{:S(2)}) collective-permute-start(bf16[240,128]{1,0:T(8,128)(2,1)S(1)} %get-tuple-element.44.mine), channel_id=1, source_target_pairs={{0,4},{1,5},{2,6},{3,7},{4,0},{5,1},{6,2},{7,3},{8,12},{9,13},{10,... | collective-permute-start | bytes 184328 | tf_op jit(solution)/shard_map/ppermute | solution.py:380
  2.3 0.9 %collective-permute-done.other = bf16[240,128]{1,0:T(8,128)(2,1)S(1)} collective-permute-done((bf16[240,128]{1,0:T(8,128)(2,1)S(1)}, bf16[240,128]{1,0:T(8,128)(2,1)S(1)}, u32[]{:S(2)}, u32[]{:S(2)}) %collective-permute-start) | collective-permute-done | bytes 61472 | tf_op jit(solution)/shard_map/ppermute | solution.py:380
  3.2 0.1 regroup.1
  3.3 3.7 %collective-permute-start.1 = (bf16[176,128]{1,0:T(8,128)(2,1)S(1)}, bf16[176,128]{1,0:T(8,128)(2,1)S(1)}, u32[]{:S(2)}, u32[]{:S(2)}) collective-permute-start(bf16[176,128]{1,0:T(8,128)(2,1)S(1)} %get-tuple-element.31), channel_id=1, source_target_pairs={{0,6},{1,7},{2,4},{3,5},{4,1},{5,2},{6,3},{7,0},{8,14},{9,15},{10,... | collective-permute-start | bytes 135176 | tf_op jit(solution)/shard_map/ppermute | solution.py:380
  7.0 1.1 %collective-permute-start.2 = (bf16[176,128]{1,0:T(8,128)(2,1)S(1)}, bf16[176,128]{1,0:T(8,128)(2,1)S(1)}, u32[]{:S(2)}, u32[]{:S(2)}) collective-permute-start(bf16[176,128]{1,0:T(8,128)(2,1)S(1)} %get-tuple-element.43), channel_id=1, source_target_pairs={{0,7},{1,4},{2,5},{3,6},{4,3},{5,0},{6,1},{7,2},{8,15},{9,12},{10,... | collective-permute-start | bytes 135176 | tf_op jit(solution)/shard_map/ppermute | solution.py:380
  8.0 1.1 %prepare.1 = (bf16[64,128]{1,0:T(8,128)(2,1)S(1)}, f32[1,512]{1,0:T(1,128)S(1)}, f32[3,4]{1,0:T(4,128)S(1)}, bf16[128,128]{1,0:T(8,128)(2,1)S(1)}, bf16[64,64]{1...) custom-call(bf16[240,128]{1,0:T(8,128)(2,1)S(1)} %get-tuple-element., ...), custom_call_target="tpu_custom_call" | custom-call | tf_op jit(solution)/shard_map/prepare/pallas_call | solution.py:419
  9.2 0.5 %collective-permute-done.1.refs_0_ = bf16[176,128]{1,0:T(8,128)(2,1)S(1)} collective-permute-done((bf16[176,128]{1,0:T(8,128)(2,1)S(1)}, bf16[176,128]{1,0:T(8,128)(2,1)S(1)}, u32[]{:S(2)}, u32[]{:S(2)}) %collective-permute-start.1) | collective-permute-done | bytes 45088 | tf_op jit(solution)/shard_map/ppermute | solution.py:380
  9.7 0.0 collective-permute-start.3
  9.7 1.1 %collective-permute-done.2.refs_1_ = bf16[176,128]{1,0:T(8,128)(2,1)S(1)} collective-permute-done((bf16[176,128]{1,0:T(8,128)(2,1)S(1)}, bf16[176,128]{1,0:T(8,128)(2,1)S(1)}, u32[]{:S(2)}, u32[]{:S(2)}) %collective-permute-start.2) | collective-permute-done | bytes 45088 | tf_op jit(solution)/shard_map/ppermute | solution.py:380
  10.8 0.1 collective-permute-done.3.refs_2_
  10.9 0.1 gather.1.refs_0_
  11.0 1.5 %collective-permute-start.4 = (bf16[144,128]{1,0:T(8,128)(2,1)S(1)}, bf16[144,128]{1,0:T(8,128)(2,1)S(1)}, u32[]{:S(2)}, u32[]{:S(2)}) collective-permute-start(bf16[144,128]{1,0:T(8,128)(2,1)S(1)} %gather.1.refs_0_), channel_id=1, source_target_pairs={{0,12},{1,13},{2,14},{3,15},{4,16},{5,17},{6,18},{7,19},{8,4},{9,5... | collective-permute-start | bytes 110600 | tf_op jit(solution)/shard_map/ppermute | solution.py:380
  12.5 1.4 %collective-permute-start.5 = (bf16[144,128]{1,0:T(8,128)(2,1)S(1)}, bf16[144,128]{1,0:T(8,128)(2,1)S(1)}, u32[]{:S(2)}, u32[]{:S(2)}) collective-permute-start(bf16[144,128]{1,0:T(8,128)(2,1)S(1)} %gather.1.refs_0_), channel_id=1, source_target_pairs={{0,28},{1,29},{2,30},{3,31},{4,24},{5,25},{6,26},{7,27},{8,20},{9,... | collective-permute-start | bytes 110600 | tf_op jit(solution)/shard_map/ppermute | solution.py:380
  14.0 0.4 %collective-permute-done.4.refs_1_ = bf16[144,128]{1,0:T(8,128)(2,1)S(1)} collective-permute-done((bf16[144,128]{1,0:T(8,128)(2,1)S(1)}, bf16[144,128]{1,0:T(8,128)(2,1)S(1)}, u32[]{:S(2)}, u32[]{:S(2)}) %collective-permute-start.4) | collective-permute-done | bytes 36896 | tf_op jit(solution)/shard_map/ppermute | solution.py:380
  14.4 0.2 collective-permute-start.6
  14.6 1.9 %arrange.1 = (bf16[256,128]{1,0:T(8,128)(2,1)S(1)}, bf16[256,512]{1,0:T(8,128)(2,1)S(1)}, bf16[512,1536]{1,0:T(8,128)(2,1)S(1)}) custom-call(bf16[240,128]{1,0:T(8,128)(2,1)S(1)} %get-tuple-element.44.mine, bf16[80,128]{1,0:T(8,128)(2,1)S(1)} %get-tuple-element.45.kept, bf16[176,128]{1,0:T(8,128)(2,1)S(1)} %collective-permute-done.1.refs_0_, ...), custom_call_target="tpu_custom_call" | custom-call | tf_op jit(solution)/shard_map/arrange/pallas_call | solution.py:419
  16.5 0.4 %collective-permute-done.5.refs_2_ = bf16[144,128]{1,0:T(8,128)(2,1)S(1)} collective-permute-done((bf16[144,128]{1,0:T(8,128)(2,1)S(1)}, bf16[144,128]{1,0:T(8,128)(2,1)S(1)}, u32[]{:S(2)}, u32[]{:S(2)}) %collective-permute-start.5) | collective-permute-done | bytes 36896 | tf_op jit(solution)/shard_map/ppermute | solution.py:380
  16.8 0.0 collective-permute-done.6.refs_3_
  16.9 1.6 %attend.1 = (bf16[4,512]{1,0:T(4,128)(2,1)}, f32[3,4]{1,0:T(4,128)}) custom-call(bf16[144,128]{1,0:T(8,128)(2,1)S(1)} %gather.1.refs_0_, bf16[144,128]{1,0:T(8,128)(2,1)S(1)} %collective-permute-done.4.refs_1_, bf16[144,128]{1,0:T(8,128)(2,1)S(1)} %collective-permute-done.5.refs_2_, bf16[144,128]{1,0:T(8,128)(2,1)S(1)} %collective-permute-done.6.refs_3_, ...), custom_call_target="tpu_custom_call" | custom-call | tf_op jit(solution)/shard_map/attend/pallas_call | solution.py:419
Async XLA Ops:
  1.8 1.4 %collective-permute-start = (bf16[240,128]{1,0:T(8,128)(2,1)S(1)}, bf16[240,128]{1,0:T(8,128)(2,1)S(1)}, u32[]{:S(2)}, u32[]{:S(2)}) collective-permute-start(bf16[240,128]{1,0:T(8,128)(2,1)S(1)} %get-tuple-element.44.mine), channel_id=1, source_target_pairs={{0,4},{1,5},{2,6},{3,7},{4,0},{5,1},{6,2},{7,3},{8,12},{9,13},{10,... | collective-permute-start | bytes 184328 | tf_op jit(solution)/shard_map/ppermute | solution.py:380
  3.3 6.5 %collective-permute-start.1 = (bf16[176,128]{1,0:T(8,128)(2,1)S(1)}, bf16[176,128]{1,0:T(8,128)(2,1)S(1)}, u32[]{:S(2)}, u32[]{:S(2)}) collective-permute-start(bf16[176,128]{1,0:T(8,128)(2,1)S(1)} %get-tuple-element.31), channel_id=1, source_target_pairs={{0,6},{1,7},{2,4},{3,5},{4,1},{5,2},{6,3},{7,0},{8,14},{9,15},{10,... | collective-permute-start | bytes 135176 | tf_op jit(solution)/shard_map/ppermute | solution.py:380
  7.0 3.8 %collective-permute-start.2 = (bf16[176,128]{1,0:T(8,128)(2,1)S(1)}, bf16[176,128]{1,0:T(8,128)(2,1)S(1)}, u32[]{:S(2)}, u32[]{:S(2)}) collective-permute-start(bf16[176,128]{1,0:T(8,128)(2,1)S(1)} %get-tuple-element.43), channel_id=1, source_target_pairs={{0,7},{1,4},{2,5},{3,6},{4,3},{5,0},{6,1},{7,2},{8,15},{9,12},{10,... | collective-permute-start | bytes 135176 | tf_op jit(solution)/shard_map/ppermute | solution.py:380
  9.7 1.2 %collective-permute-start.3 = (bf16[176,128]{1,0:T(8,128)(2,1)S(1)}, bf16[176,128]{1,0:T(8,128)(2,1)S(1)}, u32[]{:S(2)}, u32[]{:S(2)}) collective-permute-start(bf16[176,128]{1,0:T(8,128)(2,1)S(1)} %collective-permute-done.1.refs_0_), channel_id=1, source_target_pairs={{0,4},{1,5},{2,6},{3,7},{4,0},{5,1},{6,2},{7,3},{8,12},{9,13},{10,... | collective-permute-start | bytes 135176 | tf_op jit(solution)/shard_map/ppermute | solution.py:380
  11.0 3.4 %collective-permute-start.4 = (bf16[144,128]{1,0:T(8,128)(2,1)S(1)}, bf16[144,128]{1,0:T(8,128)(2,1)S(1)}, u32[]{:S(2)}, u32[]{:S(2)}) collective-permute-start(bf16[144,128]{1,0:T(8,128)(2,1)S(1)} %gather.1.refs_0_), channel_id=1, source_target_pairs={{0,12},{1,13},{2,14},{3,15},{4,16},{5,17},{6,18},{7,19},{8,4},{9,5... | collective-permute-start | bytes 110600 | tf_op jit(solution)/shard_map/ppermute | solution.py:380
  12.5 4.3 %collective-permute-start.5 = (bf16[144,128]{1,0:T(8,128)(2,1)S(1)}, bf16[144,128]{1,0:T(8,128)(2,1)S(1)}, u32[]{:S(2)}, u32[]{:S(2)}) collective-permute-start(bf16[144,128]{1,0:T(8,128)(2,1)S(1)} %gather.1.refs_0_), channel_id=1, source_target_pairs={{0,28},{1,29},{2,30},{3,31},{4,24},{5,25},{6,26},{7,27},{8,20},{9,... | collective-permute-start | bytes 110600 | tf_op jit(solution)/shard_map/ppermute | solution.py:380
  14.4 2.5 %collective-permute-start.6 = (bf16[144,128]{1,0:T(8,128)(2,1)S(1)}, bf16[144,128]{1,0:T(8,128)(2,1)S(1)}, u32[]{:S(2)}, u32[]{:S(2)}) collective-permute-start(bf16[144,128]{1,0:T(8,128)(2,1)S(1)} %collective-permute-done.4.refs_1_), channel_id=1, source_target_pairs={{0,4},{1,5},{2,6},{3,7},{4,0},{5,1},{6,2},{7,3},{8,12},{9,13},{10,... | collective-permute-start | bytes 110600 | tf_op jit(solution)/shard_map/ppermute | solution.py:380

commit v6 on v5

--- a/solution.py
+++ b/solution.py
@@ -84,24 +84,31 @@
     return jnp.concatenate(blocks + ([jnp.zeros((rest, lanes), f32)] if rest else []), axis=0)
 
 
+def normed(x, gain):
+    features = x.astype(f32)
+    centred = features - jnp.mean(features, axis=1, keepdims=True)
+    spread = jnp.mean(centred * centred, axis=1, keepdims=True)
+    return (centred * lax.rsqrt(spread + ln_epsilon) * gain).astype(bf16)
+
+
 def pack_kernel(dims, *refs):
     own, cols, width, heads, keys, kinds = dims
     bias_rows, mask_rows, first_rows, wide_table, second_rows = sizes(dims)
-    first, kept, held, masks, semaphores = refs[6], refs[7], refs[8:14], refs[14], refs[15]
-    copies = fetch(refs[:6], held, semaphores)
-    nodes, coords, types, segments, mask, bias = held
+    first, kept, held, masks, semaphores = refs[7], refs[8], refs[9:16], refs[16], refs[17]
+    copies = fetch(refs[:7], held, semaphores)
+    nodes, coords, types, segments, ln_gain, mask, bias = held
     me = lax.axis_index("col")
     pairs, fold = own * keys, lanes // heads
-    for copy in copies[:4]:
+    for copy in copies[:5]:
         copy.wait()
     high, middle, low = split3(coords[...])
     kind = (types[...] + kinds // 2 * segments[...]).astype(f32)
     blank = jnp.zeros((1, own), f32)
     table = jnp.concatenate([high, kind, low, blank, middle] + [blank] * 5, axis=0)
     table = jnp.concatenate([table, jnp.zeros((table_rows, lanes - own), f32)], axis=1)
-    full = nodes[...].astype(f32)
+    full = normed(nodes[...], ln_gain[...]).astype(f32)
     blocks = [table] + [full[:, b * lanes : (b + 1) * lanes] for b in range(width // lanes)]
-    copies[4].wait()
+    copies[5].wait()
     wide_mask = mask[...].astype(f32)
     for d in range(cols):
         row = jnp.concatenate([wide_mask[d * own + i : d * own + i + 1] for i in range(own)], axis=1)
@@ -111,7 +118,7 @@
     tail = filled(blocks + [masks[(me + k) % cols] for k in range(1, cols)], first_rows - start)
     first[start:, :] = tail.astype(bf16)
     kept[bias_rows:, :] = filled([masks[me]], kept.shape[0] - bias_rows).astype(bf16)
-    copies[5].wait()
+    copies[6].wait()
     for k in range(cols):
         tile = bias[pl.ds((me + k) % cols * own, own)].astype(f32).reshape(pairs, heads)
         wide = [tile[n * bias_rows : (n + 1) * bias_rows] for n in range(fold)]
@@ -166,18 +173,11 @@
         out[table_rows + b * each : table_rows + (b + 1) * each, :] = taken.astype(bf16)
 
 
-def normed(x, gain):
-    features = x.astype(f32)
-    centred = features - jnp.mean(features, axis=1, keepdims=True)
-    spread = jnp.mean(centred * centred, axis=1, keepdims=True)
-    return (centred * lax.rsqrt(spread + ln_epsilon) * gain).astype(bf16)
-
-
 def arrange_kernel(dims, column_parts, row_parts, mine, kept, *refs):
     own, cols, width, heads, keys, kinds = dims
     bias_rows, mask_rows, first_rows, wide_table, second_rows = sizes(dims)
     received = refs[: cols - 1]
-    ln_gain, w_source, out, keyed, w_qkv, semaphores = refs[cols - 1 :]
+    w_source, out, spread_queries, w_qkv, semaphores = refs[cols - 1 :]
     copies = fetch((w_source,), (w_qkv,), semaphores)
     atoms = out.shape[1]
     fold = lanes // heads
@@ -231,32 +231,26 @@
                 out[i * heads : (i + 1) * heads, s : s + lanes] = taken.astype(bf16)
     rows = mine[(cols - 1) * bias_rows :, :].astype(f32)[table_rows : table_rows + node_rows(width, own)]
     x = jnp.concatenate([rows[b * own : (b + 1) * own] for b in range(width // lanes)], axis=1)
-    x = normed(jnp.concatenate([x, jnp.zeros((16 - own, width), f32)], axis=0), ln_gain[...])
+    x = jnp.concatenate([x, jnp.zeros((16 - own, width), f32)], axis=0).astype(bf16)
     copies[0].wait()
     queries = jnp.dot(x, w_qkv[:, :width], preferred_element_type=f32)
     head_mask = iota((heads, width), 1) // (width // heads) == iota((heads, width), 0)
-    spread = [
-        jnp.where(head_mask, jnp.broadcast_to(queries[i : i + 1], (heads, width)), 0.0)
-        for i in range(own)
-    ]
-    spread = jnp.concatenate(spread, axis=0).astype(bf16)
-    through_keys = lax.dot_general(
-        spread, w_qkv[:, width : 2 * width], nt, preferred_element_type=f32
-    )
-    keyed[...] = (through_keys * (1.0 / math.sqrt(width // heads))).astype(bf16)
+    for i in range(own):
+        spread = jnp.where(head_mask, jnp.broadcast_to(queries[i : i + 1], (heads, width)), 0.0)
+        spread_queries[i * heads : (i + 1) * heads, :] = spread.astype(bf16)
 
 
 def prepare_kernel(dims, mine, *refs):
     own, cols, width, heads, keys, kinds = dims
     bias_rows, mask_rows, first_rows, wide_table, second_rows = sizes(dims)
-    w_heads, ln_gain, coords, w_gauss, w_coord1, w_coord2 = refs[10:16]
-    lookup, own_columns, kernels = refs[16:19]
-    mul_held, add_held, mean_held, width_held, gauss_held, coord1_held, coord2_held = refs[19:26]
+    w_heads, coords, w_gauss, w_coord1, w_coord2 = refs[9:14]
+    lookup, own_columns, kernels = refs[14:17]
+    mul_held, add_held, mean_held, width_held, gauss_held, coord1_held, coord2_held = refs[17:24]
     copies = fetch(
-        refs[:10],
-        (w_heads, ln_gain, coords, mul_held, add_held, mean_held, width_held)
+        refs[:9],
+        (w_heads, coords, mul_held, add_held, mean_held, width_held)
         + (gauss_held, coord1_held, coord2_held),
-        refs[26],
+        refs[24],
     )
     table = mine[(cols - 1) * bias_rows :, :].astype(f32)[:table_rows]
     places = (table[0:3] + table[8:11]) + table[4:7]
@@ -291,12 +285,11 @@
 def attend_kernel(dims, count, *refs):
     own, cols, width, heads, keys, kinds = dims
     pieces = refs[:count]
-    bias, keyed, w_qkv, w_heads, ln_gain, coords = refs[count : count + 6]
-    w_gauss, w_coord1, w_coord2, lookup, own_columns, kernels = refs[count + 6 : count + 12]
-    attended, moved, logits, values, places, strengths = refs[count + 12 :]
+    bias, spread_queries, w_qkv, w_heads, coords = refs[count : count + 5]
+    w_gauss, w_coord1, w_coord2, lookup, own_columns, kernels = refs[count + 5 : count + 11]
+    attended, moved, logits, values, places, strengths = refs[count + 11 :]
     atoms = bias.shape[1]
     each = 2 * own * cols
-    gain = ln_gain[...]
     centre, sharp, norming = kernels[0], kernels[1], kernels[2]
     found = lookup[...]
 
@@ -327,16 +320,20 @@
             )
             for ref in taken
         ]
-        block = normed(jnp.concatenate(x, axis=0), gain)
+        block = jnp.concatenate(x, axis=0)
+        keys_here = jnp.dot(block, w_qkv[:, width : 2 * width], preferred_element_type=f32)
+        affinity = lax.dot_general(
+            spread_queries[...], keys_here.astype(bf16), nt, preferred_element_type=f32
+        )
         values[s : s + lanes, :] = jnp.dot(
             block, w_qkv[:, 2 * width :], preferred_element_type=f32
         ).astype(bf16)
-        affinity = lax.dot_general(keyed[...], block, nt, preferred_element_type=f32)
         here = bias[:, s : s + lanes].astype(f32)
         rows = []
         for i in range(own):
             at = slice(i * heads, (i + 1) * heads)
-            row = (here[at] + affinity[at]) + geometry[:, i * lanes : (i + 1) * lanes]
+            row = here[at] + affinity[at] * (1.0 / math.sqrt(width // heads))
+            row = row + geometry[:, i * lanes : (i + 1) * lanes]
             logits[at, s : s + lanes] = jnp.where(here[at] < masked_below, masked_fill, row)
             rows.append(row.astype(bf16))
         mixed = jnp.dot(w_coord1[...], jnp.concatenate(rows, axis=1), preferred_element_type=f32)
@@ -431,6 +428,7 @@
         coords,
         atom_types[None, :],
         segment_ids[None, :],
+        ln_gain[None, :],
         pair_mask,
         pair_bias.transpose(1, 2, 0),
     )
@@ -444,7 +442,7 @@
         (),
         own_arrays,
         [pltpu.VMEM(x.shape, x.dtype) for x in own_arrays]
-        + [pltpu.VMEM((cols, mask_rows, lanes), f32), pltpu.SemaphoreType.DMA((6,))],
+        + [pltpu.VMEM((cols, mask_rows, lanes), f32), pltpu.SemaphoreType.DMA((7,))],
     )
     other = exchange(mine, near_step, still)
     grouped = call(
@@ -454,7 +452,7 @@
         (mine, other),
     )
     received = [exchange(x, near_step, shift) for x, shift in zip(grouped, along_col, strict=True)]
-    small = (w_heads.T, ln_gain[None, :], coords)
+    small = (w_heads.T, coords)
     tables = (gauss_mul, gauss_add, gauss_mean[None, :], gauss_width[None, :], w_gauss, w_coord1)
     tables += (w_coord2[None, :],)
     prepared = call(
@@ -471,11 +469,11 @@
         ],
         (lax.optimization_barrier((mine, grouped[0]))[0],),
         small + tables,
-        [pltpu.VMEM(x.shape, x.dtype) for x in tables] + [pltpu.SemaphoreType.DMA((10,))],
+        [pltpu.VMEM(x.shape, x.dtype) for x in tables] + [pltpu.SemaphoreType.DMA((9,))],
     )
     received[0], prepared = lax.optimization_barrier((received[0], prepared))
     received += [exchange(x, near_step, still) for x in received[:-1]]
-    w_heads, ln_gain, coords, w_gauss, w_coord1, w_coord2, lookup, own_columns, kernels = prepared
+    w_heads, coords, w_gauss, w_coord1, w_coord2, lookup, own_columns, kernels = prepared
     near = call(
         functools.partial(gather_kernel, dims),
         "gather",
@@ -484,7 +482,7 @@
     )
     pieces = [near] + [exchange(near, step, still) for step in along_row]
     pieces += [exchange(x, near_step, still) for x in pieces[1 : len(along_row)]]
-    bias, keyed, w_qkv = call(
+    bias, spread_queries, w_qkv = call(
         functools.partial(arrange_kernel, dims, column_parts, row_parts),
         "arrange",
         [
@@ -492,7 +490,7 @@
             shape((own * heads, width), bf16),
             shape(w_qkv.shape, bf16),
         ],
-        (lax.optimization_barrier((mine, pieces[1]))[0], kept, *received, ln_gain),
+        (lax.optimization_barrier((mine, pieces[1]))[0], kept, *received),
         (w_qkv,),
         [pltpu.SemaphoreType.DMA((1,))],
     )
@@ -500,7 +498,7 @@
         functools.partial(attend_kernel, dims, len(pieces)),
         "attend",
         [shape((own, width), bf16), shape((3, own), f32)],
-        (*pieces, bias, keyed, w_qkv, w_heads, ln_gain, coords)
+        (*pieces, bias, spread_queries, w_qkv, w_heads, coords)
         + (w_gauss, w_coord1, w_coord2, lookup, own_columns, kernels),
         (),
         [

time: 18.8 us -> 18.9 us (level)
  waiting for transfers between devices: 3.46 us -> 3.75 us
    ppermute x7, waiting for transfers between devices: 3.46 us -> 3.75 us  [exchange(): return lax.ppermute(x, ('row', 'col'), pairs)]
  transfers between devices with their start and end apart: 7 -> 7, of which waited for: 6 -> 6; matrix products, arithmetic and copies ran while one was open for 0% -> 0% of each run, Pallas kernels for 16% -> 15%
where the time goes in v6:
time: 18.9 us; the launch traced here: 18.6 us
  starting transfers between devices  8.42 us (45%)
  Pallas kernels  5.8 us (31%)
  waiting for transfers between devices  3.75 us (20%)
  between operations  0.66 us (3%)
    ppermute x7, starting transfers between devices, exchange(): return lax.ppermute(x, ('row', 'col'), pairs)  8.42 us
    pallas_call x6, Pallas kernels, call(): pl.pallas_call(kernel, out_shape=out_shape, in_specs=[vmem] * len(inputs)...  5.8 us
    ppermute x7, waiting for transfers between devices, exchange(): return lax.ppermute(x, ('row', 'col'), pairs)  3.75 us
  transfers between devices with their start and end apart: 7, of which 6 were waited for; matrix products, arithmetic and copies ran while one was open for 0% of the time, Pallas kernels for 15%

profile of v6, /device:TPU:0, one launch (start us, length us, event | category | flops | bytes accessed | tf_op | source)
XLA Modules:
  0.0 18.6 jit_solution(3567956071009755590)
XLA Ops:
  0.6 1.2 %pack.1 = (bf16[240,128]{1,0:T(8,128)(2,1)S(1)}, bf16[80,128]{1,0:T(8,128)(2,1)S(1)}) custom-call(bf16[4,512]{1,0:T(4,128)(2,1)} %refs_0_.1, f32[3,4]{1,0:T(4,128)} %refs_1_.3, s32[1,4]{1,0:T(1,128)} %bitcast.11, s32[1,4]{1,0:T(1,128)} %bitcast.12, f32[1,512]{1,0:T(1,128)} %bitcast.10, s32[16,32]{1,0:T(8,128)} %refs_5_.1, bf16[16,32,64]{2,1,0:T(8,128)(2,1)} %bitcast.8), custom_call_target="tpu_custom_call" | custom-call | tf_op jit(solution)/shard_map/pack/pallas_call | solution.py:416
  1.8 0.5 %collective-permute-start = (bf16[240,128]{1,0:T(8,128)(2,1)S(1)}, bf16[240,128]{1,0:T(8,128)(2,1)S(1)}, u32[]{:S(2)}, u32[]{:S(2)}) collective-permute-start(bf16[240,128]{1,0:T(8,128)(2,1)S(1)} %get-tuple-element.41.mine), channel_id=1, source_target_pairs={{0,4},{1,5},{2,6},{3,7},{4,0},{5,1},{6,2},{7,3},{8,12},{9,13},{10,... | collective-permute-start | bytes 184328 | tf_op jit(solution)/shard_map/ppermute | solution.py:377
  2.3 0.9 %collective-permute-done.other = bf16[240,128]{1,0:T(8,128)(2,1)S(1)} collective-permute-done((bf16[240,128]{1,0:T(8,128)(2,1)S(1)}, bf16[240,128]{1,0:T(8,128)(2,1)S(1)}, u32[]{:S(2)}, u32[]{:S(2)}) %collective-permute-start) | collective-permute-done | bytes 61472 | tf_op jit(solution)/shard_map/ppermute | solution.py:377
  3.2 0.1 regroup.1
  3.3 3.7 %collective-permute-start.1 = (bf16[176,128]{1,0:T(8,128)(2,1)S(1)}, bf16[176,128]{1,0:T(8,128)(2,1)S(1)}, u32[]{:S(2)}, u32[]{:S(2)}) collective-permute-start(bf16[176,128]{1,0:T(8,128)(2,1)S(1)} %get-tuple-element.29), channel_id=1, source_target_pairs={{0,6},{1,7},{2,4},{3,5},{4,1},{5,2},{6,3},{7,0},{8,14},{9,15},{10,... | collective-permute-start | bytes 135176 | tf_op jit(solution)/shard_map/ppermute | solution.py:377
  7.0 1.1 %collective-permute-start.2 = (bf16[176,128]{1,0:T(8,128)(2,1)S(1)}, bf16[176,128]{1,0:T(8,128)(2,1)S(1)}, u32[]{:S(2)}, u32[]{:S(2)}) collective-permute-start(bf16[176,128]{1,0:T(8,128)(2,1)S(1)} %get-tuple-element.40), channel_id=1, source_target_pairs={{0,7},{1,4},{2,5},{3,6},{4,3},{5,0},{6,1},{7,2},{8,15},{9,12},{10,... | collective-permute-start | bytes 135176 | tf_op jit(solution)/shard_map/ppermute | solution.py:377
  8.1 1.1 %prepare.1 = (bf16[64,128]{1,0:T(8,128)(2,1)S(1)}, f32[3,4]{1,0:T(4,128)S(1)}, bf16[128,128]{1,0:T(8,128)(2,1)S(1)}, bf16[64,64]{1,0:T(8,128)(2,1)S(1)}, f32[64,...) custom-call(bf16[240,128]{1,0:T(8,128)(2,1)S(1)} %get-tuple-element.41.mine, ...), custom_call_target="tpu_custom_call" | custom-call | tf_op jit(solution)/shard_map/prepare/pallas_call | solution.py:416
  9.2 0.5 %collective-permute-done.1.refs_0_ = bf16[176,128]{1,0:T(8,128)(2,1)S(1)} collective-permute-done((bf16[176,128]{1,0:T(8,128)(2,1)S(1)}, bf16[176,128]{1,0:T(8,128)(2,1)S(1)}, u32[]{:S(2)}, u32[]{:S(2)}) %collective-permute-start.1) | collective-permute-done | bytes 45088 | tf_op jit(solution)/shard_map/ppermute | solution.py:377
  9.7 0.0 collective-permute-start.3
  9.7 1.1 %collective-permute-done.2.refs_1_ = bf16[176,128]{1,0:T(8,128)(2,1)S(1)} collective-permute-done((bf16[176,128]{1,0:T(8,128)(2,1)S(1)}, bf16[176,128]{1,0:T(8,128)(2,1)S(1)}, u32[]{:S(2)}, u32[]{:S(2)}) %collective-permute-start.2) | collective-permute-done | bytes 45088 | tf_op jit(solution)/shard_map/ppermute | solution.py:377
  10.8 0.1 collective-permute-done.3.refs_2_
  11.0 0.1 gather.1.refs_0_
  11.0 1.5 %collective-permute-start.4 = (bf16[144,128]{1,0:T(8,128)(2,1)S(1)}, bf16[144,128]{1,0:T(8,128)(2,1)S(1)}, u32[]{:S(2)}, u32[]{:S(2)}) collective-permute-start(bf16[144,128]{1,0:T(8,128)(2,1)S(1)} %gather.1.refs_0_), channel_id=1, source_target_pairs={{0,12},{1,13},{2,14},{3,15},{4,16},{5,17},{6,18},{7,19},{8,4},{9,5... | collective-permute-start | bytes 110600 | tf_op jit(solution)/shard_map/ppermute | solution.py:377
  12.6 1.4 %collective-permute-start.5 = (bf16[144,128]{1,0:T(8,128)(2,1)S(1)}, bf16[144,128]{1,0:T(8,128)(2,1)S(1)}, u32[]{:S(2)}, u32[]{:S(2)}) collective-permute-start(bf16[144,128]{1,0:T(8,128)(2,1)S(1)} %gather.1.refs_0_), channel_id=1, source_target_pairs={{0,28},{1,29},{2,30},{3,31},{4,24},{5,25},{6,26},{7,27},{8,20},{9,... | collective-permute-start | bytes 110600 | tf_op jit(solution)/shard_map/ppermute | solution.py:377
  14.0 0.4 %collective-permute-done.4.refs_1_ = bf16[144,128]{1,0:T(8,128)(2,1)S(1)} collective-permute-done((bf16[144,128]{1,0:T(8,128)(2,1)S(1)}, bf16[144,128]{1,0:T(8,128)(2,1)S(1)}, u32[]{:S(2)}, u32[]{:S(2)}) %collective-permute-start.4) | collective-permute-done | bytes 36896 | tf_op jit(solution)/shard_map/ppermute | solution.py:377
  14.4 0.2 collective-permute-start.6
  14.6 1.6 %arrange.1 = (bf16[256,128]{1,0:T(8,128)(2,1)S(1)}, bf16[256,512]{1,0:T(8,128)(2,1)S(1)}, bf16[512,1536]{1,0:T(8,128)(2,1)S(1)}) custom-call(bf16[240,128]{1,0:T(8,128)(2,1)S(1)} %get-tuple-element.41.mine, bf16[80,128]{1,0:T(8,128)(2,1)S(1)} %get-tuple-element.42.kept, bf16[176,128]{1,0:T(8,128)(2,1)S(1)} %collective-permute-done.1.refs_0_, ...), custom_call_target="tpu_custom_call" | custom-call | tf_op jit(solution)/shard_map/arrange/pallas_call | solution.py:416
  16.2 0.7 %collective-permute-done.5.refs_2_ = bf16[144,128]{1,0:T(8,128)(2,1)S(1)} collective-permute-done((bf16[144,128]{1,0:T(8,128)(2,1)S(1)}, bf16[144,128]{1,0:T(8,128)(2,1)S(1)}, u32[]{:S(2)}, u32[]{:S(2)}) %collective-permute-start.5) | collective-permute-done | bytes 36896 | tf_op jit(solution)/shard_map/ppermute | solution.py:377
  16.9 0.0 collective-permute-done.6.refs_3_
  16.9 1.7 %attend.1 = (bf16[4,512]{1,0:T(4,128)(2,1)}, f32[3,4]{1,0:T(4,128)}) custom-call(bf16[144,128]{1,0:T(8,128)(2,1)S(1)} %gather.1.refs_0_, bf16[144,128]{1,0:T(8,128)(2,1)S(1)} %collective-permute-done.4.refs_1_, bf16[144,128]{1,0:T(8,128)(2,1)S(1)} %collective-permute-done.5.refs_2_, bf16[144,128]{1,0:T(8,128)(2,1)S(1)} %collective-permute-done.6.refs_3_, ...), custom_call_target="tpu_custom_call" | custom-call | tf_op jit(solution)/shard_map/attend/pallas_call | solution.py:416
Async XLA Ops:
  1.8 1.4 %collective-permute-start = (bf16[240,128]{1,0:T(8,128)(2,1)S(1)}, bf16[240,128]{1,0:T(8,128)(2,1)S(1)}, u32[]{:S(2)}, u32[]{:S(2)}) collective-permute-start(bf16[240,128]{1,0:T(8,128)(2,1)S(1)} %get-tuple-element.41.mine), channel_id=1, source_target_pairs={{0,4},{1,5},{2,6},{3,7},{4,0},{5,1},{6,2},{7,3},{8,12},{9,13},{10,... | collective-permute-start | bytes 184328 | tf_op jit(solution)/shard_map/ppermute | solution.py:377
  3.3 6.5 %collective-permute-start.1 = (bf16[176,128]{1,0:T(8,128)(2,1)S(1)}, bf16[176,128]{1,0:T(8,128)(2,1)S(1)}, u32[]{:S(2)}, u32[]{:S(2)}) collective-permute-start(bf16[176,128]{1,0:T(8,128)(2,1)S(1)} %get-tuple-element.29), channel_id=1, source_target_pairs={{0,6},{1,7},{2,4},{3,5},{4,1},{5,2},{6,3},{7,0},{8,14},{9,15},{10,... | collective-permute-start | bytes 135176 | tf_op jit(solution)/shard_map/ppermute | solution.py:377
  7.0 3.8 %collective-permute-start.2 = (bf16[176,128]{1,0:T(8,128)(2,1)S(1)}, bf16[176,128]{1,0:T(8,128)(2,1)S(1)}, u32[]{:S(2)}, u32[]{:S(2)}) collective-permute-start(bf16[176,128]{1,0:T(8,128)(2,1)S(1)} %get-tuple-element.40), channel_id=1, source_target_pairs={{0,7},{1,4},{2,5},{3,6},{4,3},{5,0},{6,1},{7,2},{8,15},{9,12},{10,... | collective-permute-start | bytes 135176 | tf_op jit(solution)/shard_map/ppermute | solution.py:377
  9.7 1.2 %collective-permute-start.3 = (bf16[176,128]{1,0:T(8,128)(2,1)S(1)}, bf16[176,128]{1,0:T(8,128)(2,1)S(1)}, u32[]{:S(2)}, u32[]{:S(2)}) collective-permute-start(bf16[176,128]{1,0:T(8,128)(2,1)S(1)} %collective-permute-done.1.refs_0_), channel_id=1, source_target_pairs={{0,4},{1,5},{2,6},{3,7},{4,0},{5,1},{6,2},{7,3},{8,12},{9,13},{10,... | collective-permute-start | bytes 135176 | tf_op jit(solution)/shard_map/ppermute | solution.py:377
  11.0 3.4 %collective-permute-start.4 = (bf16[144,128]{1,0:T(8,128)(2,1)S(1)}, bf16[144,128]{1,0:T(8,128)(2,1)S(1)}, u32[]{:S(2)}, u32[]{:S(2)}) collective-permute-start(bf16[144,128]{1,0:T(8,128)(2,1)S(1)} %gather.1.refs_0_), channel_id=1, source_target_pairs={{0,12},{1,13},{2,14},{3,15},{4,16},{5,17},{6,18},{7,19},{8,4},{9,5... | collective-permute-start | bytes 110600 | tf_op jit(solution)/shard_map/ppermute | solution.py:377
  12.6 4.3 %collective-permute-start.5 = (bf16[144,128]{1,0:T(8,128)(2,1)S(1)}, bf16[144,128]{1,0:T(8,128)(2,1)S(1)}, u32[]{:S(2)}, u32[]{:S(2)}) collective-permute-start(bf16[144,128]{1,0:T(8,128)(2,1)S(1)} %gather.1.refs_0_), channel_id=1, source_target_pairs={{0,28},{1,29},{2,30},{3,31},{4,24},{5,25},{6,26},{7,27},{8,20},{9,... | collective-permute-start | bytes 110600 | tf_op jit(solution)/shard_map/ppermute | solution.py:377
  14.4 2.5 %collective-permute-start.6 = (bf16[144,128]{1,0:T(8,128)(2,1)S(1)}, bf16[144,128]{1,0:T(8,128)(2,1)S(1)}, u32[]{:S(2)}, u32[]{:S(2)}) collective-permute-start(bf16[144,128]{1,0:T(8,128)(2,1)S(1)} %collective-permute-done.4.refs_1_), channel_id=1, source_target_pairs={{0,4},{1,5},{2,6},{3,7},{4,0},{5,1},{6,2},{7,3},{8,12},{9,13},{10,... | collective-permute-start | bytes 110600 | tf_op jit(solution)/shard_map/ppermute | solution.py:377

commit v7 on v6

--- a/solution.py
+++ b/solution.py
@@ -295,6 +295,17 @@
 
     for s in range(0, atoms, lanes):
         taken = pieces[s // each : (s + lanes) // each]
+        x = [
+            jnp.concatenate(
+                [
+                    ref[table_rows + b * each : table_rows + (b + 1) * each, :]
+                    for b in range(width // lanes)
+                ],
+                axis=1,
+            )
+            for ref in taken
+        ]
+        block = jnp.concatenate(x, axis=0)
         table = jnp.concatenate([ref[:table_rows, :].astype(f32)[:, :each] for ref in taken], axis=1)
         place = (table[0:3] + table[8:11]) + table[4:7]
         places[0:3, s : s + lanes] = place
@@ -308,26 +319,15 @@
         for i in range(own):
             scaled = (expanded[i : i + 1] - centre) * sharp
             features.append(jnp.exp2(norming - scaled * scaled).astype(bf16))
-        hidden = jnp.dot(w_gauss[...], jnp.concatenate(features, axis=1), preferred_element_type=f32)
-        geometry = jnp.dot(w_heads[...], gelu(hidden).astype(bf16), preferred_element_type=f32)
-        x = [
-            jnp.concatenate(
-                [
-                    ref[table_rows + b * each : table_rows + (b + 1) * each, :]
-                    for b in range(width // lanes)
-                ],
-                axis=1,
-            )
-            for ref in taken
-        ]
-        block = jnp.concatenate(x, axis=0)
         keys_here = jnp.dot(block, w_qkv[:, width : 2 * width], preferred_element_type=f32)
+        values[s : s + lanes, :] = jnp.dot(
+            block, w_qkv[:, 2 * width :], preferred_element_type=f32
+        ).astype(bf16)
         affinity = lax.dot_general(
             spread_queries[...], keys_here.astype(bf16), nt, preferred_element_type=f32
         )
-        values[s : s + lanes, :] = jnp.dot(
-            block, w_qkv[:, 2 * width :], preferred_element_type=f32
-        ).astype(bf16)
+        hidden = jnp.dot(w_gauss[...], jnp.concatenate(features, axis=1), preferred_element_type=f32)
+        geometry = jnp.dot(w_heads[...], gelu(hidden).astype(bf16), preferred_element_type=f32)
         here = bias[:, s : s + lanes].astype(f32)
         rows = []
         for i in range(own):

time: 18.9 us -> 18.6 us (0.984)
  Pallas kernels: 5.8 us -> 5.48 us
    pallas_call x6, Pallas kernels: 5.8 us -> 5.48 us  [call(): pl.pallas_call(kernel, out_shape=out_shape, in_specs=[vmem] * len(inputs)...]
where the time goes in v7:
time: 18.6 us; the launch traced here: 18.3 us
  starting transfers between devices  8.42 us (45%)
  Pallas kernels  5.48 us (29%)
  waiting for transfers between devices  3.75 us (20%)
  between operations  0.66 us (4%)
    ppermute x7, starting transfers between devices, exchange(): return lax.ppermute(x, ('row', 'col'), pairs)  8.42 us
    pallas_call x6, Pallas kernels, call(): pl.pallas_call(kernel, out_shape=out_shape, in_specs=[vmem] * len(inputs)...  5.48 us
    ppermute x7, waiting for transfers between devices, exchange(): return lax.ppermute(x, ('row', 'col'), pairs)  3.75 us
  transfers between devices with their start and end apart: 7, of which 6 were waited for; matrix products, arithmetic and copies ran while one was open for 0% of the time, Pallas kernels for 15%

profile of v7, /device:TPU:0, one launch (start us, length us, event | category | flops | bytes accessed | tf_op | source)
XLA Modules:
  0.0 18.3 jit_solution(3068730484491742075)
XLA Ops:
  0.6 1.2 %pack.1 = (bf16[240,128]{1,0:T(8,128)(2,1)S(1)}, bf16[80,128]{1,0:T(8,128)(2,1)S(1)}) custom-call(bf16[4,512]{1,0:T(4,128)(2,1)} %refs_0_.1, f32[3,4]{1,0:T(4,128)} %refs_1_.3, s32[1,4]{1,0:T(1,128)} %bitcast.11, s32[1,4]{1,0:T(1,128)} %bitcast.12, f32[1,512]{1,0:T(1,128)} %bitcast.10, s32[16,32]{1,0:T(8,128)} %refs_5_.1, bf16[16,32,64]{2,1,0:T(8,128)(2,1)} %bitcast.8), custom_call_target="tpu_custom_call" | custom-call | tf_op jit(solution)/shard_map/pack/pallas_call | solution.py:416
  1.8 0.5 %collective-permute-start = (bf16[240,128]{1,0:T(8,128)(2,1)S(1)}, bf16[240,128]{1,0:T(8,128)(2,1)S(1)}, u32[]{:S(2)}, u32[]{:S(2)}) collective-permute-start(bf16[240,128]{1,0:T(8,128)(2,1)S(1)} %get-tuple-element.41.mine), channel_id=1, source_target_pairs={{0,4},{1,5},{2,6},{3,7},{4,0},{5,1},{6,2},{7,3},{8,12},{9,13},{10,... | collective-permute-start | bytes 184328 | tf_op jit(solution)/shard_map/ppermute | solution.py:377
  2.3 0.9 %collective-permute-done.other = bf16[240,128]{1,0:T(8,128)(2,1)S(1)} collective-permute-done((bf16[240,128]{1,0:T(8,128)(2,1)S(1)}, bf16[240,128]{1,0:T(8,128)(2,1)S(1)}, u32[]{:S(2)}, u32[]{:S(2)}) %collective-permute-start) | collective-permute-done | bytes 61472 | tf_op jit(solution)/shard_map/ppermute | solution.py:377
  3.2 0.1 regroup.1
  3.3 3.7 %collective-permute-start.1 = (bf16[176,128]{1,0:T(8,128)(2,1)S(1)}, bf16[176,128]{1,0:T(8,128)(2,1)S(1)}, u32[]{:S(2)}, u32[]{:S(2)}) collective-permute-start(bf16[176,128]{1,0:T(8,128)(2,1)S(1)} %get-tuple-element.29), channel_id=1, source_target_pairs={{0,6},{1,7},{2,4},{3,5},{4,1},{5,2},{6,3},{7,0},{8,14},{9,15},{10,... | collective-permute-start | bytes 135176 | tf_op jit(solution)/shard_map/ppermute | solution.py:377
  7.0 1.1 %collective-permute-start.2 = (bf16[176,128]{1,0:T(8,128)(2,1)S(1)}, bf16[176,128]{1,0:T(8,128)(2,1)S(1)}, u32[]{:S(2)}, u32[]{:S(2)}) collective-permute-start(bf16[176,128]{1,0:T(8,128)(2,1)S(1)} %get-tuple-element.40), channel_id=1, source_target_pairs={{0,7},{1,4},{2,5},{3,6},{4,3},{5,0},{6,1},{7,2},{8,15},{9,12},{10,... | collective-permute-start | bytes 135176 | tf_op jit(solution)/shard_map/ppermute | solution.py:377
  8.1 1.1 %prepare.1 = (bf16[64,128]{1,0:T(8,128)(2,1)S(1)}, f32[3,4]{1,0:T(4,128)S(1)}, bf16[128,128]{1,0:T(8,128)(2,1)S(1)}, bf16[64,64]{1,0:T(8,128)(2,1)S(1)}, f32[64,...) custom-call(bf16[240,128]{1,0:T(8,128)(2,1)S(1)} %get-tuple-element.41.mine, ...), custom_call_target="tpu_custom_call" | custom-call | tf_op jit(solution)/shard_map/prepare/pallas_call | solution.py:416
  9.2 0.5 %collective-permute-done.1.refs_0_ = bf16[176,128]{1,0:T(8,128)(2,1)S(1)} collective-permute-done((bf16[176,128]{1,0:T(8,128)(2,1)S(1)}, bf16[176,128]{1,0:T(8,128)(2,1)S(1)}, u32[]{:S(2)}, u32[]{:S(2)}) %collective-permute-start.1) | collective-permute-done | bytes 45088 | tf_op jit(solution)/shard_map/ppermute | solution.py:377
  9.7 0.0 collective-permute-start.3
  9.7 1.1 %collective-permute-done.2.refs_1_ = bf16[176,128]{1,0:T(8,128)(2,1)S(1)} collective-permute-done((bf16[176,128]{1,0:T(8,128)(2,1)S(1)}, bf16[176,128]{1,0:T(8,128)(2,1)S(1)}, u32[]{:S(2)}, u32[]{:S(2)}) %collective-permute-start.2) | collective-permute-done | bytes 45088 | tf_op jit(solution)/shard_map/ppermute | solution.py:377
  10.8 0.1 collective-permute-done.3.refs_2_
  11.0 0.1 gather.1.refs_0_
  11.0 1.5 %collective-permute-start.4 = (bf16[144,128]{1,0:T(8,128)(2,1)S(1)}, bf16[144,128]{1,0:T(8,128)(2,1)S(1)}, u32[]{:S(2)}, u32[]{:S(2)}) collective-permute-start(bf16[144,128]{1,0:T(8,128)(2,1)S(1)} %gather.1.refs_0_), channel_id=1, source_target_pairs={{0,12},{1,13},{2,14},{3,15},{4,16},{5,17},{6,18},{7,19},{8,4},{9,5... | collective-permute-start | bytes 110600 | tf_op jit(solution)/shard_map/ppermute | solution.py:377
  12.6 1.4 %collective-permute-start.5 = (bf16[144,128]{1,0:T(8,128)(2,1)S(1)}, bf16[144,128]{1,0:T(8,128)(2,1)S(1)}, u32[]{:S(2)}, u32[]{:S(2)}) collective-permute-start(bf16[144,128]{1,0:T(8,128)(2,1)S(1)} %gather.1.refs_0_), channel_id=1, source_target_pairs={{0,28},{1,29},{2,30},{3,31},{4,24},{5,25},{6,26},{7,27},{8,20},{9,... | collective-permute-start | bytes 110600 | tf_op jit(solution)/shard_map/ppermute | solution.py:377
  14.0 0.4 %collective-permute-done.4.refs_1_ = bf16[144,128]{1,0:T(8,128)(2,1)S(1)} collective-permute-done((bf16[144,128]{1,0:T(8,128)(2,1)S(1)}, bf16[144,128]{1,0:T(8,128)(2,1)S(1)}, u32[]{:S(2)}, u32[]{:S(2)}) %collective-permute-start.4) | collective-permute-done | bytes 36896 | tf_op jit(solution)/shard_map/ppermute | solution.py:377
  14.4 0.2 collective-permute-start.6
  14.6 1.6 %arrange.1 = (bf16[256,128]{1,0:T(8,128)(2,1)S(1)}, bf16[256,512]{1,0:T(8,128)(2,1)S(1)}, bf16[512,1536]{1,0:T(8,128)(2,1)S(1)}) custom-call(bf16[240,128]{1,0:T(8,128)(2,1)S(1)} %get-tuple-element.41.mine, bf16[80,128]{1,0:T(8,128)(2,1)S(1)} %get-tuple-element.42.kept, bf16[176,128]{1,0:T(8,128)(2,1)S(1)} %collective-permute-done.1.refs_0_, ...), custom_call_target="tpu_custom_call" | custom-call | tf_op jit(solution)/shard_map/arrange/pallas_call | solution.py:416
  16.2 0.7 %collective-permute-done.5.refs_2_ = bf16[144,128]{1,0:T(8,128)(2,1)S(1)} collective-permute-done((bf16[144,128]{1,0:T(8,128)(2,1)S(1)}, bf16[144,128]{1,0:T(8,128)(2,1)S(1)}, u32[]{:S(2)}, u32[]{:S(2)}) %collective-permute-start.5) | collective-permute-done | bytes 36896 | tf_op jit(solution)/shard_map/ppermute | solution.py:377
  16.9 0.0 collective-permute-done.6.refs_3_
  16.9 1.4 %attend.1 = (bf16[4,512]{1,0:T(4,128)(2,1)}, f32[3,4]{1,0:T(4,128)}) custom-call(bf16[144,128]{1,0:T(8,128)(2,1)S(1)} %gather.1.refs_0_, bf16[144,128]{1,0:T(8,128)(2,1)S(1)} %collective-permute-done.4.refs_1_, bf16[144,128]{1,0:T(8,128)(2,1)S(1)} %collective-permute-done.5.refs_2_, bf16[144,128]{1,0:T(8,128)(2,1)S(1)} %collective-permute-done.6.refs_3_, ...), custom_call_target="tpu_custom_call" | custom-call | tf_op jit(solution)/shard_map/attend/pallas_call | solution.py:416
Async XLA Ops:
  1.8 1.4 %collective-permute-start = (bf16[240,128]{1,0:T(8,128)(2,1)S(1)}, bf16[240,128]{1,0:T(8,128)(2,1)S(1)}, u32[]{:S(2)}, u32[]{:S(2)}) collective-permute-start(bf16[240,128]{1,0:T(8,128)(2,1)S(1)} %get-tuple-element.41.mine), channel_id=1, source_target_pairs={{0,4},{1,5},{2,6},{3,7},{4,0},{5,1},{6,2},{7,3},{8,12},{9,13},{10,... | collective-permute-start | bytes 184328 | tf_op jit(solution)/shard_map/ppermute | solution.py:377
  3.3 6.5 %collective-permute-start.1 = (bf16[176,128]{1,0:T(8,128)(2,1)S(1)}, bf16[176,128]{1,0:T(8,128)(2,1)S(1)}, u32[]{:S(2)}, u32[]{:S(2)}) collective-permute-start(bf16[176,128]{1,0:T(8,128)(2,1)S(1)} %get-tuple-element.29), channel_id=1, source_target_pairs={{0,6},{1,7},{2,4},{3,5},{4,1},{5,2},{6,3},{7,0},{8,14},{9,15},{10,... | collective-permute-start | bytes 135176 | tf_op jit(solution)/shard_map/ppermute | solution.py:377
  7.0 3.8 %collective-permute-start.2 = (bf16[176,128]{1,0:T(8,128)(2,1)S(1)}, bf16[176,128]{1,0:T(8,128)(2,1)S(1)}, u32[]{:S(2)}, u32[]{:S(2)}) collective-permute-start(bf16[176,128]{1,0:T(8,128)(2,1)S(1)} %get-tuple-element.40), channel_id=1, source_target_pairs={{0,7},{1,4},{2,5},{3,6},{4,3},{5,0},{6,1},{7,2},{8,15},{9,12},{10,... | collective-permute-start | bytes 135176 | tf_op jit(solution)/shard_map/ppermute | solution.py:377
  9.7 1.2 %collective-permute-start.3 = (bf16[176,128]{1,0:T(8,128)(2,1)S(1)}, bf16[176,128]{1,0:T(8,128)(2,1)S(1)}, u32[]{:S(2)}, u32[]{:S(2)}) collective-permute-start(bf16[176,128]{1,0:T(8,128)(2,1)S(1)} %collective-permute-done.1.refs_0_), channel_id=1, source_target_pairs={{0,4},{1,5},{2,6},{3,7},{4,0},{5,1},{6,2},{7,3},{8,12},{9,13},{10,... | collective-permute-start | bytes 135176 | tf_op jit(solution)/shard_map/ppermute | solution.py:377
  11.0 3.4 %collective-permute-start.4 = (bf16[144,128]{1,0:T(8,128)(2,1)S(1)}, bf16[144,128]{1,0:T(8,128)(2,1)S(1)}, u32[]{:S(2)}, u32[]{:S(2)}) collective-permute-start(bf16[144,128]{1,0:T(8,128)(2,1)S(1)} %gather.1.refs_0_), channel_id=1, source_target_pairs={{0,12},{1,13},{2,14},{3,15},{4,16},{5,17},{6,18},{7,19},{8,4},{9,5... | collective-permute-start | bytes 110600 | tf_op jit(solution)/shard_map/ppermute | solution.py:377
  12.6 4.3 %collective-permute-start.5 = (bf16[144,128]{1,0:T(8,128)(2,1)S(1)}, bf16[144,128]{1,0:T(8,128)(2,1)S(1)}, u32[]{:S(2)}, u32[]{:S(2)}) collective-permute-start(bf16[144,128]{1,0:T(8,128)(2,1)S(1)} %gather.1.refs_0_), channel_id=1, source_target_pairs={{0,28},{1,29},{2,30},{3,31},{4,24},{5,25},{6,26},{7,27},{8,20},{9,... | collective-permute-start | bytes 110600 | tf_op jit(solution)/shard_map/ppermute | solution.py:377
  14.4 2.5 %collective-permute-start.6 = (bf16[144,128]{1,0:T(8,128)(2,1)S(1)}, bf16[144,128]{1,0:T(8,128)(2,1)S(1)}, u32[]{:S(2)}, u32[]{:S(2)}) collective-permute-start(bf16[144,128]{1,0:T(8,128)(2,1)S(1)} %collective-permute-done.4.refs_1_), channel_id=1, source_target_pairs={{0,4},{1,5},{2,6},{3,7},{4,0},{5,1},{6,2},{7,3},{8,12},{9,13},{10,... | collective-permute-start | bytes 110600 | tf_op jit(solution)/shard_map/ppermute | solution.py:377

commit v8 on v7

--- a/solution.py
+++ b/solution.py
@@ -177,8 +177,7 @@
     own, cols, width, heads, keys, kinds = dims
     bias_rows, mask_rows, first_rows, wide_table, second_rows = sizes(dims)
     received = refs[: cols - 1]
-    w_source, out, spread_queries, w_qkv, semaphores = refs[cols - 1 :]
-    copies = fetch((w_source,), (w_qkv,), semaphores)
+    w_qkv, out, spread_queries = refs[cols - 1 :]
     atoms = out.shape[1]
     fold = lanes // heads
     each = own // fold
@@ -232,7 +231,6 @@
     rows = mine[(cols - 1) * bias_rows :, :].astype(f32)[table_rows : table_rows + node_rows(width, own)]
     x = jnp.concatenate([rows[b * own : (b + 1) * own] for b in range(width // lanes)], axis=1)
     x = jnp.concatenate([x, jnp.zeros((16 - own, width), f32)], axis=0).astype(bf16)
-    copies[0].wait()
     queries = jnp.dot(x, w_qkv[:, :width], preferred_element_type=f32)
     head_mask = iota((heads, width), 1) // (width // heads) == iota((heads, width), 0)
     for i in range(own):
@@ -243,14 +241,14 @@
 def prepare_kernel(dims, mine, *refs):
     own, cols, width, heads, keys, kinds = dims
     bias_rows, mask_rows, first_rows, wide_table, second_rows = sizes(dims)
-    w_heads, coords, w_gauss, w_coord1, w_coord2 = refs[9:14]
-    lookup, own_columns, kernels = refs[14:17]
-    mul_held, add_held, mean_held, width_held, gauss_held, coord1_held, coord2_held = refs[17:24]
+    w_qkv, w_heads, coords, w_gauss, w_coord1, w_coord2 = refs[10:16]
+    lookup, own_columns, kernels = refs[16:19]
+    mul_held, add_held, mean_held, width_held, gauss_held, coord1_held, coord2_held = refs[19:26]
     copies = fetch(
-        refs[:9],
-        (w_heads, coords, mul_held, add_held, mean_held, width_held)
+        refs[:10],
+        (w_qkv, w_heads, coords, mul_held, add_held, mean_held, width_held)
         + (gauss_held, coord1_held, coord2_held),
-        refs[24],
+        refs[26],
     )
     table = mine[(cols - 1) * bias_rows :, :].astype(f32)[:table_rows]
     places = (table[0:3] + table[8:11]) + table[4:7]
@@ -452,7 +450,7 @@
         (mine, other),
     )
     received = [exchange(x, near_step, shift) for x, shift in zip(grouped, along_col, strict=True)]
-    small = (w_heads.T, coords)
+    small = (w_qkv, w_heads.T, coords)
     tables = (gauss_mul, gauss_add, gauss_mean[None, :], gauss_width[None, :], w_gauss, w_coord1)
     tables += (w_coord2[None, :],)
     prepared = call(
@@ -469,11 +467,11 @@
         ],
         (lax.optimization_barrier((mine, grouped[0]))[0],),
         small + tables,
-        [pltpu.VMEM(x.shape, x.dtype) for x in tables] + [pltpu.SemaphoreType.DMA((9,))],
+        [pltpu.VMEM(x.shape, x.dtype) for x in tables] + [pltpu.SemaphoreType.DMA((10,))],
     )
     received[0], prepared = lax.optimization_barrier((received[0], prepared))
     received += [exchange(x, near_step, still) for x in received[:-1]]
-    w_heads, coords, w_gauss, w_coord1, w_coord2, lookup, own_columns, kernels = prepared
+    w_qkv, w_heads, coords, w_gauss, w_coord1, w_coord2, lookup, own_columns, kernels = prepared
     near = call(
         functools.partial(gather_kernel, dims),
         "gather",
@@ -482,17 +480,14 @@
     )
     pieces = [near] + [exchange(near, step, still) for step in along_row]
     pieces += [exchange(x, near_step, still) for x in pieces[1 : len(along_row)]]
-    bias, spread_queries, w_qkv = call(
+    bias, spread_queries = call(
         functools.partial(arrange_kernel, dims, column_parts, row_parts),
         "arrange",
         [
             shape((own * heads, atoms), bf16),
             shape((own * heads, width), bf16),
-            shape(w_qkv.shape, bf16),
         ],
-        (lax.optimization_barrier((mine, pieces[1]))[0], kept, *received),
-        (w_qkv,),
-        [pltpu.SemaphoreType.DMA((1,))],
+        (lax.optimization_barrier((mine, pieces[1]))[0], kept, *received, w_qkv),
     )
     attended, moved = call(
         functools.partial(attend_kernel, dims, len(pieces)),

time: 18.6 us -> 18.5 us (level)
  Pallas kernels: 5.48 us -> 4.72 us
  starting transfers between devices: 8.42 us -> 8.91 us
  waiting for transfers between devices: 3.75 us -> 4.05 us
    pallas_call x6, Pallas kernels: 5.48 us -> 4.72 us  [call(): pl.pallas_call(kernel, out_shape=out_shape, in_specs=[vmem] * len(inputs)...]
    ppermute x7, starting transfers between devices: 8.42 us -> 8.91 us  [exchange(): return lax.ppermute(x, ('row', 'col'), pairs)]
    ppermute x7, waiting for transfers between devices: 3.75 us -> 4.05 us  [exchange(): return lax.ppermute(x, ('row', 'col'), pairs)]
  transfers between devices with their start and end apart: 7 -> 7, of which waited for: 6 -> 5; matrix products, arithmetic and copies ran while one was open for 0% -> 0% of each run, Pallas kernels for 15% -> 11%
where the time goes in v8:
time: 18.5 us; the launch traced here: 18.4 us
  starting transfers between devices  8.91 us (48%)
  Pallas kernels  4.72 us (26%)
  waiting for transfers between devices  4.05 us (22%)
  between operations  0.67 us (4%)
    ppermute x7, starting transfers between devices, exchange(): return lax.ppermute(x, ('row', 'col'), pairs)  8.91 us
    pallas_call x6, Pallas kernels, call(): pl.pallas_call(kernel, out_shape=out_shape, in_specs=[vmem] * len(inputs)...  4.72 us
    ppermute x7, waiting for transfers between devices, exchange(): return lax.ppermute(x, ('row', 'col'), pairs)  4.05 us
  transfers between devices with their start and end apart: 7, of which 5 were waited for; matrix products, arithmetic and copies ran while one was open for 0% of the time, Pallas kernels for 11%

profile of v8, /device:TPU:0, one launch (start us, length us, event | category | flops | bytes accessed | tf_op | source)
XLA Modules:
  0.0 18.4 jit_solution(10335016399941279554)
XLA Ops:
  0.6 1.2 %pack.1 = (bf16[240,128]{1,0:T(8,128)(2,1)S(1)}, bf16[80,128]{1,0:T(8,128)(2,1)S(1)}) custom-call(bf16[4,512]{1,0:T(4,128)(2,1)} %refs_0_.2, f32[3,4]{1,0:T(4,128)} %refs_2_.1, s32[1,4]{1,0:T(1,128)} %bitcast.11, s32[1,4]{1,0:T(1,128)} %bitcast.12, f32[1,512]{1,0:T(1,128)} %bitcast.10, s32[16,32]{1,0:T(8,128)} %refs_5_.1, bf16[16,32,64]{2,1,0:T(8,128)(2,1)} %bitcast.8), custom_call_target="tpu_custom_call" | custom-call | tf_op jit(solution)/shard_map/pack/pallas_call | solution.py:414
  1.8 0.5 %collective-permute-start = (bf16[240,128]{1,0:T(8,128)(2,1)S(1)}, bf16[240,128]{1,0:T(8,128)(2,1)S(1)}, u32[]{:S(2)}, u32[]{:S(2)}) collective-permute-start(bf16[240,128]{1,0:T(8,128)(2,1)S(1)} %get-tuple-element.43.mine), channel_id=1, source_target_pairs={{0,4},{1,5},{2,6},{3,7},{4,0},{5,1},{6,2},{7,3},{8,12},{9,13},{10,... | collective-permute-start | bytes 184328 | tf_op jit(solution)/shard_map/ppermute | solution.py:375
  2.3 0.9 %collective-permute-done.other = bf16[240,128]{1,0:T(8,128)(2,1)S(1)} collective-permute-done((bf16[240,128]{1,0:T(8,128)(2,1)S(1)}, bf16[240,128]{1,0:T(8,128)(2,1)S(1)}, u32[]{:S(2)}, u32[]{:S(2)}) %collective-permute-start) | collective-permute-done | bytes 61472 | tf_op jit(solution)/shard_map/ppermute | solution.py:375
  3.2 0.1 regroup.1
  3.3 3.7 %collective-permute-start.1 = (bf16[176,128]{1,0:T(8,128)(2,1)S(1)}, bf16[176,128]{1,0:T(8,128)(2,1)S(1)}, u32[]{:S(2)}, u32[]{:S(2)}) collective-permute-start(bf16[176,128]{1,0:T(8,128)(2,1)S(1)} %get-tuple-element.30), channel_id=1, source_target_pairs={{0,6},{1,7},{2,4},{3,5},{4,1},{5,2},{6,3},{7,0},{8,14},{9,15},{10,... | collective-permute-start | bytes 135176 | tf_op jit(solution)/shard_map/ppermute | solution.py:375
  7.0 1.1 %collective-permute-start.2 = (bf16[176,128]{1,0:T(8,128)(2,1)S(1)}, bf16[176,128]{1,0:T(8,128)(2,1)S(1)}, u32[]{:S(2)}, u32[]{:S(2)}) collective-permute-start(bf16[176,128]{1,0:T(8,128)(2,1)S(1)} %get-tuple-element.42), channel_id=1, source_target_pairs={{0,7},{1,4},{2,5},{3,6},{4,3},{5,0},{6,1},{7,2},{8,15},{9,12},{10,... | collective-permute-start | bytes 135176 | tf_op jit(solution)/shard_map/ppermute | solution.py:375
  8.1 1.7 %prepare.1 = (bf16[512,1536]{1,0:T(8,128)(2,1)S(1)}, bf16[64,128]{1,0:T(8,128)(2,1)S(1)}, f32[3,4]{1,0:T(4,128)S(1)}, bf16[128,128]{1,0:T(8,128)(2,1)S(1)}, bf16...) custom-call(bf16[240,128]{1,0:T(8,128)(2,1)S(1)} %get-tuple-element., ...), custom_call_target="tpu_custom_call" | custom-call | tf_op jit(solution)/shard_map/prepare/pallas_call | solution.py:414
  9.8 0.0 collective-permute-done.1.refs_0_
  9.8 0.5 %collective-permute-start.3 = (bf16[176,128]{1,0:T(8,128)(2,1)S(1)}, bf16[176,128]{1,0:T(8,128)(2,1)S(1)}, u32[]{:S(2)}, u32[]{:S(2)}) collective-permute-start(bf16[176,128]{1,0:T(8,128)(2,1)S(1)} %collective-permute-done.1.refs_0_), channel_id=1, source_target_pairs={{0,4},{1,5},{2,6},{3,7},{4,0},{5,1},{6,2},{7,3},{8,12},{9,13},{10,... | collective-permute-start | bytes 135176 | tf_op jit(solution)/shard_map/ppermute | solution.py:375
  10.2 0.6 %collective-permute-done.2.refs_1_ = bf16[176,128]{1,0:T(8,128)(2,1)S(1)} collective-permute-done((bf16[176,128]{1,0:T(8,128)(2,1)S(1)}, bf16[176,128]{1,0:T(8,128)(2,1)S(1)}, u32[]{:S(2)}, u32[]{:S(2)}) %collective-permute-start.2) | collective-permute-done | bytes 45088 | tf_op jit(solution)/shard_map/ppermute | solution.py:375
  10.8 0.3 %collective-permute-done.3.refs_2_ = bf16[176,128]{1,0:T(8,128)(2,1)S(1)} collective-permute-done((bf16[176,128]{1,0:T(8,128)(2,1)S(1)}, bf16[176,128]{1,0:T(8,128)(2,1)S(1)}, u32[]{:S(2)}, u32[]{:S(2)}) %collective-permute-start.3) | collective-permute-done | bytes 45088 | tf_op jit(solution)/shard_map/ppermute | solution.py:375
  11.1 0.1 gather.1.refs_0_
  11.2 1.4 %collective-permute-start.4 = (bf16[144,128]{1,0:T(8,128)(2,1)S(1)}, bf16[144,128]{1,0:T(8,128)(2,1)S(1)}, u32[]{:S(2)}, u32[]{:S(2)}) collective-permute-start(bf16[144,128]{1,0:T(8,128)(2,1)S(1)} %gather.1.refs_0_), channel_id=1, source_target_pairs={{0,12},{1,13},{2,14},{3,15},{4,16},{5,17},{6,18},{7,19},{8,4},{9,5... | collective-permute-start | bytes 110600 | tf_op jit(solution)/shard_map/ppermute | solution.py:375
  12.6 1.4 %collective-permute-start.5 = (bf16[144,128]{1,0:T(8,128)(2,1)S(1)}, bf16[144,128]{1,0:T(8,128)(2,1)S(1)}, u32[]{:S(2)}, u32[]{:S(2)}) collective-permute-start(bf16[144,128]{1,0:T(8,128)(2,1)S(1)} %gather.1.refs_0_), channel_id=1, source_target_pairs={{0,28},{1,29},{2,30},{3,31},{4,24},{5,25},{6,26},{7,27},{8,20},{9,... | collective-permute-start | bytes 110600 | tf_op jit(solution)/shard_map/ppermute | solution.py:375
  14.0 0.6 %collective-permute-done.4.refs_1_ = bf16[144,128]{1,0:T(8,128)(2,1)S(1)} collective-permute-done((bf16[144,128]{1,0:T(8,128)(2,1)S(1)}, bf16[144,128]{1,0:T(8,128)(2,1)S(1)}, u32[]{:S(2)}, u32[]{:S(2)}) %collective-permute-start.4) | collective-permute-done | bytes 36896 | tf_op jit(solution)/shard_map/ppermute | solution.py:375
  14.6 0.3 %collective-permute-start.6 = (bf16[144,128]{1,0:T(8,128)(2,1)S(1)}, bf16[144,128]{1,0:T(8,128)(2,1)S(1)}, u32[]{:S(2)}, u32[]{:S(2)}) collective-permute-start(bf16[144,128]{1,0:T(8,128)(2,1)S(1)} %collective-permute-done.4.refs_1_), channel_id=1, source_target_pairs={{0,4},{1,5},{2,6},{3,7},{4,0},{5,1},{6,2},{7,3},{8,12},{9,13},{10,... | collective-permute-start | bytes 110600 | tf_op jit(solution)/shard_map/ppermute | solution.py:375
  14.9 0.3 %arrange.1 = (bf16[256,128]{1,0:T(8,128)(2,1)S(1)}, bf16[256,512]{1,0:T(8,128)(2,1)S(1)}) custom-call(bf16[240,128]{1,0:T(8,128)(2,1)S(1)} %get-tuple-element.43.mine, bf16[80,128]{1,0:T(8,128)(2,1)S(1)} %get-tuple-element.44.kept, bf16[176,128]{1,0:T(8,128)(2,1)S(1)} %collective-permute-done.1.refs_0_, bf16[176,128]{1,0:T(8,128)(2,1)S(1)} %collective-permute-done.2.refs_1_, ...), custom_call_target="tpu_custom_call" | custom-call | tf_op jit(solution)/shard_map/arrange/pallas_call | solution.py:414
  15.2 1.7 %collective-permute-done.5.refs_2_ = bf16[144,128]{1,0:T(8,128)(2,1)S(1)} collective-permute-done((bf16[144,128]{1,0:T(8,128)(2,1)S(1)}, bf16[144,128]{1,0:T(8,128)(2,1)S(1)}, u32[]{:S(2)}, u32[]{:S(2)}) %collective-permute-start.5) | collective-permute-done | bytes 36896 | tf_op jit(solution)/shard_map/ppermute | solution.py:375
  16.9 0.0 collective-permute-done.6.refs_3_
  16.9 1.4 %attend.1 = (bf16[4,512]{1,0:T(4,128)(2,1)}, f32[3,4]{1,0:T(4,128)}) custom-call(bf16[144,128]{1,0:T(8,128)(2,1)S(1)} %gather.1.refs_0_, bf16[144,128]{1,0:T(8,128)(2,1)S(1)} %collective-permute-done.4.refs_1_, bf16[144,128]{1,0:T(8,128)(2,1)S(1)} %collective-permute-done.5.refs_2_, bf16[144,128]{1,0:T(8,128)(2,1)S(1)} %collective-permute-done.6.refs_3_, ...), custom_call_target="tpu_custom_call" | custom-call | tf_op jit(solution)/shard_map/attend/pallas_call | solution.py:414
Async XLA Ops:
  1.8 1.4 %collective-permute-start = (bf16[240,128]{1,0:T(8,128)(2,1)S(1)}, bf16[240,128]{1,0:T(8,128)(2,1)S(1)}, u32[]{:S(2)}, u32[]{:S(2)}) collective-permute-start(bf16[240,128]{1,0:T(8,128)(2,1)S(1)} %get-tuple-element.43.mine), channel_id=1, source_target_pairs={{0,4},{1,5},{2,6},{3,7},{4,0},{5,1},{6,2},{7,3},{8,12},{9,13},{10,... | collective-permute-start | bytes 184328 | tf_op jit(solution)/shard_map/ppermute | solution.py:375
  3.3 6.5 %collective-permute-start.1 = (bf16[176,128]{1,0:T(8,128)(2,1)S(1)}, bf16[176,128]{1,0:T(8,128)(2,1)S(1)}, u32[]{:S(2)}, u32[]{:S(2)}) collective-permute-start(bf16[176,128]{1,0:T(8,128)(2,1)S(1)} %get-tuple-element.30), channel_id=1, source_target_pairs={{0,6},{1,7},{2,4},{3,5},{4,1},{5,2},{6,3},{7,0},{8,14},{9,15},{10,... | collective-permute-start | bytes 135176 | tf_op jit(solution)/shard_map/ppermute | solution.py:375
  7.0 3.8 %collective-permute-start.2 = (bf16[176,128]{1,0:T(8,128)(2,1)S(1)}, bf16[176,128]{1,0:T(8,128)(2,1)S(1)}, u32[]{:S(2)}, u32[]{:S(2)}) collective-permute-start(bf16[176,128]{1,0:T(8,128)(2,1)S(1)} %get-tuple-element.42), channel_id=1, source_target_pairs={{0,7},{1,4},{2,5},{3,6},{4,3},{5,0},{6,1},{7,2},{8,15},{9,12},{10,... | collective-permute-start | bytes 135176 | tf_op jit(solution)/shard_map/ppermute | solution.py:375
  9.8 1.3 %collective-permute-start.3 = (bf16[176,128]{1,0:T(8,128)(2,1)S(1)}, bf16[176,128]{1,0:T(8,128)(2,1)S(1)}, u32[]{:S(2)}, u32[]{:S(2)}) collective-permute-start(bf16[176,128]{1,0:T(8,128)(2,1)S(1)} %collective-permute-done.1.refs_0_), channel_id=1, source_target_pairs={{0,4},{1,5},{2,6},{3,7},{4,0},{5,1},{6,2},{7,3},{8,12},{9,13},{10,... | collective-permute-start | bytes 135176 | tf_op jit(solution)/shard_map/ppermute | solution.py:375
  11.2 3.4 %collective-permute-start.4 = (bf16[144,128]{1,0:T(8,128)(2,1)S(1)}, bf16[144,128]{1,0:T(8,128)(2,1)S(1)}, u32[]{:S(2)}, u32[]{:S(2)}) collective-permute-start(bf16[144,128]{1,0:T(8,128)(2,1)S(1)} %gather.1.refs_0_), channel_id=1, source_target_pairs={{0,12},{1,13},{2,14},{3,15},{4,16},{5,17},{6,18},{7,19},{8,4},{9,5... | collective-permute-start | bytes 110600 | tf_op jit(solution)/shard_map/ppermute | solution.py:375
  12.6 4.3 %collective-permute-start.5 = (bf16[144,128]{1,0:T(8,128)(2,1)S(1)}, bf16[144,128]{1,0:T(8,128)(2,1)S(1)}, u32[]{:S(2)}, u32[]{:S(2)}) collective-permute-start(bf16[144,128]{1,0:T(8,128)(2,1)S(1)} %gather.1.refs_0_), channel_id=1, source_target_pairs={{0,28},{1,29},{2,30},{3,31},{4,24},{5,25},{6,26},{7,27},{8,20},{9,... | collective-permute-start | bytes 110600 | tf_op jit(solution)/shard_map/ppermute | solution.py:375
  14.6 2.3 %collective-permute-start.6 = (bf16[144,128]{1,0:T(8,128)(2,1)S(1)}, bf16[144,128]{1,0:T(8,128)(2,1)S(1)}, u32[]{:S(2)}, u32[]{:S(2)}) collective-permute-start(bf16[144,128]{1,0:T(8,128)(2,1)S(1)} %collective-permute-done.4.refs_1_), channel_id=1, source_target_pairs={{0,4},{1,5},{2,6},{3,7},{4,0},{5,1},{6,2},{7,3},{8,12},{9,13},{10,... | collective-permute-start | bytes 110600 | tf_op jit(solution)/shard_map/ppermute | solution.py:375

commit v9 on v8

--- a/solution.py
+++ b/solution.py
@@ -450,6 +450,15 @@
         (mine, other),
     )
     received = [exchange(x, near_step, shift) for x, shift in zip(grouped, along_col, strict=True)]
+    received += [exchange(x, near_step, still) for x in received[:-1]]
+    near = call(
+        functools.partial(gather_kernel, dims),
+        "gather",
+        shape((table_rows + 2 * node_rows(width, own) * cols, lanes), bf16),
+        (mine, other, *received),
+    )
+    pieces = [near] + [exchange(near, step, still) for step in along_row]
+    pieces += [exchange(x, near_step, still) for x in pieces[1 : len(along_row)]]
     small = (w_qkv, w_heads.T, coords)
     tables = (gauss_mul, gauss_add, gauss_mean[None, :], gauss_width[None, :], w_gauss, w_coord1)
     tables += (w_coord2[None, :],)
@@ -465,21 +474,11 @@
             shape((24, lanes), f32),
             shape((3, gauss, lanes), f32),
         ],
-        (lax.optimization_barrier((mine, grouped[0]))[0],),
+        (lax.optimization_barrier((mine, pieces[1]))[0],),
         small + tables,
         [pltpu.VMEM(x.shape, x.dtype) for x in tables] + [pltpu.SemaphoreType.DMA((10,))],
     )
-    received[0], prepared = lax.optimization_barrier((received[0], prepared))
-    received += [exchange(x, near_step, still) for x in received[:-1]]
     w_qkv, w_heads, coords, w_gauss, w_coord1, w_coord2, lookup, own_columns, kernels = prepared
-    near = call(
-        functools.partial(gather_kernel, dims),
-        "gather",
-        shape((table_rows + 2 * node_rows(width, own) * cols, lanes), bf16),
-        (mine, other, *received),
-    )
-    pieces = [near] + [exchange(near, step, still) for step in along_row]
-    pieces += [exchange(x, near_step, still) for x in pieces[1 : len(along_row)]]
     bias, spread_queries = call(
         functools.partial(arrange_kernel, dims, column_parts, row_parts),
         "arrange",

time: 18.5 us -> 18.5 us (level)
  starting transfers between devices: 8.91 us -> 8.42 us
  waiting for transfers between devices: 4.05 us -> 4.51 us
    ppermute x7, starting transfers between devices: 8.91 us -> 8.42 us  [exchange(): return lax.ppermute(x, ('row', 'col'), pairs)]
    ppermute x7, waiting for transfers between devices: 4.05 us -> 4.51 us  [exchange(): return lax.ppermute(x, ('row', 'col'), pairs)]
  transfers between devices with their start and end apart: 7 -> 7, of which waited for: 5 -> 6; matrix products, arithmetic and copies ran while one was open for 0% -> 0% of each run, Pallas kernels for 11% -> 11%
where the time goes in v9:
time: 18.5 us; the launch traced here: 18.3 us
  starting transfers between devices  8.42 us (46%)
  Pallas kernels  4.72 us (26%)
  waiting for transfers between devices  4.51 us (24%)
  between operations  0.66 us (4%)
    ppermute x7, starting transfers between devices, exchange(): return lax.ppermute(x, ('row', 'col'), pairs)  8.42 us
    pallas_call x6, Pallas kernels, call(): pl.pallas_call(kernel, out_shape=out_shape, in_specs=[vmem] * len(inputs)...  4.72 us
    ppermute x7, waiting for transfers between devices, exchange(): return lax.ppermute(x, ('row', 'col'), pairs)  4.51 us
  transfers between devices with their start and end apart: 7, of which 6 were waited for; matrix products, arithmetic and copies ran while one was open for 0% of the time, Pallas kernels for 11%

profile of v9, /device:TPU:0, one launch (start us, length us, event | category | flops | bytes accessed | tf_op | source)
XLA Modules:
  0.0 18.3 jit_solution(2814034030307935111)
XLA Ops:
  0.6 1.2 %pack.1 = (bf16[240,128]{1,0:T(8,128)(2,1)S(1)}, bf16[80,128]{1,0:T(8,128)(2,1)S(1)}) custom-call(bf16[4,512]{1,0:T(4,128)(2,1)} %refs_0_.2, f32[3,4]{1,0:T(4,128)} %refs_2_.1, s32[1,4]{1,0:T(1,128)} %bitcast.11, s32[1,4]{1,0:T(1,128)} %bitcast.12, f32[1,512]{1,0:T(1,128)} %bitcast.10, s32[16,32]{1,0:T(8,128)} %refs_5_.1, bf16[16,32,64]{2,1,0:T(8,128)(2,1)} %bitcast.8), custom_call_target="tpu_custom_call" | custom-call | tf_op jit(solution)/shard_map/pack/pallas_call | solution.py:414
  1.8 0.5 %collective-permute-start = (bf16[240,128]{1,0:T(8,128)(2,1)S(1)}, bf16[240,128]{1,0:T(8,128)(2,1)S(1)}, u32[]{:S(2)}, u32[]{:S(2)}) collective-permute-start(bf16[240,128]{1,0:T(8,128)(2,1)S(1)} %get-tuple-element.21.mine), channel_id=1, source_target_pairs={{0,4},{1,5},{2,6},{3,7},{4,0},{5,1},{6,2},{7,3},{8,12},{9,13},{10,... | collective-permute-start | bytes 184328 | tf_op jit(solution)/shard_map/ppermute | solution.py:375
  2.3 0.9 %collective-permute-done.other = bf16[240,128]{1,0:T(8,128)(2,1)S(1)} collective-permute-done((bf16[240,128]{1,0:T(8,128)(2,1)S(1)}, bf16[240,128]{1,0:T(8,128)(2,1)S(1)}, u32[]{:S(2)}, u32[]{:S(2)}) %collective-permute-start) | collective-permute-done | bytes 61472 | tf_op jit(solution)/shard_map/ppermute | solution.py:375
  3.2 0.1 regroup.1
  3.3 3.7 %collective-permute-start.1 = (bf16[176,128]{1,0:T(8,128)(2,1)S(1)}, bf16[176,128]{1,0:T(8,128)(2,1)S(1)}, u32[]{:S(2)}, u32[]{:S(2)}) collective-permute-start(bf16[176,128]{1,0:T(8,128)(2,1)S(1)} %get-tuple-element.19), channel_id=1, source_target_pairs={{0,6},{1,7},{2,4},{3,5},{4,1},{5,2},{6,3},{7,0},{8,14},{9,15},{10,... | collective-permute-start | bytes 135176 | tf_op jit(solution)/shard_map/ppermute | solution.py:375
  7.0 1.1 %collective-permute-start.2 = (bf16[176,128]{1,0:T(8,128)(2,1)S(1)}, bf16[176,128]{1,0:T(8,128)(2,1)S(1)}, u32[]{:S(2)}, u32[]{:S(2)}) collective-permute-start(bf16[176,128]{1,0:T(8,128)(2,1)S(1)} %get-tuple-element.20), channel_id=1, source_target_pairs={{0,7},{1,4},{2,5},{3,6},{4,3},{5,0},{6,1},{7,2},{8,15},{9,12},{10,... | collective-permute-start | bytes 135176 | tf_op jit(solution)/shard_map/ppermute | solution.py:375
  8.1 1.7 %collective-permute-done.1.refs_0_ = bf16[176,128]{1,0:T(8,128)(2,1)S(1)} collective-permute-done((bf16[176,128]{1,0:T(8,128)(2,1)S(1)}, bf16[176,128]{1,0:T(8,128)(2,1)S(1)}, u32[]{:S(2)}, u32[]{:S(2)}) %collective-permute-start.1) | collective-permute-done | bytes 45088 | tf_op jit(solution)/shard_map/ppermute | solution.py:375
  9.7 0.0 collective-permute-start.3
  9.7 1.1 %collective-permute-done.2.refs_1_ = bf16[176,128]{1,0:T(8,128)(2,1)S(1)} collective-permute-done((bf16[176,128]{1,0:T(8,128)(2,1)S(1)}, bf16[176,128]{1,0:T(8,128)(2,1)S(1)}, u32[]{:S(2)}, u32[]{:S(2)}) %collective-permute-start.2) | collective-permute-done | bytes 45088 | tf_op jit(solution)/shard_map/ppermute | solution.py:375
  10.8 0.1 collective-permute-done.3.refs_2_
  11.0 0.1 gather.1.refs_0_
  11.0 1.5 %collective-permute-start.4 = (bf16[144,128]{1,0:T(8,128)(2,1)S(1)}, bf16[144,128]{1,0:T(8,128)(2,1)S(1)}, u32[]{:S(2)}, u32[]{:S(2)}) collective-permute-start(bf16[144,128]{1,0:T(8,128)(2,1)S(1)} %gather.1.refs_0_), channel_id=1, source_target_pairs={{0,12},{1,13},{2,14},{3,15},{4,16},{5,17},{6,18},{7,19},{8,4},{9,5... | collective-permute-start | bytes 110600 | tf_op jit(solution)/shard_map/ppermute | solution.py:375
  12.6 1.4 %collective-permute-start.5 = (bf16[144,128]{1,0:T(8,128)(2,1)S(1)}, bf16[144,128]{1,0:T(8,128)(2,1)S(1)}, u32[]{:S(2)}, u32[]{:S(2)}) collective-permute-start(bf16[144,128]{1,0:T(8,128)(2,1)S(1)} %gather.1.refs_0_), channel_id=1, source_target_pairs={{0,28},{1,29},{2,30},{3,31},{4,24},{5,25},{6,26},{7,27},{8,20},{9,... | collective-permute-start | bytes 110600 | tf_op jit(solution)/shard_map/ppermute | solution.py:375
  14.0 0.4 %collective-permute-done.4.refs_1_ = bf16[144,128]{1,0:T(8,128)(2,1)S(1)} collective-permute-done((bf16[144,128]{1,0:T(8,128)(2,1)S(1)}, bf16[144,128]{1,0:T(8,128)(2,1)S(1)}, u32[]{:S(2)}, u32[]{:S(2)}) %collective-permute-start.4) | collective-permute-done | bytes 36896 | tf_op jit(solution)/shard_map/ppermute | solution.py:375
  14.4 0.2 collective-permute-start.6
  14.6 1.7 %prepare.1 = (bf16[512,1536]{1,0:T(8,128)(2,1)S(1)}, bf16[64,128]{1,0:T(8,128)(2,1)S(1)}, f32[3,4]{1,0:T(4,128)S(1)}, bf16[128,128]{1,0:T(8,128)(2,1)S(1)}, bf16...) custom-call(bf16[240,128]{1,0:T(8,128)(2,1)S(1)} %get-tuple-element., ...), custom_call_target="tpu_custom_call" | custom-call | tf_op jit(solution)/shard_map/prepare/pallas_call | solution.py:414
  16.3 0.3 %arrange.1 = (bf16[256,128]{1,0:T(8,128)(2,1)S(1)}, bf16[256,512]{1,0:T(8,128)(2,1)S(1)}) custom-call(bf16[240,128]{1,0:T(8,128)(2,1)S(1)} %get-tuple-element.21.mine, bf16[80,128]{1,0:T(8,128)(2,1)S(1)} %get-tuple-element.22.kept, bf16[176,128]{1,0:T(8,128)(2,1)S(1)} %collective-permute-done.1.refs_0_, bf16[176,128]{1,0:T(8,128)(2,1)S(1)} %collective-permute-done.2.refs_1_, ...), custom_call_target="tpu_custom_call" | custom-call | tf_op jit(solution)/shard_map/arrange/pallas_call | solution.py:414
  16.6 0.3 %collective-permute-done.5.refs_2_ = bf16[144,128]{1,0:T(8,128)(2,1)S(1)} collective-permute-done((bf16[144,128]{1,0:T(8,128)(2,1)S(1)}, bf16[144,128]{1,0:T(8,128)(2,1)S(1)}, u32[]{:S(2)}, u32[]{:S(2)}) %collective-permute-start.5) | collective-permute-done | bytes 36896 | tf_op jit(solution)/shard_map/ppermute | solution.py:375
  16.9 0.0 collective-permute-done.6.refs_3_
  16.9 1.4 %attend.1 = (bf16[4,512]{1,0:T(4,128)(2,1)}, f32[3,4]{1,0:T(4,128)}) custom-call(bf16[144,128]{1,0:T(8,128)(2,1)S(1)} %gather.1.refs_0_, bf16[144,128]{1,0:T(8,128)(2,1)S(1)} %collective-permute-done.4.refs_1_, bf16[144,128]{1,0:T(8,128)(2,1)S(1)} %collective-permute-done.5.refs_2_, bf16[144,128]{1,0:T(8,128)(2,1)S(1)} %collective-permute-done.6.refs_3_, ...), custom_call_target="tpu_custom_call" | custom-call | tf_op jit(solution)/shard_map/attend/pallas_call | solution.py:414
Async XLA Ops:
  1.8 1.4 %collective-permute-start = (bf16[240,128]{1,0:T(8,128)(2,1)S(1)}, bf16[240,128]{1,0:T(8,128)(2,1)S(1)}, u32[]{:S(2)}, u32[]{:S(2)}) collective-permute-start(bf16[240,128]{1,0:T(8,128)(2,1)S(1)} %get-tuple-element.21.mine), channel_id=1, source_target_pairs={{0,4},{1,5},{2,6},{3,7},{4,0},{5,1},{6,2},{7,3},{8,12},{9,13},{10,... | collective-permute-start | bytes 184328 | tf_op jit(solution)/shard_map/ppermute | solution.py:375
  3.3 6.5 %collective-permute-start.1 = (bf16[176,128]{1,0:T(8,128)(2,1)S(1)}, bf16[176,128]{1,0:T(8,128)(2,1)S(1)}, u32[]{:S(2)}, u32[]{:S(2)}) collective-permute-start(bf16[176,128]{1,0:T(8,128)(2,1)S(1)} %get-tuple-element.19), channel_id=1, source_target_pairs={{0,6},{1,7},{2,4},{3,5},{4,1},{5,2},{6,3},{7,0},{8,14},{9,15},{10,... | collective-permute-start | bytes 135176 | tf_op jit(solution)/shard_map/ppermute | solution.py:375
  7.0 3.8 %collective-permute-start.2 = (bf16[176,128]{1,0:T(8,128)(2,1)S(1)}, bf16[176,128]{1,0:T(8,128)(2,1)S(1)}, u32[]{:S(2)}, u32[]{:S(2)}) collective-permute-start(bf16[176,128]{1,0:T(8,128)(2,1)S(1)} %get-tuple-element.20), channel_id=1, source_target_pairs={{0,7},{1,4},{2,5},{3,6},{4,3},{5,0},{6,1},{7,2},{8,15},{9,12},{10,... | collective-permute-start | bytes 135176 | tf_op jit(solution)/shard_map/ppermute | solution.py:375
  9.7 1.2 %collective-permute-start.3 = (bf16[176,128]{1,0:T(8,128)(2,1)S(1)}, bf16[176,128]{1,0:T(8,128)(2,1)S(1)}, u32[]{:S(2)}, u32[]{:S(2)}) collective-permute-start(bf16[176,128]{1,0:T(8,128)(2,1)S(1)} %collective-permute-done.1.refs_0_), channel_id=1, source_target_pairs={{0,4},{1,5},{2,6},{3,7},{4,0},{5,1},{6,2},{7,3},{8,12},{9,13},{10,... | collective-permute-start | bytes 135176 | tf_op jit(solution)/shard_map/ppermute | solution.py:375
  11.0 3.4 %collective-permute-start.4 = (bf16[144,128]{1,0:T(8,128)(2,1)S(1)}, bf16[144,128]{1,0:T(8,128)(2,1)S(1)}, u32[]{:S(2)}, u32[]{:S(2)}) collective-permute-start(bf16[144,128]{1,0:T(8,128)(2,1)S(1)} %gather.1.refs_0_), channel_id=1, source_target_pairs={{0,12},{1,13},{2,14},{3,15},{4,16},{5,17},{6,18},{7,19},{8,4},{9,5... | collective-permute-start | bytes 110600 | tf_op jit(solution)/shard_map/ppermute | solution.py:375
  12.6 4.3 %collective-permute-start.5 = (bf16[144,128]{1,0:T(8,128)(2,1)S(1)}, bf16[144,128]{1,0:T(8,128)(2,1)S(1)}, u32[]{:S(2)}, u32[]{:S(2)}) collective-permute-start(bf16[144,128]{1,0:T(8,128)(2,1)S(1)} %gather.1.refs_0_), channel_id=1, source_target_pairs={{0,28},{1,29},{2,30},{3,31},{4,24},{5,25},{6,26},{7,27},{8,20},{9,... | collective-permute-start | bytes 110600 | tf_op jit(solution)/shard_map/ppermute | solution.py:375
  14.4 2.5 %collective-permute-start.6 = (bf16[144,128]{1,0:T(8,128)(2,1)S(1)}, bf16[144,128]{1,0:T(8,128)(2,1)S(1)}, u32[]{:S(2)}, u32[]{:S(2)}) collective-permute-start(bf16[144,128]{1,0:T(8,128)(2,1)S(1)} %collective-permute-done.4.refs_1_), channel_id=1, source_target_pairs={{0,4},{1,5},{2,6},{3,7},{4,0},{5,1},{6,2},{7,3},{8,12},{9,13},{10,... | collective-permute-start | bytes 110600 | tf_op jit(solution)/shard_map/ppermute | solution.py:375
